TPU v7x, 32 devices: a whole 2x2x4 slice. The times are simulated.
32 devices in a mesh: dp: 8 (over y, x, core), mp: 4 (over z).
Axes of the slice: x: 2, y: 2, z: 4, core: 2. Of those that a mesh axis runs over, the one named last changes fastest.
Arguments:
- image_feats: bfloat16 [4096, 1152], P(('dp', 'mp')), may hold values from -6 to 6
- text_feats: bfloat16 [4096, 1152], P(('dp', 'mp')), may hold values from -6 to 6
- image_proj: bfloat16 [1152, 1152], replicated, may hold values from -0.1875 to 0.1875
- text_proj: bfloat16 [1152, 1152], replicated, may hold values from -0.1875 to 0.1875
- log_scale: float32 [1], replicated, may hold values from 3.6 to 4.3
- logit_bias: float32 [1], replicated, may hold values from -12 to -9
Outputs:
- loss: float32 [1], replicated
- image_proj_grad: float32 [1152, 1152], P(('dp', 'mp'))
- text_proj_grad: float32 [1152, 1152], P(('dp', 'mp'))
- log_scale_grad: float32 [1], replicated
- bias_grad: float32 [1], replicated
All inputs are finite; a program needn't handle non-finite values.
Results may differ from a plain program's by a relative error of at most 0.0035.
Values may be sent and summed in bfloat16 or wider, within the bound.
No kernel may reach another device: no remote copies, remote signals or barrier semaphores. Data moves between devices by JAX's collectives and lax.ppermute only.
A program may use at most 128 MiB of HBM per device.

v0:
```python
import jax
import jax.numpy as jnp
from jax import lax
from jax.sharding import PartitionSpec as P


def normalize(features, projection):
    projected = jnp.dot(features, projection, preferred_element_type=jnp.float32)
    row_norm = jnp.sqrt(jnp.sum(projected * projected, axis=-1, keepdims=True) + 1e-06)
    return (projected / row_norm, row_norm)


def unnormalize(unit_rows, row_norm, unit_grad):
    inner_product = jnp.sum(unit_rows * unit_grad, axis=-1, keepdims=True)
    return ((unit_grad - unit_rows * inner_product) / row_norm).astype(jnp.bfloat16)


def pair_terms(cosine, label_signs, logit_scale, bias_value):
    logits = logit_scale * cosine + bias_value
    losses = -jax.nn.log_sigmoid(label_signs * logits)
    pair_grads = -label_signs * jax.nn.sigmoid(-label_signs * logits)
    return (
        jnp.sum(losses),
        jnp.sum(pair_grads * logit_scale * cosine),
        jnp.sum(pair_grads),
        pair_grads.astype(jnp.bfloat16),
    )


def pair_signs(dp_index, mp_index, own_rows, mp_size, dp_size):
    row_ids = dp_index * own_rows * mp_size + jnp.arange(own_rows * mp_size, dtype=jnp.int32)
    column = jnp.arange(own_rows * dp_size, dtype=jnp.int32)
    column_ids = (column // own_rows * mp_size + mp_index) * own_rows + column % own_rows
    return jnp.where(row_ids[:, None] == column_ids[None, :], 1.0, -1.0).astype(jnp.float32)


def per_device(image_feats, text_feats, image_proj, text_proj, log_scale, logit_bias):
    own_rows = image_feats.shape[0]
    dp_size = lax.axis_size("dp")
    mp_size = lax.axis_size("mp")
    dp_index = lax.axis_index("dp")
    mp_index = lax.axis_index("mp")
    image_unit, image_norm = normalize(image_feats, image_proj)
    text_unit, text_norm = normalize(text_feats, text_proj)
    image_half = image_unit.astype(jnp.bfloat16)
    text_half = text_unit.astype(jnp.bfloat16)
    logit_scale = jnp.exp(log_scale[0])
    bias_value = logit_bias[0]
    label_signs = pair_signs(dp_index, mp_index, own_rows, mp_size, dp_size)
    image_group = lax.all_gather(image_half, "mp", axis=0, tiled=True)
    text_loop = lax.all_gather(text_half, "dp", axis=0, tiled=True)
    cosine = jnp.einsum("id,jd->ij", image_group, text_loop, preferred_element_type=jnp.float32)
    loss_part, scale_part, bias_part, half_grads = pair_terms(
        cosine, label_signs, logit_scale, bias_value
    )
    image_terms = logit_scale * jnp.dot(half_grads, text_loop, preferred_element_type=jnp.float32)
    image_grad = lax.psum_scatter(image_terms, "mp", scatter_dimension=0, tiled=True)
    text_grad = lax.psum_scatter(
        logit_scale
        * jnp.einsum("ij,id->jd", half_grads, image_group, preferred_element_type=jnp.float32),
        "dp",
        scatter_dimension=0,
        tiled=True,
    )
    image_dy = unnormalize(image_unit, image_norm, image_grad)
    text_dy = unnormalize(text_unit, text_norm, text_grad)
    image_part = jnp.einsum("rd,re->de", image_feats, image_dy, preferred_element_type=jnp.float32)
    text_part = jnp.einsum("rd,re->de", text_feats, text_dy, preferred_element_type=jnp.float32)
    image_proj_grad, text_proj_grad = (
        lax.psum_scatter(image_part, ("dp", "mp"), scatter_dimension=0, tiled=True),
        lax.psum_scatter(text_part, ("dp", "mp"), scatter_dimension=0, tiled=True),
    )
    loss_sum, scale_sum, bias_sum = lax.psum((loss_part, scale_part, bias_part), ("dp", "mp"))
    batch_total = own_rows * dp_size * mp_size
    return (
        (loss_sum / batch_total).reshape(1),
        image_proj_grad,
        text_proj_grad,
        (scale_sum / batch_total).reshape(1),
        (bias_sum / batch_total).reshape(1),
    )


def solution(mesh):
    return jax.shard_map(
        per_device,
        mesh=mesh,
        in_specs=(P(("dp", "mp"), None), P(("dp", "mp"), None), P(), P(), P(), P()),
        out_specs=(P(), P(("dp", "mp"), None), P(("dp", "mp"), None), P(), P()),
        check_vma=False,
    )
```

profile of v0, /device:TPU:0, one launch (start us, length us, event | category | flops | bytes accessed | tf_op | source)
XLA Modules:
  0.0 429.3 jit_solution(3228055101924285267)
XLA Ops:
  7.2 1.7 copy-done
  8.9 1.6 multiply_reduce_fusion.4
  10.6 0.8 fusion.25
  11.5 0.0 all-gather.5.cloned.1.call-start
  11.5 2.4 multiply_reduce_fusion.3
  14.0 0.8 copy-done.1
  14.8 0.8 fusion.26
  17.0 27.7 %all-gather.3.cloned.1.call-done = bf16[512,1152]{1,0:T(8,128)(2,1)} async-done(((bf16[128,1152]{1,0:T(8,128)(2,1)}), bf16[512,1152]{1,0:T(8,128)(2,1)}) %all-gather.3.cloned.1.call-update) | async-done | bytes 1179664 | tf_op jit(solution)/shard_map/all_gather | solution.py:50
  44.8 30.0 %all-gather.5.cloned.1.call-done = bf16[1024,1152]{1,0:T(8,128)(2,1)} async-done(((bf16[128,1152]{1,0:T(8,128)(2,1)}), bf16[1024,1152]{1,0:T(8,128)(2,1)}) %all-gather.5.cloned.1.call-update) | async-done | bytes 2359312 | tf_op jit(solution)/shard_map/all_gather | solution.py:51
  74.8 6.4 %fusion.28 = (f32[]{:T(128)}, f32[]{:T(128)}, f32[]{:T(128)}, f32[512,1024]{1,0:T(8,128)S(1)}) fusion(f32[]{:T(128)} %bitcast.23, f32[]{:T(128)} %bitcast, s32[1024]{0:T(1024)S(1)} %fusion.23, s32[512]{0:T(512)S(1)} %iota_add_fusion, bf16[512,1152]{1,0:T(8,128)(2,1)} %all-gather.3.cloned.1.call-done, bf16[1024,1152]{1,0:T(8,128)(2,1)} %all-gather.5.cloned.1.call-done), kind=kOutput, calls=%fused_computation.53 | convolution fusion | flops 1220018176 | bytes 5642260 | tf_op jit(solution)/shard_map/id,jd->ij/dot_general | solution.py:52
  81.2 1.3 copy-done.5
  82.5 3.6 convolution_multiply_fusion.1
  86.1 6.1 %convolution_multiply_fusion = f32[1024,1152]{1,0:T(8,128)} fusion(bf16[512,1152]{1,0:T(8,128)(2,1)} %all-gather.3.cloned.1.call-done, f32[]{:T(128)} %bitcast, f32[512,1024]{1,0:T(8,128)} %copy-done.5, f32[]{:T(128)} %bitcast.25, s32[1024]{0:T(1024)S(1)} %fusion.23, s32[512]{0:T(512)S(1)} %iota_add_fusion), kind=kOutput, calls=%fused_computation.3 | convolution fusion | flops 1214906368 | bytes 8001544 | tf_op jit(solution)/shard_map/ij,id->jd/dot_general | solution.py:60
  92.3 42.0 %reduce-scatter.5.cloned.1.call-done = f32[128,1152]{1,0:T(8,128)} async-done(((f32[512,1152]{1,0:T(8,128)}), f32[128,1152]{1,0:T(8,128)}) %reduce-scatter.5.cloned.1.call-update) | async-done | bytes 589840 | tf_op jit(solution)/shard_map/reduce_scatter | solution.py:57
  134.3 1.3 multiply_reduce_fusion.2
  135.6 4.4 %convolution_bitcast_fusion.1 = f32[1152,1152]{0,1:T(8,128)} fusion(bf16[128,1152]{1,0:T(8,128)(2,1)S(1)} %copy-done.2, f32[128,1152]{1,0:T(8,128)} %reduce-scatter.5.cloned.1.call-done, f32[128]{0:T(128)S(1)} %multiply_reduce_fusion.2, f32[128]{0:T(128)S(1)} %add_sqrt_fusion.1, f32[128,1152]{1,0:T(8,128)S(1)} %get-tuple-element.24), kind=kOutput, calls=%fused_computation.1 | convolution fusion | flops 340475904 | bytes 6784000 | tf_op jit(solution)/shard_map/rd,re->de/dot_general | solution.py:67
  139.9 51.1 %reduce-scatter.7.cloned.1.call-done = f32[128,1152]{1,0:T(8,128)} async-done(((f32[1024,1152]{1,0:T(8,128)}), f32[128,1152]{1,0:T(8,128)}) %reduce-scatter.7.cloned.1.call-update) | async-done | bytes 589840 | tf_op jit(solution)/shard_map/reduce_scatter | solution.py:58
  191.0 1.5 multiply_reduce_fusion.1
  192.5 4.6 %convolution_bitcast_fusion = f32[1152,1152]{0,1:T(8,128)} fusion(bf16[128,1152]{1,0:T(8,128)(2,1)} %param.7, f32[128,1152]{1,0:T(8,128)} %reduce-scatter.7.cloned.1.call-done, f32[128]{0:T(128)S(1)} %multiply_reduce_fusion.1, f32[128]{0:T(128)S(1)} %add_sqrt_fusion, f32[128,1152]{1,0:T(8,128)} %copy-done.1), kind=kOutput, calls=%fused_computation | convolution fusion | flops 340475904 | bytes 6784000 | tf_op jit(solution)/shard_map/rd,re->de/dot_general | solution.py:68
  197.1 40.3 %all-reduce.2 = (f32[]{:T(128)}, f32[]{:T(128)}, f32[]{:T(128)}) all-reduce(f32[]{:T(128)} %get-tuple-element.17, f32[]{:T(128)} %get-tuple-element.16, f32[]{:T(128)} %get-tuple-element.15), channel_id=1, replica_groups=mesh['dp'=8,'mp'=4] {'dp','mp'}, use_global_device_ids=true, to_apply=%region_3.4 | all-reduce | flops 3 | bytes 24 | tf_op jit(solution)/shard_map/psum | solution.py:73
  239.5 174.2 %all-reduce.6.cloned.1.call-done = (f32[1152,1152]{0,1:T(8,128)}, f32[1152,1152]{0,1:T(8,128)}) async-done(((f32[1152,1152]{0,1:T(8,128)}, f32[1152,1152]{0,1:T(8,128)}), (f32[1152,1152]{0,1:T(8,128)}, f32[1152,1152]{0,1:T(8,128)})) %all-reduce.6.cloned.1.call-update) | async-done | bytes 10616848
  413.7 2.8 constant_dynamic-slice_fusion
  416.5 2.0 copy.13
  418.4 0.9 copy.14
  (22 shorter events, 0.3 us)
Async XLA Ops:
  7.2 1.8 copy-start
  7.2 4.3 %copy-start.3 = (bf16[128,1152]{1,0:T(8,128)(2,1)S(1)}, bf16[128,1152]{1,0:T(8,128)(2,1)}, u32[]{:S(2)}) copy-start(bf16[128,1152]{1,0:T(8,128)(2,1)} %param.7) | copy-start | bytes 884740
  7.2 37.6 %all-gather.3.cloned.1.call-start = ((), (), s32[]{:S(2)}) async-start(), calls=%async_computation.2 | async-start | bytes 1474560 | tf_op jit(solution)/shard_map/all_gather | solution.py:50
  11.5 63.3 %all-gather.5.cloned.1.call-start = ((), (), s32[]{:S(2)}) async-start(), calls=%async_computation.3 | async-start | bytes 2654208 | tf_op jit(solution)/shard_map/all_gather | solution.py:51
  14.0 0.8 copy-start.1
  15.6 118.7 %reduce-scatter.5.cloned.1.call-start = ((), (), s32[]{:S(2)}) async-start(), calls=%async_computation.4 | async-start | bytes 2949120 | tf_op jit(solution)/shard_map/reduce_scatter | solution.py:57
  74.8 7.7 %copy-start.4 = (bf16[1024,1152]{1,0:T(8,128)(2,1)S(1)}, bf16[1024,1152]{1,0:T(8,128)(2,1)}, u32[]{:S(2)}) copy-start(bf16[1024,1152]{1,0:T(8,128)(2,1)} %all-gather.5.cloned.1.call-done) | copy-start | bytes 7077892
  81.2 1.3 copy-start.5
  86.1 104.9 %reduce-scatter.7.cloned.1.call-start = ((), (), s32[]{:S(2)}) async-start(), calls=%async_computation.5 | async-start | bytes 5308416 | tf_op jit(solution)/shard_map/reduce_scatter | solution.py:58
  92.2 43.3 %copy-start.2 = (bf16[128,1152]{1,0:T(8,128)(2,1)S(1)}, bf16[128,1152]{1,0:T(8,128)(2,1)}, u32[]{:S(2)}) copy-start(bf16[128,1152]{1,0:T(8,128)(2,1)} %param.6) | copy-start | bytes 884740
  92.3 321.4 %all-reduce.6.cloned.1.call-start = ((), (), s32[]{:S(2)}) async-start(), calls=%async_computation.6 | async-start | bytes 21233664
Sparse Core Ops, SparseCore 0:
  11.6 33.1 all-gather.2
  46.6 28.1 all-gather.4
  86.2 48.0 reduce-scatter.4
  137.6 53.3 reduce-scatter.6
  198.4 215.2 all-reduce.5
where the time goes:
time: 430 us; the launch traced here: 429 us
  waiting for transfers between devices  325 us (76%)
  blocking collectives  40.3 us (9%)
  matrix products  29.1 us (7%)
  between operations  20.6 us (5%)
  local copies, waits for them, and re-layouts  9.48 us (2%)
  other arithmetic  4.41 us (1%)
    unnamed x6, waiting for transfers between devices  174 us
    reduce_scatter x1, waiting for transfers between devices, per_device(): lax.psum_scatter(logit_scale * jnp.einsum('ij,id->jd', half_grads, image_...  51.1 us
    reduce_scatter x1, waiting for transfers between devices, per_device(): lax.psum_scatter(image_terms, 'mp', scatter_dimension=0, tiled=True)  42 us
    psum x1, blocking collectives, per_device(): lax.psum((loss_part, scale_part, bias_part), ('dp', 'mp'))  40.3 us
    all_gather x1, waiting for transfers between devices, per_device(): text_loop = lax.all_gather(text_half, 'dp', axis=0, tiled=True)  30 us
    all_gather x1, waiting for transfers between devices, per_device(): image_group = lax.all_gather(image_half, 'mp', axis=0, tiled=True)  27.7 us
    unnamed x15, local copies, waits for them, and re-layouts  9.48 us
  transfers between devices with their start and end apart: 5, of which 5 were waited for; matrix products, arithmetic and copies ran while one was open for 3% of the time, Pallas kernels for 0%

commit v1 on v0

v1 whole, which is shorter than its diff:
```python
import functools
import math

import jax
import jax.numpy as jnp
from jax import lax
from jax.experimental import pallas as pl
from jax.experimental.pallas import tpu as pltpu
from jax.sharding import PartitionSpec as P

F32 = jnp.float32
BF16 = jnp.bfloat16
AXES = ("dp", "mp")


class Layout:
    def __init__(self, dp_size, mp_size):
        self.dp, self.mp = dp_size, mp_size
        self.units = dp_size * mp_size // 2
        self.side = math.isqrt(self.units)
        if self.side * self.side != self.units or self.side % mp_size:
            raise ValueError("unsupported mesh")

    def device(self, unit, core):
        return (2 * (unit // self.mp) + core) * self.mp + unit % self.mp

    def permutation(self, row_step, column_step, flip):
        s = self.side
        pairs = []
        for unit in range(self.units):
            row, column = divmod(unit, s)
            target = (row + row_step) % s * s + (column + column_step) % s
            for core in range(2):
                pairs.append((self.device(unit, core), self.device(target, core ^ flip)))
        return pairs


def block_kernel(
    side, shard_rows, tile, scalars, image_proj, text_proj, *refs
):
    shards = 2 * side
    image_shards, text_shards = refs[:shards], refs[shards : 2 * shards]
    outs = refs[2 * shards : 3 * shards - side]
    stats, feats, projs, other_half, dy, grad, sems = refs[3 * shards - side :]
    rows, width = dy.shape
    chunk = width // side
    mp_size = lax.axis_size("mp")
    dp_index, mp_index = lax.axis_index("dp"), lax.axis_index("mp")
    core = lax.rem(dp_index, 2)
    unit_row = (dp_index // 2 * mp_size + mp_index) // side
    scale, bias = scalars[0], scalars[1]

    copies = {}

    def start(name, source, target):
        copies[name] = pltpu.make_async_copy(source, target, sems.at[len(copies)])
        copies[name].start()

    start("text_proj", text_proj, projs.at[1 - core])
    start("image_proj", image_proj, projs.at[core])
    for i in range(shards):
        place = pl.ds(i * shard_rows, shard_rows)
        start(("text", i), text_shards[i], feats.at[1 - core, place])
        start(("image", i), image_shards[i], feats.at[core, place])
    for copy in copies.values():
        copy.wait()

    def project(which, place):
        raw = jnp.dot(feats[which, place, :], projs[which], preferred_element_type=F32)
        inverse = lax.rsqrt(jnp.sum(raw * raw, axis=-1, keepdims=True) + 1e-06)
        return raw * inverse, inverse

    @pl.loop(0, rows // tile)
    def _(i):
        place = pl.ds(pl.multiple_of(i * tile, tile), tile)
        unit, _ = project(1, place)
        other_half[place, :] = unit.astype(BF16)

    stats[...] = jnp.zeros_like(stats)

    def lanes(values):
        total = jnp.sum(values, axis=0, keepdims=True)
        return sum(total[:, j : j + 128] for j in range(0, total.shape[1], 128))

    @pl.loop(0, rows // tile)
    def _(i):
        place = pl.ds(pl.multiple_of(i * tile, tile), tile)
        unit, inverse = project(0, place)
        cosine = lax.dot_general(
            unit.astype(BF16), other_half[...], (((1,), (1,)), ((), ())), preferred_element_type=F32
        )
        logits = scale * cosine + bias
        small = jnp.exp(-jnp.abs(logits))
        inverse_sum = 1.0 / (1.0 + small)
        large_side = logits >= 0.0
        upper = jnp.where(large_side, inverse_sum, small * inverse_sum)
        lower = jnp.where(large_side, small * inverse_sum, inverse_sum)
        row_ids = i * tile + lax.broadcasted_iota(jnp.int32, (tile, 1), 0)
        row_ids = jnp.where(row_ids < 2 * shard_rows, row_ids, -1)
        equal = row_ids == lax.broadcasted_iota(jnp.int32, cosine.shape, 1)
        losses = jnp.maximum(jnp.where(equal, -logits, logits), 0.0) + jnp.log1p(small)
        pair_grads = jnp.where(equal, -lower, upper)
        half_grads = pair_grads.astype(BF16)
        stats[0:1, :] += lanes(losses)
        stats[1:2, :] += lanes(pair_grads * cosine)
        stats[2:3, :] += lanes(pair_grads)
        inner = jnp.sum(half_grads.astype(F32) * cosine, axis=-1, keepdims=True)
        grads = jnp.dot(half_grads, other_half[...], preferred_element_type=F32)
        dy[place, :] = ((grads - unit * inner) * (scale * inverse)).astype(BF16)

    stats[1:2, :] = stats[1:2, :] * scale
    for j in range(0, width, 128):
        grad[j : j + 128, :] = lax.dot_general(
            feats[0, :, j : j + 128], dy[...], (((0,), (0,)), ((), ())), preferred_element_type=F32
        )
    for t in range(side):
        first = pl.multiple_of(lax.rem(unit_row + t, side) * chunk, chunk)
        outs[t][...] = grad[pl.ds(first, chunk), :].astype(outs[t].dtype)


def block_grads(layout, scalars, image_proj, text_proj, image_shards, text_shards):
    side = layout.side
    shard_rows, width = image_shards[0].shape
    rows = 2 * side * shard_rows
    chunk = width // side
    tile = 256
    anywhere = pl.BlockSpec(memory_space=pl.ANY)
    vmem = pl.BlockSpec(memory_space=pltpu.VMEM)
    copies = 4 * side + 2
    return pl.pallas_call(
        functools.partial(block_kernel, side, shard_rows, tile),
        out_shape=[jax.ShapeDtypeStruct((chunk, width), F32)]
        + [jax.ShapeDtypeStruct((chunk, width), BF16)] * (side - 1)
        + [jax.ShapeDtypeStruct((8, 128), F32)],
        in_specs=[pl.BlockSpec(memory_space=pltpu.SMEM)] + [anywhere] * copies,
        out_specs=[vmem] * (side + 1),
        scratch_shapes=[
            pltpu.VMEM((2, rows, width), BF16),
            pltpu.VMEM((2, width, width), BF16),
            pltpu.VMEM((rows, width), BF16),
            pltpu.VMEM((rows, width), BF16),
            pltpu.VMEM((width, width), F32),
            pltpu.SemaphoreType.DMA((copies,)),
        ],
        compiler_params=pltpu.CompilerParams(vmem_limit_bytes=56 * 1024 * 1024),
        cost_estimate=pl.CostEstimate(
            flops=2 * rows * width * (2 * width + 2 * rows + width),
            bytes_accessed=4 * rows * width + 8 * width * width,
            transcendentals=3 * rows * rows,
        ),
        name="block",
    )(scalars, image_proj, text_proj, *image_shards, *text_shards)


def per_device(layout, image_feats, text_feats, image_proj, text_proj, log_scale, logit_bias):
    side, mp_size = layout.side, layout.mp
    own_rows, width = image_feats.shape
    devices = layout.dp * layout.mp
    out_rows = width // devices
    batch_total = own_rows * devices
    dp_index, mp_index = lax.axis_index("dp"), lax.axis_index("mp")
    core = dp_index % 2
    unit_column = (dp_index // 2 * mp_size + mp_index) % side

    def send(value, row_step, column_step, flip):
        return lax.ppermute(value, AXES, layout.permutation(row_step, column_step, flip))

    scalars = jnp.concatenate([jnp.exp(log_scale), logit_bias])
    images, texts = [image_feats], [text_feats]
    for t in range(1, side):
        images.append(send(image_feats, 0, t, 0))
        texts.append(send(text_feats, t, 0, 0))
    image_shards = [y for x in images for y in (x, send(x, 0, 0, 1))]
    text_shards = [y for x in texts for y in (x, send(x, 0, 0, 1))]

    own, *messages, stats = block_grads(
        layout, scalars, image_proj, text_proj, image_shards, text_shards
    )
    all_stats = lax.all_gather(stats, AXES, axis=0)
    for t in range(1, side):
        own = own + send(messages[t - 1], t, 0, 0).astype(F32)

    blocks = own.reshape(side // mp_size, 2, mp_size, out_rows, width)

    def piece(column, role):
        start = (column // mp_size, role, column % mp_size, 0, 0)
        return lax.dynamic_slice(blocks, start, (1, 1, 1, out_rows, width))[0, 0, 0]

    sums = []
    for flip in range(2):
        total = None
        for t in range(side):
            part = piece((unit_column + t) % side, core ^ flip)
            if t or flip:
                part = send(part.astype(BF16), 0, t, flip).astype(F32)
            total = part if total is None else total + part
        sums.append(total)
    same, other = sums
    image_proj_grad = jnp.where(core == 0, same, other)
    text_proj_grad = jnp.where(core == 0, other, same)
    totals = jnp.sum(all_stats, axis=(0, 2)) * (0.5 / batch_total)
    return totals[0:1], image_proj_grad, text_proj_grad, totals[1:2], totals[2:3]


def solution(mesh):
    layout = Layout(mesh.shape["dp"], mesh.shape["mp"])
    return jax.shard_map(
        functools.partial(per_device, layout),
        mesh=mesh,
        in_specs=(P(AXES, None), P(AXES, None), P(), P(), P(), P()),
        out_specs=(P(), P(AXES, None), P(AXES, None), P(), P()),
        check_vma=False,
    )
```

time: 430 us -> 166 us (0.39)
  waiting for transfers between devices: 325 us -> 31.6 us
  blocking collectives: 40.3 us -> 74 us
  matrix products: 29.1 us -> 0 us
  Pallas kernels: 0 us -> 28.9 us
  starting transfers between devices: 0.21 us -> 23.1 us
  between operations: 20.6 us -> 2.22 us
  local copies, waits for them, and re-layouts: 9.48 us -> 2.56 us
    unnamed x6 -> x0, waiting for transfers between devices: 174 us -> none
    reduce_scatter x2 -> x0, waiting for transfers between devices: 93.1 us -> none  [the longest x1 51.1 us: per_device(): lax.psum_scatter(logit_scale * jnp.einsum('ij,id->jd', half_grads, image_...]
    all_gather x0 -> x1, blocking collectives: none -> 74 us  [per_device(): all_stats = lax.all_gather(stats, AXES, axis=0)]
    all_gather x2 -> x0, waiting for transfers between devices: 57.8 us -> none  [the longest x1 30 us: per_device(): text_loop = lax.all_gather(text_half, 'dp', axis=0, tiled=True)]
    psum x1 -> x0, blocking collectives: 40.3 us -> none  [per_device(): lax.psum((loss_part, scale_part, bias_part), ('dp', 'mp'))]
    ppermute x0 -> x24, waiting for transfers between devices: none -> 31.6 us  [send(): lax.ppermute(value, AXES, layout.permutation(row_step, column_step, flip))]
    dot_general x7 -> x0, matrix products: 29.1 us -> none  [the longest x1 6.4 us: per_device(): jnp.einsum('id,jd->ij', image_group, text_loop, preferred_element_type=jn...]
    pallas_call x0 -> x1, Pallas kernels: none -> 28.9 us  [block_grads(): pl.pallas_call(functools.partial(block_kernel, side, shard_rows, tile), o...]
  transfers between devices with their start and end apart: 5 -> 24, of which waited for: 5 -> 6; matrix products, arithmetic and copies ran while one was open for 3% -> 1% of each run, Pallas kernels for 0% -> 0%
where the time goes in v1:
time: 166 us
  blocking collectives  74 us (45%)
  waiting for transfers between devices  31.6 us (19%)
  Pallas kernels  28.9 us (17%)
  starting transfers between devices  23.1 us (14%)
  other arithmetic  3.16 us (2%)
  local copies, waits for them, and re-layouts  2.56 us (2%)
  between operations  2.22 us (1%)
    all_gather x1, blocking collectives, per_device(): all_stats = lax.all_gather(stats, AXES, axis=0)  74 us
    ppermute x24, waiting for transfers between devices, send(): lax.ppermute(value, AXES, layout.permutation(row_step, column_step, flip))  31.6 us
    pallas_call x1, Pallas kernels, block_grads(): pl.pallas_call(functools.partial(block_kernel, side, shard_rows, tile), o...  28.9 us
    ppermute x24, starting transfers between devices, send(): lax.ppermute(value, AXES, layout.permutation(row_step, column_step, flip))  23.1 us
  transfers between devices with their start and end apart: 24, of which 6 were waited for; matrix products, arithmetic and copies ran while one was open for 1% of the time, Pallas kernels for 0%

profile of v1, /device:TPU:0, one launch (start us, length us, event | category | flops | bytes accessed | tf_op | source)
XLA Modules:
  0.0 165.5 jit_solution(5751366588575263500)
XLA Ops:
  1.1 2.6 %collective-permute-start.1 = (bf16[128,1152]{1,0:T(8,128)(2,1)}, bf16[128,1152]{1,0:T(8,128)(2,1)S(1)}, u32[]{:S(2)}, u32[]{:S(2)}) collective-permute-start(bf16[128,1152]{1,0:T(8,128)(2,1)} %refs_0_.1), channel_id=1, source_target_pairs={{0,1},{4,5},{1,2},{5,6},{2,3},{6,7},{3,0},{7,4},{8,9},{12,13},{9,1... | collective-permute-start | bytes 884744 | tf_op jit(solution)/shard_map/ppermute | solution.py:166
  3.8 2.6 %collective-permute-start.3 = (bf16[128,1152]{1,0:T(8,128)(2,1)}, bf16[128,1152]{1,0:T(8,128)(2,1)S(1)}, u32[]{:S(2)}, u32[]{:S(2)}) collective-permute-start(bf16[128,1152]{1,0:T(8,128)(2,1)} %refs_0_.1), channel_id=1, source_target_pairs={{0,2},{4,6},{1,3},{5,7},{2,0},{6,4},{3,1},{7,5},{8,10},{12,14},{9,... | collective-permute-start | bytes 884744 | tf_op jit(solution)/shard_map/ppermute | solution.py:166
  6.4 1.3 collective-permute-start.5
  7.7 1.5 collective-permute-start.8
  9.3 4.7 %collective-permute-done.1.refs_2_ = bf16[128,1152]{1,0:T(8,128)(2,1)S(1)} collective-permute-done((bf16[128,1152]{1,0:T(8,128)(2,1)}, bf16[128,1152]{1,0:T(8,128)(2,1)S(1)}, u32[]{:S(2)}, u32[]{:S(2)}) %collective-permute-start.1) | collective-permute-done | bytes 294944 | tf_op jit(solution)/shard_map/ppermute | solution.py:166
  14.0 1.7 %collective-permute-start.10 = (bf16[128,1152]{1,0:T(8,128)(2,1)}, bf16[128,1152]{1,0:T(8,128)(2,1)S(1)}, u32[]{:S(2)}, u32[]{:S(2)}) collective-permute-start(bf16[128,1152]{1,0:T(8,128)(2,1)} %refs_8_.1), channel_id=1, source_target_pairs={{0,16},{4,20},{1,17},{5,21},{2,18},{6,22},{3,19},{7,23},{8,24},{12... | collective-permute-start | bytes 884744 | tf_op jit(solution)/shard_map/ppermute | solution.py:166
  15.7 10.7 %collective-permute-done.3.refs_4_ = bf16[128,1152]{1,0:T(8,128)(2,1)S(1)} collective-permute-done((bf16[128,1152]{1,0:T(8,128)(2,1)}, bf16[128,1152]{1,0:T(8,128)(2,1)S(1)}, u32[]{:S(2)}, u32[]{:S(2)}) %collective-permute-start.3) | collective-permute-done | bytes 294944 | tf_op jit(solution)/shard_map/ppermute | solution.py:166
  26.4 2.4 %collective-permute-start.12 = (bf16[128,1152]{1,0:T(8,128)(2,1)}, bf16[128,1152]{1,0:T(8,128)(2,1)S(1)}, u32[]{:S(2)}, u32[]{:S(2)}) collective-permute-start(bf16[128,1152]{1,0:T(8,128)(2,1)} %refs_8_.1), channel_id=1, source_target_pairs={{0,24},{4,28},{1,25},{5,29},{2,26},{6,30},{3,27},{7,31},{8,0},{12,... | collective-permute-start | bytes 884744 | tf_op jit(solution)/shard_map/ppermute | solution.py:166
  29.9 5.7 %collective-permute-done.12.refs_14_ = bf16[128,1152]{1,0:T(8,128)(2,1)S(1)} collective-permute-done((bf16[128,1152]{1,0:T(8,128)(2,1)}, bf16[128,1152]{1,0:T(8,128)(2,1)S(1)}, u32[]{:S(2)}, u32[]{:S(2)}) %collective-permute-start.12) | collective-permute-done | bytes 294944 | tf_op jit(solution)/shard_map/ppermute | solution.py:166
  37.4 0.6 pad_maximum_fusion.scalars
  38.2 0.6 copy-done.9
  39.1 0.7 copy-done.13
  39.8 28.9 %block.1 = (f32[288,1152]{1,0:T(8,128)}, bf16[288,1152]{1,0:T(8,128)(2,1)}, bf16[288,1152]{1,0:T(8,128)(2,1)}, bf16[288,1152]{1,0:T(8,128)(2,1)}, f32[8,128]{1,0:T(8,128)}) custom-call(f32[2]{0:T(128)} %pad_maximum_fusion.scalars, bf16[1152,1152]{1,0:T(8,128)(2,1)} %image_proj.1, bf16[1152,1152]{1,0:T(8,128)(2,1)} %text_proj.1, bf16[128,1152]{1,0:T(8,128)(2,1)} %refs_0_.1, ...), custom_call_target="tpu_custom_call" | custom-call | flops 12985565184 | bytes 15335424 | tf_op jit(solution)/shard_map/block/pallas_call | solution.py:130
  68.7 3.3 %collective-permute-start.16 = (bf16[288,1152]{1,0:T(8,128)(2,1)}, bf16[288,1152]{1,0:T(8,128)(2,1)S(1)}, u32[]{:S(2)}, u32[]{:S(2)}) collective-permute-start(bf16[288,1152]{1,0:T(8,128)(2,1)} %get-tuple-element.14), channel_id=1, source_target_pairs={{0,24},{4,28},{1,25},{5,29},{2,26},{6,30},{3,27},{7,31},{8,0},{12,... | collective-permute-start | bytes 1990664 | tf_op jit(solution)/shard_map/ppermute | solution.py:166
  72.7 74.0 %all-gather = f32[256,128]{1,0:T(8,128)S(1)} all-gather(f32[8,128]{1,0:T(8,128)} %get-tuple-element.10), channel_id=2, replica_groups=mesh['dp'=8,'mp'=4] {'dp','mp'}, dimensions={0}, use_global_device_ids=true | all-gather | bytes 135168 | tf_op jit(solution)/shard_map/all_gather | solution.py:179
  146.9 1.6 convert_add_fusion
  148.9 1.6 collective-permute-start.21
  150.6 2.4 %collective-permute-start.19 = (bf16[36,1152]{1,0:T(8,128)(2,1)S(1)}, bf16[36,1152]{1,0:T(8,128)(2,1)S(1)}, u32[]{:S(2)}, u32[]{:S(2)}) collective-permute-start(bf16[36,1152]{1,0:T(8,128)(2,1)S(1)} %get-tuple-element.22), channel_id=1, source_target_pairs={{0,3},{4,7},{1,0},{5,4},{2,1},{6,5},{3,2},{7,6},{8,11},{12,15},{9,... | collective-permute-start | bytes 248840 | tf_op jit(solution)/shard_map/ppermute | solution.py:166
  153.0 2.0 %collective-permute-done.23 = bf16[36,1152]{1,0:T(8,128)(2,1)S(1)} collective-permute-done((bf16[36,1152]{1,0:T(8,128)(2,1)S(1)}, bf16[36,1152]{1,0:T(8,128)(2,1)S(1)}, u32[]{:S(2)}, u32[]{:S(2)}) %collective-permute-start.23) | collective-permute-done | bytes 82976 | tf_op jit(solution)/shard_map/ppermute | solution.py:166
  155.0 0.7 collective-permute-start.17
  155.7 0.6 fusion.9
  156.3 1.6 collective-permute-done.19
  157.9 6.8 %collective-permute-done.18 = bf16[36,1152]{1,0:T(8,128)(2,1)S(1)} collective-permute-done((bf16[36,1152]{1,0:T(8,128)(2,1)S(1)}, bf16[36,1152]{1,0:T(8,128)(2,1)S(1)}, u32[]{:S(2)}, u32[]{:S(2)}) %collective-permute-start.18) | collective-permute-done | bytes 82976 | tf_op jit(solution)/shard_map/ppermute | solution.py:166
  164.7 0.8 broadcast_select_fusion
  (64 shorter events, 3.7 us)
Async XLA Ops:
  0.6 7.1 %collective-permute-start = (bf16[128,1152]{1,0:T(8,128)(2,1)}, bf16[128,1152]{1,0:T(8,128)(2,1)S(1)}, u32[]{:S(2)}, u32[]{:S(2)}) collective-permute-start(bf16[128,1152]{1,0:T(8,128)(2,1)} %refs_0_.1), channel_id=1, source_target_pairs={{0,4},{4,0},{1,5},{5,1},{2,6},{6,2},{3,7},{7,3},{8,12},{12,8},{9,1... | collective-permute-start | bytes 884744 | tf_op jit(solution)/shard_map/ppermute | solution.py:166
  1.1 12.9 %collective-permute-start.1 = (bf16[128,1152]{1,0:T(8,128)(2,1)}, bf16[128,1152]{1,0:T(8,128)(2,1)S(1)}, u32[]{:S(2)}, u32[]{:S(2)}) collective-permute-start(bf16[128,1152]{1,0:T(8,128)(2,1)} %refs_0_.1), channel_id=1, source_target_pairs={{0,1},{4,5},{1,2},{5,6},{2,3},{6,7},{3,0},{7,4},{8,9},{12,13},{9,1... | collective-permute-start | bytes 884744 | tf_op jit(solution)/shard_map/ppermute | solution.py:166
  3.8 22.6 %collective-permute-start.3 = (bf16[128,1152]{1,0:T(8,128)(2,1)}, bf16[128,1152]{1,0:T(8,128)(2,1)S(1)}, u32[]{:S(2)}, u32[]{:S(2)}) collective-permute-start(bf16[128,1152]{1,0:T(8,128)(2,1)} %refs_0_.1), channel_id=1, source_target_pairs={{0,2},{4,6},{1,3},{5,7},{2,0},{6,4},{3,1},{7,5},{8,10},{12,14},{9,... | collective-permute-start | bytes 884744 | tf_op jit(solution)/shard_map/ppermute | solution.py:166
  6.4 22.5 %collective-permute-start.5 = (bf16[128,1152]{1,0:T(8,128)(2,1)}, bf16[128,1152]{1,0:T(8,128)(2,1)S(1)}, u32[]{:S(2)}, u32[]{:S(2)}) collective-permute-start(bf16[128,1152]{1,0:T(8,128)(2,1)} %refs_0_.1), channel_id=1, source_target_pairs={{0,3},{4,7},{1,0},{5,4},{2,1},{6,5},{3,2},{7,6},{8,11},{12,15},{9,... | collective-permute-start | bytes 884744 | tf_op jit(solution)/shard_map/ppermute | solution.py:166
  7.7 21.1 %collective-permute-start.7 = (bf16[128,1152]{1,0:T(8,128)(2,1)}, bf16[128,1152]{1,0:T(8,128)(2,1)S(1)}, u32[]{:S(2)}, u32[]{:S(2)}) collective-permute-start(bf16[128,1152]{1,0:T(8,128)(2,1)} %refs_8_.1), channel_id=1, source_target_pairs={{0,4},{4,0},{1,5},{5,1},{2,6},{6,2},{3,7},{7,3},{8,12},{12,8},{9,1... | collective-permute-start | bytes 884744 | tf_op jit(solution)/shard_map/ppermute | solution.py:166
  7.7 21.6 %collective-permute-start.8 = (bf16[128,1152]{1,0:T(8,128)(2,1)}, bf16[128,1152]{1,0:T(8,128)(2,1)S(1)}, u32[]{:S(2)}, u32[]{:S(2)}) collective-permute-start(bf16[128,1152]{1,0:T(8,128)(2,1)} %refs_8_.1), channel_id=1, source_target_pairs={{0,8},{4,12},{1,9},{5,13},{2,10},{6,14},{3,11},{7,15},{8,16},{12,2... | collective-permute-start | bytes 884744 | tf_op jit(solution)/shard_map/ppermute | solution.py:166
  14.0 15.4 %collective-permute-start.10 = (bf16[128,1152]{1,0:T(8,128)(2,1)}, bf16[128,1152]{1,0:T(8,128)(2,1)S(1)}, u32[]{:S(2)}, u32[]{:S(2)}) collective-permute-start(bf16[128,1152]{1,0:T(8,128)(2,1)} %refs_8_.1), channel_id=1, source_target_pairs={{0,16},{4,20},{1,17},{5,21},{2,18},{6,22},{3,19},{7,23},{8,24},{12... | collective-permute-start | bytes 884744 | tf_op jit(solution)/shard_map/ppermute | solution.py:166
  26.4 9.2 %collective-permute-start.12 = (bf16[128,1152]{1,0:T(8,128)(2,1)}, bf16[128,1152]{1,0:T(8,128)(2,1)S(1)}, u32[]{:S(2)}, u32[]{:S(2)}) collective-permute-start(bf16[128,1152]{1,0:T(8,128)(2,1)} %refs_8_.1), channel_id=1, source_target_pairs={{0,24},{4,28},{1,25},{5,29},{2,26},{6,30},{3,27},{7,31},{8,0},{12,... | collective-permute-start | bytes 884744 | tf_op jit(solution)/shard_map/ppermute | solution.py:166
  28.8 6.7 %collective-permute-start.2 = (bf16[128,1152]{1,0:T(8,128)(2,1)S(1)}, bf16[128,1152]{1,0:T(8,128)(2,1)S(1)}, u32[]{:S(2)}, u32[]{:S(2)}) collective-permute-start(bf16[128,1152]{1,0:T(8,128)(2,1)S(1)} %collective-permute-done.1.refs_2_), channel_id=1, source_target_pairs={{0,4},{4,0},{1,5},{5,1},{2,6},{6,2},{3,7},{7,3},{8,12},{12,8},{9,1... | collective-permute-start | bytes 884744 | tf_op jit(solution)/shard_map/ppermute | solution.py:166
  28.9 9.1 %collective-permute-start.4 = (bf16[128,1152]{1,0:T(8,128)(2,1)S(1)}, bf16[128,1152]{1,0:T(8,128)(2,1)S(1)}, u32[]{:S(2)}, u32[]{:S(2)}) collective-permute-start(bf16[128,1152]{1,0:T(8,128)(2,1)S(1)} %collective-permute-done.3.refs_4_), channel_id=1, source_target_pairs={{0,4},{4,0},{1,5},{5,1},{2,6},{6,2},{3,7},{7,3},{8,12},{12,8},{9,1... | collective-permute-start | bytes 884744 | tf_op jit(solution)/shard_map/ppermute | solution.py:166
  29.4 8.6 %collective-permute-start.6 = (bf16[128,1152]{1,0:T(8,128)(2,1)S(1)}, bf16[128,1152]{1,0:T(8,128)(2,1)S(1)}, u32[]{:S(2)}, u32[]{:S(2)}) collective-permute-start(bf16[128,1152]{1,0:T(8,128)(2,1)S(1)} %collective-permute-done.5.refs_6_), channel_id=1, source_target_pairs={{0,4},{4,0},{1,5},{5,1},{2,6},{6,2},{3,7},{7,3},{8,12},{12,8},{9,1... | collective-permute-start | bytes 884744 | tf_op jit(solution)/shard_map/ppermute | solution.py:166
  29.5 8.6 %collective-permute-start.9 = (bf16[128,1152]{1,0:T(8,128)(2,1)S(1)}, bf16[128,1152]{1,0:T(8,128)(2,1)S(1)}, u32[]{:S(2)}, u32[]{:S(2)}) collective-permute-start(bf16[128,1152]{1,0:T(8,128)(2,1)S(1)} %collective-permute-done.8.refs_10_), channel_id=1, source_target_pairs={{0,4},{4,0},{1,5},{5,1},{2,6},{6,2},{3,7},{7,3},{8,12},{12,8},{9,1... | collective-permute-start | bytes 884744 | tf_op jit(solution)/shard_map/ppermute | solution.py:166
  35.6 2.5 %collective-permute-start.11 = (bf16[128,1152]{1,0:T(8,128)(2,1)S(1)}, bf16[128,1152]{1,0:T(8,128)(2,1)S(1)}, u32[]{:S(2)}, u32[]{:S(2)}) collective-permute-start(bf16[128,1152]{1,0:T(8,128)(2,1)S(1)} %collective-permute-done.10.refs_12_), channel_id=1, source_target_pairs={{0,4},{4,0},{1,5},{5,1},{2,6},{6,2},{3,7},{7,3},{8,12},{12,8},{9,1... | collective-permute-start | bytes 884744 | tf_op jit(solution)/shard_map/ppermute | solution.py:166
  35.6 2.5 %collective-permute-start.13 = (bf16[128,1152]{1,0:T(8,128)(2,1)S(1)}, bf16[128,1152]{1,0:T(8,128)(2,1)S(1)}, u32[]{:S(2)}, u32[]{:S(2)}) collective-permute-start(bf16[128,1152]{1,0:T(8,128)(2,1)S(1)} %collective-permute-done.12.refs_14_), channel_id=1, source_target_pairs={{0,4},{4,0},{1,5},{5,1},{2,6},{6,2},{3,7},{7,3},{8,12},{12,8},{9,1... | collective-permute-start | bytes 884744 | tf_op jit(solution)/shard_map/ppermute | solution.py:166
  68.7 78.2 %collective-permute-start.16 = (bf16[288,1152]{1,0:T(8,128)(2,1)}, bf16[288,1152]{1,0:T(8,128)(2,1)S(1)}, u32[]{:S(2)}, u32[]{:S(2)}) collective-permute-start(bf16[288,1152]{1,0:T(8,128)(2,1)} %get-tuple-element.14), channel_id=1, source_target_pairs={{0,24},{4,28},{1,25},{5,29},{2,26},{6,30},{3,27},{7,31},{8,0},{12,... | collective-permute-start | bytes 1990664 | tf_op jit(solution)/shard_map/ppermute | solution.py:166
  72.0 74.9 %collective-permute-start.15 = (bf16[288,1152]{1,0:T(8,128)(2,1)}, bf16[288,1152]{1,0:T(8,128)(2,1)S(1)}, u32[]{:S(2)}, u32[]{:S(2)}) collective-permute-start(bf16[288,1152]{1,0:T(8,128)(2,1)} %get-tuple-element.13), channel_id=1, source_target_pairs={{0,16},{4,20},{1,17},{5,21},{2,18},{6,22},{3,19},{7,23},{8,24},{12... | collective-permute-start | bytes 1990664 | tf_op jit(solution)/shard_map/ppermute | solution.py:166
  72.5 74.4 %collective-permute-start.14 = (bf16[288,1152]{1,0:T(8,128)(2,1)}, bf16[288,1152]{1,0:T(8,128)(2,1)S(1)}, u32[]{:S(2)}, u32[]{:S(2)}) collective-permute-start(bf16[288,1152]{1,0:T(8,128)(2,1)} %get-tuple-element.12), channel_id=1, source_target_pairs={{0,8},{4,12},{1,9},{5,13},{2,10},{6,14},{3,11},{7,15},{8,16},{12,2... | collective-permute-start | bytes 1990664 | tf_op jit(solution)/shard_map/ppermute | solution.py:166
  148.8 6.2 %collective-permute-start.23 = (bf16[36,1152]{1,0:T(8,128)(2,1)S(1)}, bf16[36,1152]{1,0:T(8,128)(2,1)S(1)}, u32[]{:S(2)}, u32[]{:S(2)}) collective-permute-start(bf16[36,1152]{1,0:T(8,128)(2,1)S(1)} %get-tuple-element.18), channel_id=1, source_target_pairs={{0,7},{4,3},{1,4},{5,0},{2,5},{6,1},{3,6},{7,2},{8,15},{12,11},{9,... | collective-permute-start | bytes 248840 | tf_op jit(solution)/shard_map/ppermute | solution.py:166
  148.8 6.1 %collective-permute-start.22 = (bf16[36,1152]{1,0:T(8,128)(2,1)S(1)}, bf16[36,1152]{1,0:T(8,128)(2,1)S(1)}, u32[]{:S(2)}, u32[]{:S(2)}) collective-permute-start(bf16[36,1152]{1,0:T(8,128)(2,1)S(1)} %get-tuple-element.19), channel_id=1, source_target_pairs={{0,6},{4,2},{1,7},{5,3},{2,4},{6,0},{3,5},{7,1},{8,14},{12,10},{9,... | collective-permute-start | bytes 248840 | tf_op jit(solution)/shard_map/ppermute | solution.py:166
  148.9 7.3 %collective-permute-start.21 = (bf16[36,1152]{1,0:T(8,128)(2,1)S(1)}, bf16[36,1152]{1,0:T(8,128)(2,1)S(1)}, u32[]{:S(2)}, u32[]{:S(2)}) collective-permute-start(bf16[36,1152]{1,0:T(8,128)(2,1)S(1)} %get-tuple-element.20), channel_id=1, source_target_pairs={{0,5},{4,1},{1,6},{5,2},{2,7},{6,3},{3,4},{7,0},{8,13},{12,9},{9,1... | collective-permute-start | bytes 248840 | tf_op jit(solution)/shard_map/ppermute | solution.py:166
  150.6 5.7 %collective-permute-start.20 = (bf16[36,1152]{1,0:T(8,128)(2,1)S(1)}, bf16[36,1152]{1,0:T(8,128)(2,1)S(1)}, u32[]{:S(2)}, u32[]{:S(2)}) collective-permute-start(bf16[36,1152]{1,0:T(8,128)(2,1)S(1)} %get-tuple-element.21), channel_id=1, source_target_pairs={{0,4},{4,0},{1,5},{5,1},{2,6},{6,2},{3,7},{7,3},{8,12},{12,8},{9,1... | collective-permute-start | bytes 248840 | tf_op jit(solution)/shard_map/ppermute | solution.py:166
  150.6 7.3 %collective-permute-start.19 = (bf16[36,1152]{1,0:T(8,128)(2,1)S(1)}, bf16[36,1152]{1,0:T(8,128)(2,1)S(1)}, u32[]{:S(2)}, u32[]{:S(2)}) collective-permute-start(bf16[36,1152]{1,0:T(8,128)(2,1)S(1)} %get-tuple-element.22), channel_id=1, source_target_pairs={{0,3},{4,7},{1,0},{5,4},{2,1},{6,5},{3,2},{7,6},{8,11},{12,15},{9,... | collective-permute-start | bytes 248840 | tf_op jit(solution)/shard_map/ppermute | solution.py:166
  155.0 9.7 %collective-permute-start.18 = (bf16[36,1152]{1,0:T(8,128)(2,1)S(1)}, bf16[36,1152]{1,0:T(8,128)(2,1)S(1)}, u32[]{:S(2)}, u32[]{:S(2)}) collective-permute-start(bf16[36,1152]{1,0:T(8,128)(2,1)S(1)} %get-tuple-element.23), channel_id=1, source_target_pairs={{0,2},{4,6},{1,3},{5,7},{2,0},{6,4},{3,1},{7,5},{8,10},{12,14},{9,... | collective-permute-start | bytes 248840 | tf_op jit(solution)/shard_map/ppermute | solution.py:166
  155.0 9.7 %collective-permute-start.17 = (bf16[36,1152]{1,0:T(8,128)(2,1)S(1)}, bf16[36,1152]{1,0:T(8,128)(2,1)S(1)}, u32[]{:S(2)}, u32[]{:S(2)}) collective-permute-start(bf16[36,1152]{1,0:T(8,128)(2,1)S(1)} %get-tuple-element.17), channel_id=1, source_target_pairs={{0,1},{4,5},{1,2},{5,6},{2,3},{6,7},{3,0},{7,4},{8,9},{12,13},{9,1... | collective-permute-start | bytes 248840 | tf_op jit(solution)/shard_map/ppermute | solution.py:166
  (14 other events, 111.4 us)

commit v2 on v1

v2 whole, which is shorter than its diff:
```python
import functools
import math

import jax
import jax.numpy as jnp
from jax import lax
from jax.experimental import pallas as pl
from jax.experimental.pallas import tpu as pltpu
from jax.sharding import PartitionSpec as P

F32 = jnp.float32
BF16 = jnp.bfloat16
AXES = ("dp", "mp")


class Layout:
    def __init__(self, dp_size, mp_size):
        self.dp, self.mp = dp_size, mp_size
        self.units = dp_size * mp_size // 2
        self.side = math.isqrt(self.units)
        if self.side * self.side != self.units or self.side % mp_size or self.side & (self.side - 1):
            raise ValueError("unsupported mesh")

    def device(self, unit, core):
        return (2 * (unit // self.mp) + core) * self.mp + unit % self.mp

    def send(self, value, step):
        s = self.side
        pairs = []
        for unit in range(self.units):
            for core in range(2):
                row, column, other = step(*divmod(unit, s), core)
                pairs.append((self.device(unit, core), self.device(row * s + column, other)))
        return lax.ppermute(value, AXES, pairs)

    def along_column(self, value, t):
        return self.send(value, lambda r, c, core: (r ^ t, c, core))

    def along_row(self, value, t):
        return self.send(value, lambda r, c, core: (r, c ^ t, core))

    def along_role(self, value, t):
        return self.send(value, lambda r, c, core: (r ^ t, c, 1) if core else (r, c ^ t, 0))

    def sibling(self, value):
        return self.send(value, lambda r, c, core: (r, c, 1 - core))


def tree_sum(values):
    values = list(values)
    while len(values) > 1:
        values = [a + b for a, b in zip(values[::2], values[1::2])]
    return values[0]


def load_projections(image_proj, text_proj, projs, sems):
    core = lax.rem(lax.axis_index("dp"), 2)
    own = pltpu.make_async_copy(image_proj, projs.at[core], sems.at[0])
    other = pltpu.make_async_copy(text_proj, projs.at[1 - core], sems.at[1])
    own.start()
    other.start()
    return own, other


def project(rows, projection):
    raw = jnp.dot(rows, projection, preferred_element_type=F32)
    inverse = lax.rsqrt(jnp.sum(raw * raw, axis=-1, keepdims=True) + 1e-06)
    return raw * inverse, inverse


def project_kernel(image_proj, text_proj, own, other, own_unit, own_inverse, other_half, projs, sems):
    for copy in load_projections(image_proj, text_proj, projs, sems):
        copy.wait()
    unit, _ = project(other[...], projs[1])
    other_half[...] = unit.astype(BF16)
    unit, inverse = project(own[...], projs[0])
    own_unit[...] = unit
    own_inverse[...] = jnp.broadcast_to(inverse, own_inverse.shape)


def project_chunks(image_proj, text_proj, own, other):
    rows, width = own.shape
    anywhere = pl.BlockSpec(memory_space=pl.ANY)
    vmem = pl.BlockSpec(memory_space=pltpu.VMEM)
    return pl.pallas_call(
        project_kernel,
        out_shape=[
            jax.ShapeDtypeStruct((rows, width), F32),
            jax.ShapeDtypeStruct((rows, 128), F32),
            jax.ShapeDtypeStruct((rows, width), BF16),
        ],
        in_specs=[anywhere] * 2 + [vmem] * 2,
        out_specs=[vmem] * 3,
        scratch_shapes=[pltpu.VMEM((2, width, width), BF16), pltpu.SemaphoreType.DMA((2,))],
        compiler_params=pltpu.CompilerParams(vmem_limit_bytes=20 * 1024 * 1024),
        cost_estimate=pl.CostEstimate(
            flops=4 * rows * width * width,
            bytes_accessed=4 * width * width + 10 * rows * width,
            transcendentals=2 * rows,
        ),
        name="project",
    )(image_proj, text_proj, own, other)


def pair_terms(cosine, scale, bias, masked):
    logits = scale * cosine + bias
    small = jnp.exp(-jnp.abs(logits))
    inverse_sum = 1.0 / (1.0 + small)
    large_side = logits >= 0.0
    pair_grads = jnp.where(large_side, inverse_sum, small * inverse_sum)
    tops = jnp.maximum(logits, 0.0)
    if masked:
        equal = lax.broadcasted_iota(jnp.int32, cosine.shape, 0) == lax.broadcasted_iota(
            jnp.int32, cosine.shape, 1
        )
        lower = jnp.where(large_side, small * inverse_sum, inverse_sum)
        pair_grads = jnp.where(equal, -lower, pair_grads)
        tops = jnp.where(equal, jnp.maximum(-logits, 0.0), tops)
    return tops + jnp.log1p(small), pair_grads


def lane_sums(values):
    total = jnp.sum(values, axis=0, keepdims=True)
    return sum(total[:, j : j + 128] for j in range(0, total.shape[1], 128))


def block_kernel(side, mp_size, first_width, scalars, image_proj, text_proj, *refs):
    own_chunks, refs = refs[:side], refs[side:]
    last_other, refs = refs[0], refs[1:]
    own_units, refs = refs[: side - 1], refs[side - 1 :]
    own_inverses, refs = refs[: side - 1], refs[side - 1 :]
    other_halves, refs = refs[: side - 1], refs[side - 1 :]
    firsts, refs = refs[:side], refs[side:]
    lates, refs = refs[:side], refs[side:]
    stats, projs, last, feats, units, inverses, other_half, dy, grad, piece, sems = refs
    rows, width = dy.shape
    chunk_rows = rows // side
    rest = rows - chunk_rows
    dp_index, mp_index = lax.axis_index("dp"), lax.axis_index("mp")
    unit_index = dp_index // 2 * mp_size + mp_index
    unit_row, unit_column = unit_index // side, lax.rem(unit_index, side)
    scale, bias = scalars[0], scalars[1]

    count = 2

    def start(source, target):
        nonlocal count
        copy = pltpu.make_async_copy(source, target, sems.at[count])
        copy.start()
        count += 1
        return copy

    def places(i):
        return pl.ds(i * chunk_rows, chunk_rows)

    last_copy = start(last_other, last)
    own_copies = [start(own_chunks[side - 1], feats.at[places(side - 1)])]
    proj_copies = load_projections(image_proj, text_proj, projs, sems)
    other_copies = [start(other_halves[i], other_half.at[places(i)]) for i in range(side - 1)]
    unit_copies = [start(own_units[i], units.at[places(i)]) for i in range(side - 1)]
    unit_copies += [start(own_inverses[i], inverses.at[places(i)]) for i in range(side - 1)]
    feat_copies = [start(own_chunks[i], feats.at[places(i)]) for i in range(side - 1)]

    for copy in [last_copy, *own_copies, *proj_copies]:
        copy.wait()
    unit, _ = project(last[...], projs[1])
    other_half[rest:, :] = unit.astype(BF16)
    unit, inverse = project(feats[rest:, :], projs[0])
    units[rest:, :] = unit
    inverses[rest:, :] = jnp.broadcast_to(inverse, (chunk_rows, 128))
    for copy in other_copies + unit_copies:
        copy.wait()

    def tile(place, with_partners):
        unit = units[place, :]
        cosine = lax.dot_general(
            unit.astype(BF16), other_half[...], (((1,), (1,)), ((), ())), preferred_element_type=F32
        )
        if with_partners:
            terms = [
                pair_terms(cosine[:, :chunk_rows], scale, bias, True),
                pair_terms(cosine[:, chunk_rows:], scale, bias, False),
            ]
            losses, pair_grads = [jnp.concatenate(x, axis=1) for x in zip(*terms)]
        else:
            losses, pair_grads = pair_terms(cosine, scale, bias, False)
        half_grads = pair_grads.astype(BF16)
        sums = jnp.concatenate(
            [lane_sums(losses), lane_sums(pair_grads * cosine) * scale, lane_sums(pair_grads)], axis=1
        )
        stats[0:1, :] = sums if with_partners else stats[0:1, :] + sums
        inner = jnp.sum(half_grads.astype(F32) * cosine, axis=-1, keepdims=True)
        grads = jnp.dot(half_grads, other_half[...], preferred_element_type=F32)
        dy[place, :] = ((grads - unit * inner) * (scale * inverses[place, 0:1])).astype(BF16)

    tile(pl.ds(0, chunk_rows), True)

    @pl.loop(1, side)
    def _(i):
        tile(pl.ds(pl.multiple_of(i * chunk_rows, chunk_rows), chunk_rows), False)

    for copy in feat_copies:
        copy.wait()
    for j in range(0, width, 128):
        grad[j : j + 128, :] = lax.dot_general(
            feats[:, j : j + 128], dy[...], (((0,), (0,)), ((), ())), preferred_element_type=F32
        )

    sums = stats[0:1, :]
    stats[...] = jnp.broadcast_to(sums, stats.shape)
    chunk = width // side
    for t in range(side):
        first = pl.multiple_of(jnp.bitwise_xor(unit_row, t) * chunk, chunk)
        firsts[t][:chunk, :] = grad[pl.ds(first, chunk), :first_width].astype(firsts[t].dtype)
        if t:
            firsts[t][chunk:, :] = stat_rows(sums, first_width).astype(BF16)

    out_rows = chunk // (2 * side)
    for column in range(side):
        for i in range(side):
            for core in range(2):
                source = i * chunk + shard_of(column, core, mp_size) * out_rows
                target = (2 * i + core) * out_rows
                piece[target : target + out_rows, :] = grad[source : source + out_rows, first_width:]
        store_for(column, unit_column, piece, lates)


def shard_of(column, core, mp_size):
    return column // mp_size * 2 * mp_size + core * mp_size + column % mp_size


def store_for(index, own_index, piece, outs):
    for t, out in enumerate(outs):

        @pl.when(jnp.bitwise_xor(own_index, t) == index)
        def _():
            out[...] = piece[...].astype(out.dtype)


def stat_rows(sums, width):
    part0 = sums.astype(BF16).astype(F32)
    part1 = (sums - part0).astype(BF16).astype(F32)
    part2 = sums - part0 - part1
    line = lax.broadcasted_iota(jnp.int32, (8, sums.shape[1]), 0)
    parts = jnp.where(line == 0, part0, jnp.where(line == 1, part1, jnp.where(line == 2, part2, 0.0)))
    if width > sums.shape[1]:
        parts = jnp.concatenate([parts, jnp.zeros((8, width - sums.shape[1]), F32)], axis=1)
    return parts


def block_grads(
    layout, first_width, scalars, image_proj, text_proj, own_chunks, last_other, projected
):
    side = layout.side
    chunk_rows, width = own_chunks[0].shape
    rows = side * chunk_rows
    chunk = width // side
    anywhere = pl.BlockSpec(memory_space=pl.ANY)
    vmem = pl.BlockSpec(memory_space=pltpu.VMEM)
    late_width = width - first_width
    operands = [image_proj, text_proj, *own_chunks, last_other]
    operands += [x for column in zip(*projected) for x in column]
    return pl.pallas_call(
        functools.partial(block_kernel, side, layout.mp, first_width),
        out_shape=[jax.ShapeDtypeStruct((chunk, first_width), F32)]
        + [jax.ShapeDtypeStruct((chunk + 8, first_width), BF16)] * (side - 1)
        + [jax.ShapeDtypeStruct((chunk, late_width), F32)]
        + [jax.ShapeDtypeStruct((chunk, late_width), BF16)] * (side - 1)
        + [jax.ShapeDtypeStruct((8, 384), F32)],
        in_specs=[pl.BlockSpec(memory_space=pltpu.SMEM)] + [anywhere] * len(operands),
        out_specs=[vmem] * (2 * side + 1),
        scratch_shapes=[
            pltpu.VMEM((2, width, width), BF16),
            pltpu.VMEM((chunk_rows, width), BF16),
            pltpu.VMEM((rows, width), BF16),
            pltpu.VMEM((rows, width), F32),
            pltpu.VMEM((rows, 128), F32),
            pltpu.VMEM((rows, width), BF16),
            pltpu.VMEM((rows, width), BF16),
            pltpu.VMEM((width, width), F32),
            pltpu.VMEM((chunk, late_width), F32),
            pltpu.SemaphoreType.DMA((len(operands),)),
        ],
        compiler_params=pltpu.CompilerParams(vmem_limit_bytes=56 * 1024 * 1024),
        cost_estimate=pl.CostEstimate(
            flops=2 * rows * width * (2 * rows + width) + 4 * chunk_rows * width * width,
            bytes_accessed=8 * rows * width + 8 * width * width,
            transcendentals=3 * rows * rows,
        ),
        name="block",
    )(scalars, *operands)


def arrived_sum(own, arrived, rows):
    return tree_sum([own[:rows, :]] + [x[:rows, :].astype(F32) for x in arrived])


def first_kernel(side, mp_size, own, own_stats, *refs):
    arrived, outs = refs[: side - 1], refs[side - 1 : 2 * side - 1]
    stats, total, piece = refs[2 * side - 1 :]
    chunk, width = own.shape
    out_rows = chunk // (2 * side)
    total[...] = arrived_sum(own, arrived, chunk)
    parts = [x[chunk:, :384].astype(F32) for x in arrived]
    sums = tree_sum([own_stats[0:1, :]] + [x[0:1] + x[1:2] + x[2:3] for x in parts])
    stats[...] = jnp.broadcast_to(sums, stats.shape)
    dp_index, mp_index = lax.axis_index("dp"), lax.axis_index("mp")
    unit_column = lax.rem(dp_index // 2 * mp_size + mp_index, side)
    piece[2 * out_rows :, :] = jnp.zeros((piece.shape[0] - 2 * out_rows, width), F32)
    piece[piece.shape[0] - 8 :, :] = stat_rows(sums, width)
    for column in range(side):
        for core in range(2):
            source = shard_of(column, core, mp_size) * out_rows
            piece[core * out_rows : (core + 1) * out_rows, :] = total[source : source + out_rows, :]
        store_for(column, unit_column, piece, outs)


def first_pieces(layout, own, own_stats, arrived):
    side = layout.side
    chunk, width = own.shape
    rows = (2 * (chunk // (2 * side)) + 7) // 8 * 8 + 8
    vmem = pl.BlockSpec(memory_space=pltpu.VMEM)
    return pl.pallas_call(
        functools.partial(first_kernel, side, layout.mp),
        out_shape=[jax.ShapeDtypeStruct((rows, width), F32)]
        + [jax.ShapeDtypeStruct((rows, width), BF16)] * (side - 1)
        + [jax.ShapeDtypeStruct((8, 384), F32)],
        in_specs=[vmem] * (side + 1),
        out_specs=[vmem] * (side + 1),
        scratch_shapes=[pltpu.VMEM((chunk, width), F32), pltpu.VMEM((rows, width), F32)],
        compiler_params=pltpu.CompilerParams(vmem_limit_bytes=12 * 1024 * 1024),
        name="first",
    )(own, own_stats, *arrived)


def late_kernel(side, mp_size, own, *refs):
    arrived, outs, total = refs[: side - 1], refs[side - 1 : 2 * side - 1], refs[-1]
    chunk = own.shape[0]
    total[...] = arrived_sum(own, arrived, chunk)
    dp_index, mp_index = lax.axis_index("dp"), lax.axis_index("mp")
    unit_row = (dp_index // 2 * mp_size + mp_index) // side
    rows = chunk // side
    for row in range(side):
        store_for(row, unit_row, total.at[row * rows : (row + 1) * rows, :], outs)


def late_pieces(layout, own, arrived):
    side = layout.side
    chunk, width = own.shape
    rows = chunk // side
    vmem = pl.BlockSpec(memory_space=pltpu.VMEM)
    return pl.pallas_call(
        functools.partial(late_kernel, side, layout.mp),
        out_shape=[jax.ShapeDtypeStruct((rows, width), F32)]
        + [jax.ShapeDtypeStruct((rows, width), BF16)] * (side - 1),
        in_specs=[vmem] * side,
        out_specs=[vmem] * side,
        scratch_shapes=[pltpu.VMEM((chunk, width), F32)],
        compiler_params=pltpu.CompilerParams(vmem_limit_bytes=12 * 1024 * 1024),
        name="late",
    )(own, *arrived)


def per_device(layout, image_feats, text_feats, image_proj, text_proj, log_scale, logit_bias):
    side = layout.side
    own_rows, width = image_feats.shape
    devices = layout.dp * layout.mp
    out_rows = width // devices
    batch_total = own_rows * devices
    is_image = lax.axis_index("dp") % 2 == 0

    scalars = jnp.concatenate([jnp.exp(log_scale), logit_bias])
    sibling_image, sibling_text = layout.sibling(image_feats), layout.sibling(text_feats)
    own_unit = jnp.concatenate(
        [jnp.where(is_image, image_feats, sibling_text), jnp.where(is_image, sibling_image, text_feats)]
    )
    other_unit = jnp.concatenate(
        [jnp.where(is_image, text_feats, sibling_image), jnp.where(is_image, sibling_text, image_feats)]
    )
    own_chunks, other_chunks = {0: own_unit}, {0: other_unit}
    bit = side // 2
    projected = {}
    while bit:
        sources = list(own_chunks)
        if bit == 1:
            own_chunks[1] = layout.along_role(own_unit, 1)
            projected[0] = project_chunks(image_proj, text_proj, own_unit, other_unit)
            own_chunks, projected = lax.optimization_barrier((own_chunks, projected))
        for t in sources:
            if t ^ bit not in own_chunks:
                own_chunks[t ^ bit] = layout.along_role(own_chunks[t], bit)
        bit //= 2
    last = side - 1
    for t in range(1, last):
        other_chunks[t] = layout.sibling(own_chunks[t])
        projected[t] = project_chunks(image_proj, text_proj, own_chunks[t], other_chunks[t])
    own_chunks[last], projected = lax.optimization_barrier((own_chunks[last], projected))
    other_chunks[last] = layout.sibling(own_chunks[last])
    first_width = width - width // 3
    results = block_grads(
        layout,
        first_width,
        scalars,
        image_proj,
        text_proj,
        [own_chunks[t] for t in range(side)],
        other_chunks[last],
        [projected[t] for t in range(last)],
    )
    firsts, lates, stats = list(results[:side]), list(results[side : 2 * side]), results[-1]

    firsts[1:] = [layout.along_column(firsts[t], t) for t in range(1, side)]
    lates[1:] = [layout.along_row(lates[t], t) for t in range(1, side)]
    *firsts, stats = first_pieces(layout, firsts[0], stats, firsts[1:])
    lates = list(late_pieces(layout, lates[0], lates[1:]))

    firsts[1:] = [layout.along_row(firsts[t], t) for t in range(1, side)]
    lates[1:] = [layout.along_column(lates[t], t) for t in range(1, side)]
    last_rows = 2 * out_rows
    first_sum = tree_sum([x[:last_rows].astype(F32) for x in firsts])
    late_sum = tree_sum([x.astype(F32) for x in lates])
    total = jnp.concatenate([first_sum, late_sum], axis=1)
    parts = [x[-8:-5, :384].astype(F32) for x in firsts[1:]]
    stat_total = tree_sum([stats[0]] + [x[0] + x[1] + x[2] for x in parts])

    upper, lower = total[:out_rows], total[out_rows:]
    keep, give = jnp.where(is_image, upper, lower), jnp.where(is_image, lower, upper)
    got = layout.sibling(give)
    image_proj_grad = jnp.where(is_image, keep, got)
    text_proj_grad = jnp.where(is_image, got, keep)
    stat_total = stat_total + layout.sibling(stat_total)
    totals = jnp.sum(stat_total.reshape(3, 128), axis=1) * (0.5 / batch_total)
    return totals[0:1], image_proj_grad, text_proj_grad, totals[1:2], totals[2:3]


def solution(mesh):
    layout = Layout(mesh.shape["dp"], mesh.shape["mp"])
    return jax.shard_map(
        functools.partial(per_device, layout),
        mesh=mesh,
        in_specs=(P(AXES, None), P(AXES, None), P(), P(), P(), P()),
        out_specs=(P(), P(AXES, None), P(AXES, None), P(), P()),
        check_vma=False,
    )
```

time: 166 us -> 105 us (0.63)
  blocking collectives: 74 us -> 0 us
  starting transfers between devices: 23.1 us -> 31.8 us
  local copies, waits for them, and re-layouts: 2.56 us -> 8.99 us
    all_gather x1 -> x0, blocking collectives: 74 us -> none  [per_device(): all_stats = lax.all_gather(stats, AXES, axis=0)]
    ppermute x24 -> x22, starting transfers between devices: 23.1 us -> 31.8 us  [send(): return lax.ppermute(value, AXES, pairs)]
    unnamed x28 -> x40, local copies, waits for them, and re-layouts: 1.64 us -> 8.4 us
    ppermute x24 -> x22, waiting for transfers between devices: 31.6 us -> 30.1 us  [send(): return lax.ppermute(value, AXES, pairs)]
    pallas_call x1 -> x6, Pallas kernels: 28.9 us -> 28.8 us  [the longest x1 20.8 us: block_grads(): pl.pallas_call(functools.partial(block_kernel, side, layout.mp, first_wid...]
  transfers between devices with their start and end apart: 24 -> 22, of which waited for: 6 -> 9; matrix products, arithmetic and copies ran while one was open for 1% -> 2% of each run, Pallas kernels for 0% -> 8%
where the time goes in v2:
time: 105 us
  starting transfers between devices  31.8 us (30%)
  waiting for transfers between devices  30.1 us (29%)
  Pallas kernels  28.8 us (27%)
  local copies, waits for them, and re-layouts  8.99 us (9%)
  other arithmetic  2.81 us (3%)
  between operations  2.28 us (2%)
    ppermute x22, starting transfers between devices, send(): return lax.ppermute(value, AXES, pairs)  31.8 us
    ppermute x22, waiting for transfers between devices, send(): return lax.ppermute(value, AXES, pairs)  30.1 us
    pallas_call x1, Pallas kernels, block_grads(): pl.pallas_call(functools.partial(block_kernel, side, layout.mp, first_wid...  20.8 us
    unnamed x40, local copies, waits for them, and re-layouts  8.4 us
    pallas_call x3, Pallas kernels, project_chunks(): pl.pallas_call(project_kernel, out_shape=[jax.ShapeDtypeStruct((rows, wid...  7.31 us
  transfers between devices with their start and end apart: 22, of which 9 were waited for; matrix products, arithmetic and copies ran while one was open for 2% of the time, Pallas kernels for 8%

profile of v2, /device:TPU:0, one launch (start us, length us, event | category | flops | bytes accessed | tf_op | source)
XLA Modules:
  0.0 104.7 jit_solution(6427006037265963828)
XLA Ops:
  1.2 1.3 %collective-permute-done.1 = bf16[128,1152]{1,0:T(8,128)(2,1)S(1)} collective-permute-done((bf16[128,1152]{1,0:T(8,128)(2,1)}, bf16[128,1152]{1,0:T(8,128)(2,1)S(1)}, u32[]{:S(2)}, u32[]{:S(2)}) %collective-permute-start.1) | collective-permute-done | bytes 294944 | tf_op jit(solution)/shard_map/ppermute | solution.py:34
  2.6 1.0 broadcast_select_fusion.1
  3.8 4.0 %collective-permute-start.3 = (bf16[256,1152]{1,0:T(8,128)(2,1)S(1)}, bf16[256,1152]{1,0:T(8,128)(2,1)S(1)}, u32[]{:S(2)}, u32[]{:S(2)}) collective-permute-start(bf16[256,1152]{1,0:T(8,128)(2,1)S(1)} %pad_maximum_fusion.own.refs_0_), channel_id=1, source_target_pairs={{0,2},{4,20},{1,3},{5,21},{2,0},{6,22},{3,1},{7,23},{8,10},{12,28}... | collective-permute-start | bytes 1769480 | tf_op jit(solution)/shard_map/ppermute | solution.py:34
  7.8 1.6 %collective-permute-start.2 = (bf16[256,1152]{1,0:T(8,128)(2,1)S(1)}, bf16[256,1152]{1,0:T(8,128)(2,1)S(1)}, u32[]{:S(2)}, u32[]{:S(2)}) collective-permute-start(bf16[256,1152]{1,0:T(8,128)(2,1)S(1)} %pad_maximum_fusion.own.refs_0_), channel_id=1, source_target_pairs={{0,1},{4,12},{1,0},{5,13},{2,3},{6,14},{3,2},{7,15},{8,9},{12,4},{... | collective-permute-start | bytes 1769480 | tf_op jit(solution)/shard_map/ppermute | solution.py:34
  9.4 1.7 %copy-done.1 = bf16[1152,1152]{1,0:T(8,128)(2,1)S(1)} copy-done((bf16[1152,1152]{1,0:T(8,128)(2,1)S(1)}, bf16[1152,1152]{1,0:T(8,128)(2,1)}, u32[]{:S(2)}) %copy-start.1) | copy-done | bytes 2654232
  11.2 2.4 %project.3 = (f32[256,1152]{1,0:T(8,128)S(1)}, f32[256,128]{1,0:T(8,128)S(1)}, bf16[256,1152]{1,0:T(8,128)(2,1)S(1)}) custom-call(bf16[1152,1152]{1,0:T(8,128)(2,1)S(1)} %copy-done, bf16[1152,1152]{1,0:T(8,128)(2,1)S(1)} %copy-done.1, bf16[256,1152]{1,0:T(8,128)(2,1)S(1)} %pad_maximum_fusion.own.refs_0_, bf16[256,1152]{1,0:T(8,128)(2,1)S(1)} %pad_maximum_fusion.1.other), custom_call_target="tpu_custom_call" | custom-call | flops 1358954496 | bytes 8257536 | tf_op jit(solution)/shard_map/project/pallas_call | solution.py:85
  15.1 6.9 %collective-permute-done.3.own.refs_2_ = bf16[256,1152]{1,0:T(8,128)(2,1)S(1)} collective-permute-done((bf16[256,1152]{1,0:T(8,128)(2,1)S(1)}, bf16[256,1152]{1,0:T(8,128)(2,1)S(1)}, u32[]{:S(2)}, u32[]{:S(2)}) %collective-permute-start.3) | collective-permute-done | bytes 589856 | tf_op jit(solution)/shard_map/ppermute | solution.py:34
  23.1 1.5 %collective-permute-start.4 = (bf16[256,1152]{1,0:T(8,128)(2,1)S(1)}, bf16[256,1152]{1,0:T(8,128)(2,1)S(1)}, u32[]{:S(2)}, u32[]{:S(2)}) collective-permute-start(bf16[256,1152]{1,0:T(8,128)(2,1)S(1)} %collective-permute-done.3.own.refs_2_), channel_id=1, source_target_pairs={{0,1},{4,12},{1,0},{5,13},{2,3},{6,14},{3,2},{7,15},{8,9},{12,4},{... | collective-permute-start | bytes 1769480 | tf_op jit(solution)/shard_map/ppermute | solution.py:34
  24.6 2.4 %project.5 = (f32[256,1152]{1,0:T(8,128)S(1)}, f32[256,128]{1,0:T(8,128)S(1)}, bf16[256,1152]{1,0:T(8,128)(2,1)S(1)}) custom-call(bf16[1152,1152]{1,0:T(8,128)(2,1)S(1)} %copy-done, bf16[1152,1152]{1,0:T(8,128)(2,1)S(1)} %copy-done.1, bf16[256,1152]{1,0:T(8,128)(2,1)S(1)} %collective-permute-done.3.own.refs_2_, ...), custom_call_target="tpu_custom_call" | custom-call | flops 1358954496 | bytes 8257536 | tf_op jit(solution)/shard_map/project/pallas_call | solution.py:85
  27.1 2.5 %project.4 = (f32[256,1152]{1,0:T(8,128)S(1)}, f32[256,128]{1,0:T(8,128)S(1)}, bf16[256,1152]{1,0:T(8,128)(2,1)S(1)}) custom-call(bf16[1152,1152]{1,0:T(8,128)(2,1)S(1)} %copy-done, bf16[1152,1152]{1,0:T(8,128)(2,1)S(1)} %copy-done.1, bf16[256,1152]{1,0:T(8,128)(2,1)S(1)} %collective-permute-done.2.own.refs_1_, ...), custom_call_target="tpu_custom_call" | custom-call | flops 1358954496 | bytes 8257536 | tf_op jit(solution)/shard_map/project/pallas_call | solution.py:85
  35.8 20.8 %block.1 = (f32[288,768]{1,0:T(8,128)}, bf16[296,768]{1,0:T(8,128)(2,1)}, bf16[296,768]{1,0:T(8,128)(2,1)}, bf16[296,768]{1,0:T(8,128)(2,1)}, f32[288,384]{1,0:T...) custom-call(f32[2]{0:T(128)} %pad_maximum_fusion.3.scalars, ...), custom_call_target="tpu_custom_call" | custom-call | flops 8908701696 | bytes 20054016 | tf_op jit(solution)/shard_map/block/pallas_call | solution.py:263
  56.6 1.9 %collective-permute-start.8 = (bf16[296,768]{1,0:T(8,128)(2,1)}, bf16[296,768]{1,0:T(8,128)(2,1)S(1)}, u32[]{:S(2)}, u32[]{:S(2)}) collective-permute-start(bf16[296,768]{1,0:T(8,128)(2,1)} %get-tuple-element.75), channel_id=1, source_target_pairs={{0,8},{4,12},{1,9},{5,13},{2,10},{6,14},{3,11},{7,15},{8,0},{12,4}... | collective-permute-start | bytes 1363976 | tf_op jit(solution)/shard_map/ppermute | solution.py:34
  58.5 1.2 %collective-permute-start.15 = (bf16[288,384]{1,0:T(8,128)(2,1)}, bf16[288,384]{1,0:T(8,128)(2,1)S(1)}, u32[]{:S(2)}, u32[]{:S(2)}) collective-permute-start(bf16[288,384]{1,0:T(8,128)(2,1)} %get-tuple-element.84), channel_id=1, source_target_pairs={{0,1},{4,5},{1,0},{5,4},{2,3},{6,7},{3,2},{7,6},{8,9},{12,13},{9,8... | collective-permute-start | bytes 663560 | tf_op jit(solution)/shard_map/ppermute | solution.py:34
  59.6 1.5 %collective-permute-start.9 = (bf16[296,768]{1,0:T(8,128)(2,1)}, bf16[296,768]{1,0:T(8,128)(2,1)S(1)}, u32[]{:S(2)}, u32[]{:S(2)}) collective-permute-start(bf16[296,768]{1,0:T(8,128)(2,1)} %get-tuple-element.76), channel_id=1, source_target_pairs={{0,16},{4,20},{1,17},{5,21},{2,18},{6,22},{3,19},{7,23},{8,24},{12... | collective-permute-start | bytes 1363976 | tf_op jit(solution)/shard_map/ppermute | solution.py:34
  61.6 2.4 %collective-permute-start.16 = (bf16[288,384]{1,0:T(8,128)(2,1)}, bf16[288,384]{1,0:T(8,128)(2,1)S(1)}, u32[]{:S(2)}, u32[]{:S(2)}) collective-permute-start(bf16[288,384]{1,0:T(8,128)(2,1)} %get-tuple-element.85), channel_id=1, source_target_pairs={{0,2},{4,6},{1,3},{5,7},{2,0},{6,4},{3,1},{7,5},{8,10},{12,14},{9,... | collective-permute-start | bytes 663560 | tf_op jit(solution)/shard_map/ppermute | solution.py:34
  64.0 5.0 %collective-permute-done.15.refs_0_ = bf16[288,384]{1,0:T(8,128)(2,1)S(1)} collective-permute-done((bf16[288,384]{1,0:T(8,128)(2,1)}, bf16[288,384]{1,0:T(8,128)(2,1)S(1)}, u32[]{:S(2)}, u32[]{:S(2)}) %collective-permute-start.15) | collective-permute-done | bytes 221216 | tf_op jit(solution)/shard_map/ppermute | solution.py:34
  69.0 2.6 %collective-permute-start.17 = (bf16[288,384]{1,0:T(8,128)(2,1)}, bf16[288,384]{1,0:T(8,128)(2,1)S(1)}, u32[]{:S(2)}, u32[]{:S(2)}) collective-permute-start(bf16[288,384]{1,0:T(8,128)(2,1)} %get-tuple-element.86), channel_id=1, source_target_pairs={{0,3},{4,7},{1,2},{5,6},{2,1},{6,5},{3,0},{7,4},{8,11},{12,15},{9,... | collective-permute-start | bytes 663560 | tf_op jit(solution)/shard_map/ppermute | solution.py:34
  71.6 8.9 %collective-permute-done.16.refs_1_ = bf16[288,384]{1,0:T(8,128)(2,1)S(1)} collective-permute-done((bf16[288,384]{1,0:T(8,128)(2,1)}, bf16[288,384]{1,0:T(8,128)(2,1)S(1)}, u32[]{:S(2)}, u32[]{:S(2)}) %collective-permute-start.16) | collective-permute-done | bytes 221216 | tf_op jit(solution)/shard_map/ppermute | solution.py:34
  81.8 1.4 %collective-permute-start.18 = (bf16[72,384]{1,0:T(8,128)(2,1)S(1)}, bf16[72,384]{1,0:T(8,128)(2,1)S(1)}, u32[]{:S(2)}, u32[]{:S(2)}) collective-permute-start(bf16[72,384]{1,0:T(8,128)(2,1)S(1)} %get-tuple-element.88), channel_id=1, source_target_pairs={{0,8},{4,12},{1,9},{5,13},{2,10},{6,14},{3,11},{7,15},{8,0},{12,4}... | collective-permute-start | bytes 165896 | tf_op jit(solution)/shard_map/ppermute | solution.py:34
  83.2 1.5 %collective-permute-start.19 = (bf16[72,384]{1,0:T(8,128)(2,1)S(1)}, bf16[72,384]{1,0:T(8,128)(2,1)S(1)}, u32[]{:S(2)}, u32[]{:S(2)}) collective-permute-start(bf16[72,384]{1,0:T(8,128)(2,1)S(1)} %get-tuple-element.89), channel_id=1, source_target_pairs={{0,16},{4,20},{1,17},{5,21},{2,18},{6,22},{3,19},{7,23},{8,24},{12... | collective-permute-start | bytes 165896 | tf_op jit(solution)/shard_map/ppermute | solution.py:34
  86.6 3.7 %collective-permute-start.11 = (bf16[80,768]{1,0:T(8,128)(2,1)S(1)}, bf16[80,768]{1,0:T(8,128)(2,1)S(1)}, u32[]{:S(2)}, u32[]{:S(2)}) collective-permute-start(bf16[80,768]{1,0:T(8,128)(2,1)S(1)} %get-tuple-element.79), channel_id=1, source_target_pairs={{0,1},{4,5},{1,0},{5,4},{2,3},{6,7},{3,2},{7,6},{8,9},{12,13},{9,8... | collective-permute-start | bytes 368648 | tf_op jit(solution)/shard_map/ppermute | solution.py:34
  90.4 3.9 %collective-permute-start.12 = (bf16[80,768]{1,0:T(8,128)(2,1)S(1)}, bf16[80,768]{1,0:T(8,128)(2,1)S(1)}, u32[]{:S(2)}, u32[]{:S(2)}) collective-permute-start(bf16[80,768]{1,0:T(8,128)(2,1)S(1)} %get-tuple-element.80), channel_id=1, source_target_pairs={{0,2},{4,6},{1,3},{5,7},{2,0},{6,4},{3,1},{7,5},{8,10},{12,14},{9,... | collective-permute-start | bytes 368648 | tf_op jit(solution)/shard_map/ppermute | solution.py:34
  94.3 1.7 %collective-permute-start.13 = (bf16[80,768]{1,0:T(8,128)(2,1)S(1)}, bf16[80,768]{1,0:T(8,128)(2,1)S(1)}, u32[]{:S(2)}, u32[]{:S(2)}) collective-permute-start(bf16[80,768]{1,0:T(8,128)(2,1)S(1)} %get-tuple-element.81), channel_id=1, source_target_pairs={{0,3},{4,7},{1,2},{5,6},{2,1},{6,5},{3,0},{7,4},{8,11},{12,15},{9,... | collective-permute-start | bytes 368648 | tf_op jit(solution)/shard_map/ppermute | solution.py:34
  96.0 5.9 %collective-permute-done.12 = bf16[80,768]{1,0:T(8,128)(2,1)S(1)} collective-permute-done((bf16[80,768]{1,0:T(8,128)(2,1)S(1)}, bf16[80,768]{1,0:T(8,128)(2,1)S(1)}, u32[]{:S(2)}, u32[]{:S(2)}) %collective-permute-start.12) | collective-permute-done | bytes 122912 | tf_op jit(solution)/shard_map/ppermute | solution.py:34
  (82 shorter events, 14.5 us)
Async XLA Ops:
  0.6 1.9 %collective-permute-start.1 = (bf16[128,1152]{1,0:T(8,128)(2,1)}, bf16[128,1152]{1,0:T(8,128)(2,1)S(1)}, u32[]{:S(2)}, u32[]{:S(2)}) collective-permute-start(bf16[128,1152]{1,0:T(8,128)(2,1)} %param.6), channel_id=1, source_target_pairs={{0,4},{4,0},{1,5},{5,1},{2,6},{6,2},{3,7},{7,3},{8,12},{12,8},{9,1... | collective-permute-start | bytes 884744 | tf_op jit(solution)/shard_map/ppermute | solution.py:34
  1.2 2.4 %collective-permute-start = (bf16[128,1152]{1,0:T(8,128)(2,1)}, bf16[128,1152]{1,0:T(8,128)(2,1)S(1)}, u32[]{:S(2)}, u32[]{:S(2)}) collective-permute-start(bf16[128,1152]{1,0:T(8,128)(2,1)} %param.7), channel_id=1, source_target_pairs={{0,4},{4,0},{1,5},{5,1},{2,6},{6,2},{3,7},{7,3},{8,12},{12,8},{9,1... | collective-permute-start | bytes 884744 | tf_op jit(solution)/shard_map/ppermute | solution.py:34
  3.8 18.3 %collective-permute-start.3 = (bf16[256,1152]{1,0:T(8,128)(2,1)S(1)}, bf16[256,1152]{1,0:T(8,128)(2,1)S(1)}, u32[]{:S(2)}, u32[]{:S(2)}) collective-permute-start(bf16[256,1152]{1,0:T(8,128)(2,1)S(1)} %pad_maximum_fusion.own.refs_0_), channel_id=1, source_target_pairs={{0,2},{4,20},{1,3},{5,21},{2,0},{6,22},{3,1},{7,23},{8,10},{12,28}... | collective-permute-start | bytes 1769480 | tf_op jit(solution)/shard_map/ppermute | solution.py:34
  7.8 14.8 %collective-permute-start.2 = (bf16[256,1152]{1,0:T(8,128)(2,1)S(1)}, bf16[256,1152]{1,0:T(8,128)(2,1)S(1)}, u32[]{:S(2)}, u32[]{:S(2)}) collective-permute-start(bf16[256,1152]{1,0:T(8,128)(2,1)S(1)} %pad_maximum_fusion.own.refs_0_), channel_id=1, source_target_pairs={{0,1},{4,12},{1,0},{5,13},{2,3},{6,14},{3,2},{7,15},{8,9},{12,4},{... | collective-permute-start | bytes 1769480 | tf_op jit(solution)/shard_map/ppermute | solution.py:34
  15.1 11.9 %copy-start.8 = (f32[256,1152]{1,0:T(8,128)}, f32[256,1152]{1,0:T(8,128)S(1)}, u32[]{:S(2)}) copy-start(f32[256,1152]{1,0:T(8,128)S(1)} %get-tuple-element.64.refs_5_) | copy-start | bytes 3538948
  22.6 2.0 %collective-permute-start.6 = (bf16[256,1152]{1,0:T(8,128)(2,1)S(1)}, bf16[256,1152]{1,0:T(8,128)(2,1)S(1)}, u32[]{:S(2)}, u32[]{:S(2)}) collective-permute-start(bf16[256,1152]{1,0:T(8,128)(2,1)S(1)} %collective-permute-done.3.own.refs_2_), channel_id=1, source_target_pairs={{0,4},{4,0},{1,5},{5,1},{2,6},{6,2},{3,7},{7,3},{8,12},{12,8},{9,1... | collective-permute-start | bytes 1769480 | tf_op jit(solution)/shard_map/ppermute | solution.py:34
  22.6 4.5 %collective-permute-start.5 = (bf16[256,1152]{1,0:T(8,128)(2,1)S(1)}, bf16[256,1152]{1,0:T(8,128)(2,1)S(1)}, u32[]{:S(2)}, u32[]{:S(2)}) collective-permute-start(bf16[256,1152]{1,0:T(8,128)(2,1)S(1)} %collective-permute-done.2.own.refs_1_), channel_id=1, source_target_pairs={{0,4},{4,0},{1,5},{5,1},{2,6},{6,2},{3,7},{7,3},{8,12},{12,8},{9,1... | collective-permute-start | bytes 1769480 | tf_op jit(solution)/shard_map/ppermute | solution.py:34
  23.1 9.9 %collective-permute-start.4 = (bf16[256,1152]{1,0:T(8,128)(2,1)S(1)}, bf16[256,1152]{1,0:T(8,128)(2,1)S(1)}, u32[]{:S(2)}, u32[]{:S(2)}) collective-permute-start(bf16[256,1152]{1,0:T(8,128)(2,1)S(1)} %collective-permute-done.3.own.refs_2_), channel_id=1, source_target_pairs={{0,1},{4,12},{1,0},{5,13},{2,3},{6,14},{3,2},{7,15},{8,9},{12,4},{... | collective-permute-start | bytes 1769480 | tf_op jit(solution)/shard_map/ppermute | solution.py:34
  33.0 2.0 %collective-permute-start.7 = (bf16[256,1152]{1,0:T(8,128)(2,1)S(1)}, bf16[256,1152]{1,0:T(8,128)(2,1)S(1)}, u32[]{:S(2)}, u32[]{:S(2)}) collective-permute-start(bf16[256,1152]{1,0:T(8,128)(2,1)S(1)} %collective-permute-done.4.refs_3_), channel_id=1, source_target_pairs={{0,4},{4,0},{1,5},{5,1},{2,6},{6,2},{3,7},{7,3},{8,12},{12,8},{9,1... | collective-permute-start | bytes 1769480 | tf_op jit(solution)/shard_map/ppermute | solution.py:34
  56.5 28.8 %copy-start.3 = (f32[288,768]{1,0:T(8,128)S(1)}, f32[288,768]{1,0:T(8,128)}, u32[]{:S(2)}) copy-start(f32[288,768]{1,0:T(8,128)} %get-tuple-element.73.own) | copy-start | bytes 2654212
  56.6 28.1 %collective-permute-start.8 = (bf16[296,768]{1,0:T(8,128)(2,1)}, bf16[296,768]{1,0:T(8,128)(2,1)S(1)}, u32[]{:S(2)}, u32[]{:S(2)}) collective-permute-start(bf16[296,768]{1,0:T(8,128)(2,1)} %get-tuple-element.75), channel_id=1, source_target_pairs={{0,8},{4,12},{1,9},{5,13},{2,10},{6,14},{3,11},{7,15},{8,0},{12,4}... | collective-permute-start | bytes 1363976 | tf_op jit(solution)/shard_map/ppermute | solution.py:34
  58.5 10.5 %collective-permute-start.15 = (bf16[288,384]{1,0:T(8,128)(2,1)}, bf16[288,384]{1,0:T(8,128)(2,1)S(1)}, u32[]{:S(2)}, u32[]{:S(2)}) collective-permute-start(bf16[288,384]{1,0:T(8,128)(2,1)} %get-tuple-element.84), channel_id=1, source_target_pairs={{0,1},{4,5},{1,0},{5,4},{2,3},{6,7},{3,2},{7,6},{8,9},{12,13},{9,8... | collective-permute-start | bytes 663560 | tf_op jit(solution)/shard_map/ppermute | solution.py:34
  59.6 25.7 %collective-permute-start.9 = (bf16[296,768]{1,0:T(8,128)(2,1)}, bf16[296,768]{1,0:T(8,128)(2,1)S(1)}, u32[]{:S(2)}, u32[]{:S(2)}) collective-permute-start(bf16[296,768]{1,0:T(8,128)(2,1)} %get-tuple-element.76), channel_id=1, source_target_pairs={{0,16},{4,20},{1,17},{5,21},{2,18},{6,22},{3,19},{7,23},{8,24},{12... | collective-permute-start | bytes 1363976 | tf_op jit(solution)/shard_map/ppermute | solution.py:34
  61.1 24.2 %collective-permute-start.10 = (bf16[296,768]{1,0:T(8,128)(2,1)}, bf16[296,768]{1,0:T(8,128)(2,1)S(1)}, u32[]{:S(2)}, u32[]{:S(2)}) collective-permute-start(bf16[296,768]{1,0:T(8,128)(2,1)} %get-tuple-element.77), channel_id=1, source_target_pairs={{0,24},{4,28},{1,25},{5,29},{2,26},{6,30},{3,27},{7,31},{8,16},{12... | collective-permute-start | bytes 1363976 | tf_op jit(solution)/shard_map/ppermute | solution.py:34
  61.6 19.0 %collective-permute-start.16 = (bf16[288,384]{1,0:T(8,128)(2,1)}, bf16[288,384]{1,0:T(8,128)(2,1)S(1)}, u32[]{:S(2)}, u32[]{:S(2)}) collective-permute-start(bf16[288,384]{1,0:T(8,128)(2,1)} %get-tuple-element.85), channel_id=1, source_target_pairs={{0,2},{4,6},{1,3},{5,7},{2,0},{6,4},{3,1},{7,5},{8,10},{12,14},{9,... | collective-permute-start | bytes 663560 | tf_op jit(solution)/shard_map/ppermute | solution.py:34
  69.0 11.6 %collective-permute-start.17 = (bf16[288,384]{1,0:T(8,128)(2,1)}, bf16[288,384]{1,0:T(8,128)(2,1)S(1)}, u32[]{:S(2)}, u32[]{:S(2)}) collective-permute-start(bf16[288,384]{1,0:T(8,128)(2,1)} %get-tuple-element.86), channel_id=1, source_target_pairs={{0,3},{4,7},{1,2},{5,6},{2,1},{6,5},{3,0},{7,4},{8,11},{12,15},{9,... | collective-permute-start | bytes 663560 | tf_op jit(solution)/shard_map/ppermute | solution.py:34
  81.8 8.6 %collective-permute-start.18 = (bf16[72,384]{1,0:T(8,128)(2,1)S(1)}, bf16[72,384]{1,0:T(8,128)(2,1)S(1)}, u32[]{:S(2)}, u32[]{:S(2)}) collective-permute-start(bf16[72,384]{1,0:T(8,128)(2,1)S(1)} %get-tuple-element.88), channel_id=1, source_target_pairs={{0,8},{4,12},{1,9},{5,13},{2,10},{6,14},{3,11},{7,15},{8,0},{12,4}... | collective-permute-start | bytes 165896 | tf_op jit(solution)/shard_map/ppermute | solution.py:34
  83.2 7.1 %collective-permute-start.19 = (bf16[72,384]{1,0:T(8,128)(2,1)S(1)}, bf16[72,384]{1,0:T(8,128)(2,1)S(1)}, u32[]{:S(2)}, u32[]{:S(2)}) collective-permute-start(bf16[72,384]{1,0:T(8,128)(2,1)S(1)} %get-tuple-element.89), channel_id=1, source_target_pairs={{0,16},{4,20},{1,17},{5,21},{2,18},{6,22},{3,19},{7,23},{8,24},{12... | collective-permute-start | bytes 165896 | tf_op jit(solution)/shard_map/ppermute | solution.py:34
  84.7 5.6 %collective-permute-start.20 = (bf16[72,384]{1,0:T(8,128)(2,1)S(1)}, bf16[72,384]{1,0:T(8,128)(2,1)S(1)}, u32[]{:S(2)}, u32[]{:S(2)}) collective-permute-start(bf16[72,384]{1,0:T(8,128)(2,1)S(1)} %get-tuple-element.90), channel_id=1, source_target_pairs={{0,24},{4,28},{1,25},{5,29},{2,26},{6,30},{3,27},{7,31},{8,16},{12... | collective-permute-start | bytes 165896 | tf_op jit(solution)/shard_map/ppermute | solution.py:34
  86.6 9.4 %collective-permute-start.11 = (bf16[80,768]{1,0:T(8,128)(2,1)S(1)}, bf16[80,768]{1,0:T(8,128)(2,1)S(1)}, u32[]{:S(2)}, u32[]{:S(2)}) collective-permute-start(bf16[80,768]{1,0:T(8,128)(2,1)S(1)} %get-tuple-element.79), channel_id=1, source_target_pairs={{0,1},{4,5},{1,0},{5,4},{2,3},{6,7},{3,2},{7,6},{8,9},{12,13},{9,8... | collective-permute-start | bytes 368648 | tf_op jit(solution)/shard_map/ppermute | solution.py:34
  90.4 11.6 %collective-permute-start.12 = (bf16[80,768]{1,0:T(8,128)(2,1)S(1)}, bf16[80,768]{1,0:T(8,128)(2,1)S(1)}, u32[]{:S(2)}, u32[]{:S(2)}) collective-permute-start(bf16[80,768]{1,0:T(8,128)(2,1)S(1)} %get-tuple-element.80), channel_id=1, source_target_pairs={{0,2},{4,6},{1,3},{5,7},{2,0},{6,4},{3,1},{7,5},{8,10},{12,14},{9,... | collective-permute-start | bytes 368648 | tf_op jit(solution)/shard_map/ppermute | solution.py:34
  94.3 7.7 %collective-permute-start.13 = (bf16[80,768]{1,0:T(8,128)(2,1)S(1)}, bf16[80,768]{1,0:T(8,128)(2,1)S(1)}, u32[]{:S(2)}, u32[]{:S(2)}) collective-permute-start(bf16[80,768]{1,0:T(8,128)(2,1)S(1)} %get-tuple-element.81), channel_id=1, source_target_pairs={{0,3},{4,7},{1,2},{5,6},{2,1},{6,5},{3,0},{7,4},{8,11},{12,15},{9,... | collective-permute-start | bytes 368648 | tf_op jit(solution)/shard_map/ppermute | solution.py:34
  102.0 1.2 %collective-permute-start.14 = (f32[384]{0:T(512)S(1)}, f32[384]{0:T(512)S(1)}, u32[]{:S(2)}, u32[]{:S(2)}) collective-permute-start(f32[384]{0:T(512)S(1)} %fusion.4), channel_id=1, source_target_pairs={{0,4},{4,0},{1,5},{5,1},{2,6},{6,2},{3,7},{7,3},{8,12},{12,8},{9,1... | collective-permute-start | bytes 4616 | tf_op jit(solution)/shard_map/ppermute | solution.py:34
  102.2 1.8 %collective-permute-start.21 = (f32[36,1152]{1,0:T(8,128)S(1)}, f32[36,1152]{1,0:T(8,128)S(1)}, u32[]{:S(2)}, u32[]{:S(2)}) collective-permute-start(f32[36,1152]{1,0:T(8,128)S(1)} %broadcast_select_fusion.6), channel_id=1, source_target_pairs={{0,4},{4,0},{1,5},{5,1},{2,6},{6,2},{3,7},{7,3},{8,12},{12,8},{9,1... | collective-permute-start | bytes 497672 | tf_op jit(solution)/shard_map/ppermute | solution.py:34
  (18 other events, 46.0 us)

commit v3 on v2

--- a/solution.py
+++ b/solution.py
@@ -39,9 +39,6 @@
     def along_row(self, value, t):
         return self.send(value, lambda r, c, core: (r, c ^ t, core))
 
-    def along_role(self, value, t):
-        return self.send(value, lambda r, c, core: (r ^ t, c, 1) if core else (r, c ^ t, 0))
-
     def sibling(self, value):
         return self.send(value, lambda r, c, core: (r, c, 1 - core))
 
@@ -53,13 +50,29 @@
     return values[0]
 
 
+def this_core():
+    return lax.rem(lax.axis_index("dp"), 2)
+
+
 def load_projections(image_proj, text_proj, projs, sems):
-    core = lax.rem(lax.axis_index("dp"), 2)
+    core = this_core()
     own = pltpu.make_async_copy(image_proj, projs.at[core], sems.at[0])
     other = pltpu.make_async_copy(text_proj, projs.at[1 - core], sems.at[1])
     own.start()
     other.start()
-    return own, other
+    return [own, other]
+
+
+def load_chunk(shards, feats, sems):
+    core = this_core()
+    rows = shards[0].shape[0]
+    copies = []
+    for i, shard in enumerate(shards):
+        place = pl.ds((core if i < 2 else 1 - core) * rows, rows)
+        side = core if i % 2 == 0 else 1 - core
+        copies.append(pltpu.make_async_copy(shard, feats.at[side, place], sems.at[i]))
+        copies[-1].start()
+    return copies
 
 
 def project(rows, projection):
@@ -68,38 +81,50 @@
     return raw * inverse, inverse
 
 
-def project_kernel(image_proj, text_proj, own, other, own_unit, own_inverse, other_half, projs, sems):
-    for copy in load_projections(image_proj, text_proj, projs, sems):
+def project_kernel(image_proj, text_proj, *refs):
+    shards, (own_chunk, own_unit, own_inverse, other_half, feats, projs, sems) = refs[:4], refs[4:]
+    copies = load_chunk(shards, feats, sems.at[pl.ds(2, 4)])
+    copies += load_projections(image_proj, text_proj, projs, sems.at[pl.ds(0, 2)])
+    for copy in copies:
         copy.wait()
-    unit, _ = project(other[...], projs[1])
+    unit, _ = project(feats[1], projs[1])
     other_half[...] = unit.astype(BF16)
-    unit, inverse = project(own[...], projs[0])
+    unit, inverse = project(feats[0], projs[0])
     own_unit[...] = unit
     own_inverse[...] = jnp.broadcast_to(inverse, own_inverse.shape)
-
-
-def project_chunks(image_proj, text_proj, own, other):
-    rows, width = own.shape
+    own_chunk[...] = feats[0]
+
+
+def project_chunk(image_proj, text_proj, shards):
+    rows, width = shards[0].shape
+    rows = 2 * rows
     anywhere = pl.BlockSpec(memory_space=pl.ANY)
     vmem = pl.BlockSpec(memory_space=pltpu.VMEM)
     return pl.pallas_call(
         project_kernel,
         out_shape=[
+            jax.ShapeDtypeStruct((rows, width), BF16),
             jax.ShapeDtypeStruct((rows, width), F32),
             jax.ShapeDtypeStruct((rows, 128), F32),
             jax.ShapeDtypeStruct((rows, width), BF16),
         ],
-        in_specs=[anywhere] * 2 + [vmem] * 2,
-        out_specs=[vmem] * 3,
-        scratch_shapes=[pltpu.VMEM((2, width, width), BF16), pltpu.SemaphoreType.DMA((2,))],
-        compiler_params=pltpu.CompilerParams(vmem_limit_bytes=20 * 1024 * 1024),
+        in_specs=[anywhere] * 6,
+        out_specs=[vmem] * 4,
+        scratch_shapes=[
+            pltpu.VMEM((2, rows, width), BF16),
+            pltpu.VMEM((2, width, width), BF16),
+            pltpu.SemaphoreType.DMA((6,)),
+        ],
+        compiler_params=pltpu.CompilerParams(
+            vmem_limit_bytes=4 * width * width + 24 * rows * width + 4 * 1024 * 1024
+        ),
         cost_estimate=pl.CostEstimate(
             flops=4 * rows * width * width,
-            bytes_accessed=4 * width * width + 10 * rows * width,
+            bytes_accessed=4 * width * width + 12 * rows * width,
             transcendentals=2 * rows,
         ),
         name="project",
-    )(image_proj, text_proj, own, other)
+    )(image_proj, text_proj, *shards)
 
 
 def pair_terms(cosine, scale, bias, masked):
@@ -125,8 +150,8 @@
 
 
 def block_kernel(side, mp_size, first_width, scalars, image_proj, text_proj, *refs):
-    own_chunks, refs = refs[:side], refs[side:]
-    last_other, refs = refs[0], refs[1:]
+    last_shards, refs = refs[:4], refs[4:]
+    own_chunks, refs = refs[: side - 1], refs[side - 1 :]
     own_units, refs = refs[: side - 1], refs[side - 1 :]
     own_inverses, refs = refs[: side - 1], refs[side - 1 :]
     other_halves, refs = refs[: side - 1], refs[side - 1 :]
@@ -141,7 +166,7 @@
     unit_row, unit_column = unit_index // side, lax.rem(unit_index, side)
     scale, bias = scalars[0], scalars[1]
 
-    count = 2
+    count = 6
 
     def start(source, target):
         nonlocal count
@@ -153,21 +178,21 @@
     def places(i):
         return pl.ds(i * chunk_rows, chunk_rows)
 
-    last_copy = start(last_other, last)
-    own_copies = [start(own_chunks[side - 1], feats.at[places(side - 1)])]
-    proj_copies = load_projections(image_proj, text_proj, projs, sems)
+    first_copies = load_chunk(last_shards, last, sems.at[pl.ds(2, 4)])
+    first_copies += load_projections(image_proj, text_proj, projs, sems.at[pl.ds(0, 2)])
     other_copies = [start(other_halves[i], other_half.at[places(i)]) for i in range(side - 1)]
     unit_copies = [start(own_units[i], units.at[places(i)]) for i in range(side - 1)]
     unit_copies += [start(own_inverses[i], inverses.at[places(i)]) for i in range(side - 1)]
     feat_copies = [start(own_chunks[i], feats.at[places(i)]) for i in range(side - 1)]
 
-    for copy in [last_copy, *own_copies, *proj_copies]:
+    for copy in first_copies:
         copy.wait()
-    unit, _ = project(last[...], projs[1])
+    unit, _ = project(last[1], projs[1])
     other_half[rest:, :] = unit.astype(BF16)
-    unit, inverse = project(feats[rest:, :], projs[0])
+    unit, inverse = project(last[0], projs[0])
     units[rest:, :] = unit
     inverses[rest:, :] = jnp.broadcast_to(inverse, (chunk_rows, 128))
+    feats[rest:, :] = last[0]
     for copy in other_copies + unit_copies:
         copy.wait()
 
@@ -214,7 +239,6 @@
         firsts[t][:chunk, :] = grad[pl.ds(first, chunk), :first_width].astype(firsts[t].dtype)
         if t:
             firsts[t][chunk:, :] = stat_rows(sums, first_width).astype(BF16)
-
     out_rows = chunk // (2 * side)
     for column in range(side):
         for i in range(side):
@@ -248,18 +272,18 @@
     return parts
 
 
-def block_grads(
-    layout, first_width, scalars, image_proj, text_proj, own_chunks, last_other, projected
-):
+def block_grads(layout, first_width, scalars, image_proj, text_proj, last_shards, projected):
     side = layout.side
-    chunk_rows, width = own_chunks[0].shape
+    chunk_rows, width = projected[0][0].shape
     rows = side * chunk_rows
     chunk = width // side
     anywhere = pl.BlockSpec(memory_space=pl.ANY)
     vmem = pl.BlockSpec(memory_space=pltpu.VMEM)
     late_width = width - first_width
-    operands = [image_proj, text_proj, *own_chunks, last_other]
+    operands = [image_proj, text_proj, *last_shards]
     operands += [x for column in zip(*projected) for x in column]
+    needed = 4 * width * width + 12 * rows * width + 4 * chunk_rows * width
+    needed += 4 * width * (width + late_width) + 24 * chunk_rows * rows + 14 * 1024 * 1024
     return pl.pallas_call(
         functools.partial(block_kernel, side, layout.mp, first_width),
         out_shape=[jax.ShapeDtypeStruct((chunk, first_width), F32)]
@@ -271,7 +295,7 @@
         out_specs=[vmem] * (2 * side + 1),
         scratch_shapes=[
             pltpu.VMEM((2, width, width), BF16),
-            pltpu.VMEM((chunk_rows, width), BF16),
+            pltpu.VMEM((2, chunk_rows, width), BF16),
             pltpu.VMEM((rows, width), BF16),
             pltpu.VMEM((rows, width), F32),
             pltpu.VMEM((rows, 128), F32),
@@ -281,10 +305,10 @@
             pltpu.VMEM((chunk, late_width), F32),
             pltpu.SemaphoreType.DMA((len(operands),)),
         ],
-        compiler_params=pltpu.CompilerParams(vmem_limit_bytes=56 * 1024 * 1024),
+        compiler_params=pltpu.CompilerParams(vmem_limit_bytes=min(needed, 60 * 1024 * 1024)),
         cost_estimate=pl.CostEstimate(
             flops=2 * rows * width * (2 * rows + width) + 4 * chunk_rows * width * width,
-            bytes_accessed=8 * rows * width + 8 * width * width,
+            bytes_accessed=12 * rows * width + 4 * width * width,
             transcendentals=3 * rows * rows,
         ),
         name="block",
@@ -370,41 +394,44 @@
     is_image = lax.axis_index("dp") % 2 == 0
 
     scalars = jnp.concatenate([jnp.exp(log_scale), logit_bias])
-    sibling_image, sibling_text = layout.sibling(image_feats), layout.sibling(text_feats)
-    own_unit = jnp.concatenate(
-        [jnp.where(is_image, image_feats, sibling_text), jnp.where(is_image, sibling_image, text_feats)]
+
+    images, texts, swapped, projected = {0: image_feats}, {0: text_feats}, {}, {}
+
+    def swap(t):
+        swapped[t] = layout.sibling(images[t]), layout.sibling(texts[t])
+
+    def project_next(t):
+        projected[t] = project_chunk(image_proj, text_proj, [images[t], texts[t], *swapped[t]])
+
+    last = side - 1
+    bit = side // 2
+    while bit > 1:
+        for t in list(images):
+            images[t ^ bit] = layout.along_row(images[t], bit)
+            texts[t ^ bit] = layout.along_column(texts[t], bit)
+        bit //= 2
+    sources = [t for t in images if t]
+    images[1] = layout.along_row(image_feats, 1)
+    texts[1] = layout.along_column(text_feats, 1)
+    for t in sources:
+        images[t ^ 1] = layout.along_row(images[t], 1)
+        texts[t ^ 1] = layout.along_column(texts[t], 1)
+    images[0], texts[0], texts[1] = lax.optimization_barrier((image_feats, text_feats, texts[1]))
+    for t in range(last):
+        swap(t)
+        project_next(t)
+    images[last], texts[last], projected = lax.optimization_barrier(
+        (images[last], texts[last], projected)
     )
-    other_unit = jnp.concatenate(
-        [jnp.where(is_image, text_feats, sibling_image), jnp.where(is_image, sibling_text, image_feats)]
-    )
-    own_chunks, other_chunks = {0: own_unit}, {0: other_unit}
-    bit = side // 2
-    projected = {}
-    while bit:
-        sources = list(own_chunks)
-        if bit == 1:
-            own_chunks[1] = layout.along_role(own_unit, 1)
-            projected[0] = project_chunks(image_proj, text_proj, own_unit, other_unit)
-            own_chunks, projected = lax.optimization_barrier((own_chunks, projected))
-        for t in sources:
-            if t ^ bit not in own_chunks:
-                own_chunks[t ^ bit] = layout.along_role(own_chunks[t], bit)
-        bit //= 2
-    last = side - 1
-    for t in range(1, last):
-        other_chunks[t] = layout.sibling(own_chunks[t])
-        projected[t] = project_chunks(image_proj, text_proj, own_chunks[t], other_chunks[t])
-    own_chunks[last], projected = lax.optimization_barrier((own_chunks[last], projected))
-    other_chunks[last] = layout.sibling(own_chunks[last])
-    first_width = width - width // 3
+    swap(last)
+    first_width = width - 256
     results = block_grads(
         layout,
         first_width,
         scalars,
         image_proj,
         text_proj,
-        [own_chunks[t] for t in range(side)],
-        other_chunks[last],
+        [images[last], texts[last], *swapped[last]],
         [projected[t] for t in range(last)],
     )
     firsts, lates, stats = list(results[:side]), list(results[side : 2 * side]), results[-1]
@@ -412,9 +439,10 @@
     firsts[1:] = [layout.along_column(firsts[t], t) for t in range(1, side)]
     lates[1:] = [layout.along_row(lates[t], t) for t in range(1, side)]
     *firsts, stats = first_pieces(layout, firsts[0], stats, firsts[1:])
+
+    firsts[1:] = [layout.along_row(firsts[t], t) for t in range(1, side)]
+    lates, firsts[1] = lax.optimization_barrier((lates, firsts[1]))
     lates = list(late_pieces(layout, lates[0], lates[1:]))
-
-    firsts[1:] = [layout.along_row(firsts[t], t) for t in range(1, side)]
     lates[1:] = [layout.along_column(lates[t], t) for t in range(1, side)]
     last_rows = 2 * out_rows
     first_sum = tree_sum([x[:last_rows].astype(F32) for x in firsts])

time: 105 us -> 109 us (1.038)
  waiting for transfers between devices: 30.1 us -> 37.9 us
  starting transfers between devices: 31.8 us -> 27.9 us
  other arithmetic: 2.81 us -> 1.12 us
  local copies, waits for them, and re-layouts: 8.99 us -> 10.3 us
    ppermute x22 -> x28, waiting for transfers between devices: 30.1 us -> 37.9 us  [send(): return lax.ppermute(value, AXES, pairs)]
    ppermute x22 -> x28, starting transfers between devices: 31.8 us -> 27.9 us  [send(): return lax.ppermute(value, AXES, pairs)]
    unnamed x40 -> x16, local copies, waits for them, and re-layouts: 8.4 us -> 9.7 us
  transfers between devices with their start and end apart: 22 -> 28, of which waited for: 9 -> 11; matrix products, arithmetic and copies ran while one was open for 2% -> 1% of each run, Pallas kernels for 8% -> 8%
where the time goes in v3:
time: 109 us; the launch traced here: 108 us
  waiting for transfers between devices  37.9 us (35%)
  Pallas kernels  28.9 us (27%)
  starting transfers between devices  27.9 us (26%)
  local copies, waits for them, and re-layouts  10.3 us (9%)
  between operations  2.12 us (2%)
  other arithmetic  1.12 us (1%)
    ppermute x28, waiting for transfers between devices, send(): return lax.ppermute(value, AXES, pairs)  37.9 us
    ppermute x28, starting transfers between devices, send(): return lax.ppermute(value, AXES, pairs)  27.9 us
    pallas_call x1, Pallas kernels, block_grads(): pl.pallas_call(functools.partial(block_kernel, side, layout.mp, first_wid...  19.9 us
    unnamed x16, local copies, waits for them, and re-layouts  9.7 us
    pallas_call x3, Pallas kernels, project_chunk(): pl.pallas_call(project_kernel, out_shape=[jax.ShapeDtypeStruct((rows, wid...  8.28 us
  transfers between devices with their start and end apart: 28, of which 11 were waited for; matrix products, arithmetic and copies ran while one was open for 1% of the time, Pallas kernels for 8%

profile of v3, /device:TPU:0, one launch (start us, length us, event | category | flops | bytes accessed | tf_op | source)
XLA Modules:
  0.0 108.3 jit_solution(5131962720040117075)
XLA Ops:
  0.6 3.0 %collective-permute-start.4 = (bf16[128,1152]{1,0:T(8,128)(2,1)}, bf16[128,1152]{1,0:T(8,128)(2,1)S(1)}, u32[]{:S(2)}, u32[]{:S(2)}) collective-permute-start(bf16[128,1152]{1,0:T(8,128)(2,1)} %refs_1_), channel_id=1, source_target_pairs={{0,8},{4,12},{1,9},{5,13},{2,10},{6,14},{3,11},{7,15},{8,0},{12,4}... | collective-permute-start | bytes 884744 | tf_op jit(solution)/shard_map/ppermute | solution.py:34
  3.6 1.6 %collective-permute-start.7 = (bf16[128,1152]{1,0:T(8,128)(2,1)}, bf16[128,1152]{1,0:T(8,128)(2,1)S(1)}, u32[]{:S(2)}, u32[]{:S(2)}) collective-permute-start(bf16[128,1152]{1,0:T(8,128)(2,1)} %refs_0_), channel_id=1, source_target_pairs={{0,1},{4,5},{1,0},{5,4},{2,3},{6,7},{3,2},{7,6},{8,9},{12,13},{9,8... | collective-permute-start | bytes 884744 | tf_op jit(solution)/shard_map/ppermute | solution.py:34
  5.2 2.6 %collective-permute-start = (bf16[128,1152]{1,0:T(8,128)(2,1)}, bf16[128,1152]{1,0:T(8,128)(2,1)S(1)}, u32[]{:S(2)}, u32[]{:S(2)}) collective-permute-start(bf16[128,1152]{1,0:T(8,128)(2,1)} %refs_0_), channel_id=1, source_target_pairs={{0,2},{4,6},{1,3},{5,7},{2,0},{6,4},{3,1},{7,5},{8,10},{12,14},{9,... | collective-permute-start | bytes 884744 | tf_op jit(solution)/shard_map/ppermute | solution.py:34
  7.8 1.5 %collective-permute-start.2 = (bf16[128,1152]{1,0:T(8,128)(2,1)}, bf16[128,1152]{1,0:T(8,128)(2,1)S(1)}, u32[]{:S(2)}, u32[]{:S(2)}) collective-permute-start(bf16[128,1152]{1,0:T(8,128)(2,1)} %refs_1_), channel_id=1, source_target_pairs={{0,16},{4,20},{1,17},{5,21},{2,18},{6,22},{3,19},{7,23},{8,24},{12... | collective-permute-start | bytes 884744 | tf_op jit(solution)/shard_map/ppermute | solution.py:34
  9.3 1.5 %collective-permute-done.4.refs_1_ = bf16[128,1152]{1,0:T(8,128)(2,1)S(1)} collective-permute-done((bf16[128,1152]{1,0:T(8,128)(2,1)}, bf16[128,1152]{1,0:T(8,128)(2,1)S(1)}, u32[]{:S(2)}, u32[]{:S(2)}) %collective-permute-start.4) | collective-permute-done | bytes 294944 | tf_op jit(solution)/shard_map/ppermute | solution.py:34
  11.4 7.1 %collective-permute-done.7.refs_0_ = bf16[128,1152]{1,0:T(8,128)(2,1)S(1)} collective-permute-done((bf16[128,1152]{1,0:T(8,128)(2,1)}, bf16[128,1152]{1,0:T(8,128)(2,1)S(1)}, u32[]{:S(2)}, u32[]{:S(2)}) %collective-permute-start.7) | collective-permute-done | bytes 294944 | tf_op jit(solution)/shard_map/ppermute | solution.py:34
  18.5 2.4 %collective-permute-done.refs_0_ = bf16[128,1152]{1,0:T(8,128)(2,1)S(1)} collective-permute-done((bf16[128,1152]{1,0:T(8,128)(2,1)}, bf16[128,1152]{1,0:T(8,128)(2,1)S(1)}, u32[]{:S(2)}, u32[]{:S(2)}) %collective-permute-start) | collective-permute-done | bytes 294944 | tf_op jit(solution)/shard_map/ppermute | solution.py:34
  22.5 1.7 %copy-done = bf16[1152,1152]{1,0:T(8,128)(2,1)S(1)} copy-done((bf16[1152,1152]{1,0:T(8,128)(2,1)S(1)}, bf16[1152,1152]{1,0:T(8,128)(2,1)}, u32[]{:S(2)}) %copy-start) | copy-done | bytes 2654232
  24.2 1.7 %copy-done.1 = bf16[1152,1152]{1,0:T(8,128)(2,1)S(1)} copy-done((bf16[1152,1152]{1,0:T(8,128)(2,1)S(1)}, bf16[1152,1152]{1,0:T(8,128)(2,1)}, u32[]{:S(2)}) %copy-start.1) | copy-done | bytes 2654232
  27.9 2.8 %project.3 = (bf16[256,1152]{1,0:T(8,128)(2,1)S(1)}, f32[256,1152]{1,0:T(8,128)S(1)}, f32[256,128]{1,0:T(8,128)S(1)}, bf16[256,1152]{1,0:T(8,128)(2,1)S(1)}) custom-call(bf16[1152,1152]{1,0:T(8,128)(2,1)S(1)} %copy-done, bf16[1152,1152]{1,0:T(8,128)(2,1)S(1)} %copy-done.1, bf16[128,1152]{1,0:T(8,128)(2,1)S(1)} %copy-done.3, bf16[128,1152]{1,0:T(8,128)(2,1)S(1)} %copy-done.4, ...), custom_call_target="tpu_custom_call" | custom-call | flops 1358954496 | bytes 8847360 | tf_op jit(solution)/shard_map/project/pallas_call | solution.py:103
  31.7 2.8 %project.4 = (bf16[256,1152]{1,0:T(8,128)(2,1)S(1)}, f32[256,1152]{1,0:T(8,128)S(1)}, f32[256,128]{1,0:T(8,128)S(1)}, bf16[256,1152]{1,0:T(8,128)(2,1)S(1)}) custom-call(bf16[1152,1152]{1,0:T(8,128)(2,1)S(1)} %copy-done, bf16[1152,1152]{1,0:T(8,128)(2,1)S(1)} %copy-done.1, bf16[128,1152]{1,0:T(8,128)(2,1)S(1)} %collective-permute-done.7.refs_0_, ...), custom_call_target="tpu_custom_call" | custom-call | flops 1358954496 | bytes 8847360 | tf_op jit(solution)/shard_map/project/pallas_call | solution.py:103
  35.5 2.8 %project.5 = (bf16[256,1152]{1,0:T(8,128)(2,1)S(1)}, f32[256,1152]{1,0:T(8,128)S(1)}, f32[256,128]{1,0:T(8,128)S(1)}, bf16[256,1152]{1,0:T(8,128)(2,1)S(1)}) custom-call(bf16[1152,1152]{1,0:T(8,128)(2,1)S(1)} %copy-done, bf16[1152,1152]{1,0:T(8,128)(2,1)S(1)} %copy-done.1, bf16[128,1152]{1,0:T(8,128)(2,1)S(1)} %collective-permute-done.refs_0_, ...), custom_call_target="tpu_custom_call" | custom-call | flops 1358954496 | bytes 8847360 | tf_op jit(solution)/shard_map/project/pallas_call | solution.py:103
  41.3 19.9 %block.1 = (f32[288,896]{1,0:T(8,128)}, bf16[296,896]{1,0:T(8,128)(2,1)S(1)}, bf16[296,896]{1,0:T(8,128)(2,1)S(1)}, bf16[296,896]{1,0:T(8,128)(2,1)S(1)}, f32[28...) custom-call(f32[2]{0:T(128)S(1)} %pad_maximum_fusion.1.scalars, ...), custom_call_target="tpu_custom_call" | custom-call | flops 8908701696 | bytes 19464192 | tf_op jit(solution)/shard_map/block/pallas_call | solution.py:287
  61.2 1.6 %collective-permute-start.14 = (bf16[296,896]{1,0:T(8,128)(2,1)S(1)}, bf16[296,896]{1,0:T(8,128)(2,1)S(1)}, u32[]{:S(2)}, u32[]{:S(2)}) collective-permute-start(bf16[296,896]{1,0:T(8,128)(2,1)S(1)} %get-tuple-element.88), channel_id=1, source_target_pairs={{0,8},{4,12},{1,9},{5,13},{2,10},{6,14},{3,11},{7,15},{8,0},{12,4}... | collective-permute-start | bytes 1591304 | tf_op jit(solution)/shard_map/ppermute | solution.py:34
  62.7 1.5 %collective-permute-start.15 = (bf16[296,896]{1,0:T(8,128)(2,1)S(1)}, bf16[296,896]{1,0:T(8,128)(2,1)S(1)}, u32[]{:S(2)}, u32[]{:S(2)}) collective-permute-start(bf16[296,896]{1,0:T(8,128)(2,1)S(1)} %get-tuple-element.89), channel_id=1, source_target_pairs={{0,16},{4,20},{1,17},{5,21},{2,18},{6,22},{3,19},{7,23},{8,24},{12... | collective-permute-start | bytes 1591304 | tf_op jit(solution)/shard_map/ppermute | solution.py:34
  64.7 1.6 %collective-permute-start.17 = (bf16[288,256]{1,0:T(8,128)(2,1)S(1)}, bf16[288,256]{1,0:T(8,128)(2,1)S(1)}, u32[]{:S(2)}, u32[]{:S(2)}) collective-permute-start(bf16[288,256]{1,0:T(8,128)(2,1)S(1)} %get-tuple-element.93), channel_id=1, source_target_pairs={{0,1},{4,5},{1,0},{5,4},{2,3},{6,7},{3,2},{7,6},{8,9},{12,13},{9,8... | collective-permute-start | bytes 442376 | tf_op jit(solution)/shard_map/ppermute | solution.py:34
  67.4 8.7 %collective-permute-done.14.refs_0_ = bf16[296,896]{1,0:T(8,128)(2,1)S(1)} collective-permute-done((bf16[296,896]{1,0:T(8,128)(2,1)S(1)}, bf16[296,896]{1,0:T(8,128)(2,1)S(1)}, u32[]{:S(2)}, u32[]{:S(2)}) %collective-permute-start.14) | collective-permute-done | bytes 530464 | tf_op jit(solution)/shard_map/ppermute | solution.py:34
  76.1 2.1 %collective-permute-start.19 = (bf16[288,256]{1,0:T(8,128)(2,1)S(1)}, bf16[288,256]{1,0:T(8,128)(2,1)S(1)}, u32[]{:S(2)}, u32[]{:S(2)}) collective-permute-start(bf16[288,256]{1,0:T(8,128)(2,1)S(1)} %get-tuple-element.95), channel_id=1, source_target_pairs={{0,3},{4,7},{1,2},{5,6},{2,1},{6,5},{3,0},{7,4},{8,11},{12,15},{9,... | collective-permute-start | bytes 442376 | tf_op jit(solution)/shard_map/ppermute | solution.py:34
  78.2 9.7 %collective-permute-done.15.refs_1_ = bf16[296,896]{1,0:T(8,128)(2,1)S(1)} collective-permute-done((bf16[296,896]{1,0:T(8,128)(2,1)S(1)}, bf16[296,896]{1,0:T(8,128)(2,1)S(1)}, u32[]{:S(2)}, u32[]{:S(2)}) %collective-permute-start.15) | collective-permute-done | bytes 530464 | tf_op jit(solution)/shard_map/ppermute | solution.py:34
  89.8 1.7 %collective-permute-start.20 = (bf16[80,896]{1,0:T(8,128)(2,1)S(1)}, bf16[80,896]{1,0:T(8,128)(2,1)S(1)}, u32[]{:S(2)}, u32[]{:S(2)}) collective-permute-start(bf16[80,896]{1,0:T(8,128)(2,1)S(1)} %get-tuple-element.96), channel_id=1, source_target_pairs={{0,1},{4,5},{1,0},{5,4},{2,3},{6,7},{3,2},{7,6},{8,9},{12,13},{9,8... | collective-permute-start | bytes 430088 | tf_op jit(solution)/shard_map/ppermute | solution.py:34
  92.6 1.7 %collective-permute-start.22 = (bf16[80,896]{1,0:T(8,128)(2,1)S(1)}, bf16[80,896]{1,0:T(8,128)(2,1)S(1)}, u32[]{:S(2)}, u32[]{:S(2)}) collective-permute-start(bf16[80,896]{1,0:T(8,128)(2,1)S(1)} %get-tuple-element.99), channel_id=1, source_target_pairs={{0,3},{4,7},{1,2},{5,6},{2,1},{6,5},{3,0},{7,4},{8,11},{12,15},{9,... | collective-permute-start | bytes 430088 | tf_op jit(solution)/shard_map/ppermute | solution.py:34
  94.2 2.4 %collective-permute-done.20 = bf16[80,896]{1,0:T(8,128)(2,1)S(1)} collective-permute-done((bf16[80,896]{1,0:T(8,128)(2,1)S(1)}, bf16[80,896]{1,0:T(8,128)(2,1)S(1)}, u32[]{:S(2)}, u32[]{:S(2)}) %collective-permute-start.20) | collective-permute-done | bytes 143392 | tf_op jit(solution)/shard_map/ppermute | solution.py:34
  100.3 2.5 %collective-permute-done.22 = bf16[80,896]{1,0:T(8,128)(2,1)S(1)} collective-permute-done((bf16[80,896]{1,0:T(8,128)(2,1)S(1)}, bf16[80,896]{1,0:T(8,128)(2,1)S(1)}, u32[]{:S(2)}, u32[]{:S(2)}) %collective-permute-start.22) | collective-permute-done | bytes 143392 | tf_op jit(solution)/shard_map/ppermute | solution.py:34
  102.8 1.8 %collective-permute-done.21 = bf16[80,896]{1,0:T(8,128)(2,1)S(1)} collective-permute-done((bf16[80,896]{1,0:T(8,128)(2,1)S(1)}, bf16[80,896]{1,0:T(8,128)(2,1)S(1)}, u32[]{:S(2)}, u32[]{:S(2)}) %collective-permute-start.21) | collective-permute-done | bytes 143392 | tf_op jit(solution)/shard_map/ppermute | solution.py:34
  (66 shorter events, 19.6 us)
Async XLA Ops:
  0.6 10.2 %collective-permute-start.4 = (bf16[128,1152]{1,0:T(8,128)(2,1)}, bf16[128,1152]{1,0:T(8,128)(2,1)S(1)}, u32[]{:S(2)}, u32[]{:S(2)}) collective-permute-start(bf16[128,1152]{1,0:T(8,128)(2,1)} %refs_1_), channel_id=1, source_target_pairs={{0,8},{4,12},{1,9},{5,13},{2,10},{6,14},{3,11},{7,15},{8,0},{12,4}... | collective-permute-start | bytes 884744 | tf_op jit(solution)/shard_map/ppermute | solution.py:34
  3.6 14.9 %collective-permute-start.7 = (bf16[128,1152]{1,0:T(8,128)(2,1)}, bf16[128,1152]{1,0:T(8,128)(2,1)S(1)}, u32[]{:S(2)}, u32[]{:S(2)}) collective-permute-start(bf16[128,1152]{1,0:T(8,128)(2,1)} %refs_0_), channel_id=1, source_target_pairs={{0,1},{4,5},{1,0},{5,4},{2,3},{6,7},{3,2},{7,6},{8,9},{12,13},{9,8... | collective-permute-start | bytes 884744 | tf_op jit(solution)/shard_map/ppermute | solution.py:34
  5.2 15.7 %collective-permute-start = (bf16[128,1152]{1,0:T(8,128)(2,1)}, bf16[128,1152]{1,0:T(8,128)(2,1)S(1)}, u32[]{:S(2)}, u32[]{:S(2)}) collective-permute-start(bf16[128,1152]{1,0:T(8,128)(2,1)} %refs_0_), channel_id=1, source_target_pairs={{0,2},{4,6},{1,3},{5,7},{2,0},{6,4},{3,1},{7,5},{8,10},{12,14},{9,... | collective-permute-start | bytes 884744 | tf_op jit(solution)/shard_map/ppermute | solution.py:34
  7.8 13.1 %collective-permute-start.2 = (bf16[128,1152]{1,0:T(8,128)(2,1)}, bf16[128,1152]{1,0:T(8,128)(2,1)S(1)}, u32[]{:S(2)}, u32[]{:S(2)}) collective-permute-start(bf16[128,1152]{1,0:T(8,128)(2,1)} %refs_1_), channel_id=1, source_target_pairs={{0,16},{4,20},{1,17},{5,21},{2,18},{6,22},{3,19},{7,23},{8,24},{12... | collective-permute-start | bytes 884744 | tf_op jit(solution)/shard_map/ppermute | solution.py:34
  10.9 10.6 %collective-permute-start.5 = (bf16[128,1152]{1,0:T(8,128)(2,1)}, bf16[128,1152]{1,0:T(8,128)(2,1)S(1)}, u32[]{:S(2)}, u32[]{:S(2)}) collective-permute-start(bf16[128,1152]{1,0:T(8,128)(2,1)} %refs_0_), channel_id=1, source_target_pairs={{0,4},{4,0},{1,5},{5,1},{2,6},{6,2},{3,7},{7,3},{8,12},{12,8},{9,1... | collective-permute-start | bytes 884744 | tf_op jit(solution)/shard_map/ppermute | solution.py:34
  10.9 10.6 %collective-permute-start.6 = (bf16[128,1152]{1,0:T(8,128)(2,1)}, bf16[128,1152]{1,0:T(8,128)(2,1)S(1)}, u32[]{:S(2)}, u32[]{:S(2)}) collective-permute-start(bf16[128,1152]{1,0:T(8,128)(2,1)} %refs_1_), channel_id=1, source_target_pairs={{0,4},{4,0},{1,5},{5,1},{2,6},{6,2},{3,7},{7,3},{8,12},{12,8},{9,1... | collective-permute-start | bytes 884744 | tf_op jit(solution)/shard_map/ppermute | solution.py:34
  18.5 3.4 %collective-permute-start.9 = (bf16[128,1152]{1,0:T(8,128)(2,1)S(1)}, bf16[128,1152]{1,0:T(8,128)(2,1)S(1)}, u32[]{:S(2)}, u32[]{:S(2)}) collective-permute-start(bf16[128,1152]{1,0:T(8,128)(2,1)S(1)} %collective-permute-done.4.refs_1_), channel_id=1, source_target_pairs={{0,4},{4,0},{1,5},{5,1},{2,6},{6,2},{3,7},{7,3},{8,12},{12,8},{9,1... | collective-permute-start | bytes 884744 | tf_op jit(solution)/shard_map/ppermute | solution.py:34
  20.9 10.8 %collective-permute-start.8 = (bf16[128,1152]{1,0:T(8,128)(2,1)S(1)}, bf16[128,1152]{1,0:T(8,128)(2,1)S(1)}, u32[]{:S(2)}, u32[]{:S(2)}) collective-permute-start(bf16[128,1152]{1,0:T(8,128)(2,1)S(1)} %collective-permute-done.7.refs_0_), channel_id=1, source_target_pairs={{0,4},{4,0},{1,5},{5,1},{2,6},{6,2},{3,7},{7,3},{8,12},{12,8},{9,1... | collective-permute-start | bytes 884744 | tf_op jit(solution)/shard_map/ppermute | solution.py:34
  20.9 14.6 %collective-permute-start.10 = (bf16[128,1152]{1,0:T(8,128)(2,1)S(1)}, bf16[128,1152]{1,0:T(8,128)(2,1)S(1)}, u32[]{:S(2)}, u32[]{:S(2)}) collective-permute-start(bf16[128,1152]{1,0:T(8,128)(2,1)S(1)} %collective-permute-done.refs_0_), channel_id=1, source_target_pairs={{0,4},{4,0},{1,5},{5,1},{2,6},{6,2},{3,7},{7,3},{8,12},{12,8},{9,1... | collective-permute-start | bytes 884744 | tf_op jit(solution)/shard_map/ppermute | solution.py:34
  21.4 14.1 %collective-permute-start.11 = (bf16[128,1152]{1,0:T(8,128)(2,1)S(1)}, bf16[128,1152]{1,0:T(8,128)(2,1)S(1)}, u32[]{:S(2)}, u32[]{:S(2)}) collective-permute-start(bf16[128,1152]{1,0:T(8,128)(2,1)S(1)} %collective-permute-done.2.refs_1_), channel_id=1, source_target_pairs={{0,4},{4,0},{1,5},{5,1},{2,6},{6,2},{3,7},{7,3},{8,12},{12,8},{9,1... | collective-permute-start | bytes 884744 | tf_op jit(solution)/shard_map/ppermute | solution.py:34
  21.5 17.8 %collective-permute-start.1 = (bf16[128,1152]{1,0:T(8,128)(2,1)S(1)}, bf16[128,1152]{1,0:T(8,128)(2,1)S(1)}, u32[]{:S(2)}, u32[]{:S(2)}) collective-permute-start(bf16[128,1152]{1,0:T(8,128)(2,1)S(1)} %collective-permute-done.refs_0_), channel_id=1, source_target_pairs={{0,1},{4,5},{1,0},{5,4},{2,3},{6,7},{3,2},{7,6},{8,9},{12,13},{9,8... | collective-permute-start | bytes 884744 | tf_op jit(solution)/shard_map/ppermute | solution.py:34
  21.9 17.4 %collective-permute-start.3 = (bf16[128,1152]{1,0:T(8,128)(2,1)S(1)}, bf16[128,1152]{1,0:T(8,128)(2,1)S(1)}, u32[]{:S(2)}, u32[]{:S(2)}) collective-permute-start(bf16[128,1152]{1,0:T(8,128)(2,1)S(1)} %collective-permute-done.2.refs_1_), channel_id=1, source_target_pairs={{0,8},{4,12},{1,9},{5,13},{2,10},{6,14},{3,11},{7,15},{8,0},{12,4}... | collective-permute-start | bytes 884744 | tf_op jit(solution)/shard_map/ppermute | solution.py:34
  61.2 15.0 %collective-permute-start.14 = (bf16[296,896]{1,0:T(8,128)(2,1)S(1)}, bf16[296,896]{1,0:T(8,128)(2,1)S(1)}, u32[]{:S(2)}, u32[]{:S(2)}) collective-permute-start(bf16[296,896]{1,0:T(8,128)(2,1)S(1)} %get-tuple-element.88), channel_id=1, source_target_pairs={{0,8},{4,12},{1,9},{5,13},{2,10},{6,14},{3,11},{7,15},{8,0},{12,4}... | collective-permute-start | bytes 1591304 | tf_op jit(solution)/shard_map/ppermute | solution.py:34
  62.7 25.2 %collective-permute-start.15 = (bf16[296,896]{1,0:T(8,128)(2,1)S(1)}, bf16[296,896]{1,0:T(8,128)(2,1)S(1)}, u32[]{:S(2)}, u32[]{:S(2)}) collective-permute-start(bf16[296,896]{1,0:T(8,128)(2,1)S(1)} %get-tuple-element.89), channel_id=1, source_target_pairs={{0,16},{4,20},{1,17},{5,21},{2,18},{6,22},{3,19},{7,23},{8,24},{12... | collective-permute-start | bytes 1591304 | tf_op jit(solution)/shard_map/ppermute | solution.py:34
  64.2 23.7 %collective-permute-start.16 = (bf16[296,896]{1,0:T(8,128)(2,1)S(1)}, bf16[296,896]{1,0:T(8,128)(2,1)S(1)}, u32[]{:S(2)}, u32[]{:S(2)}) collective-permute-start(bf16[296,896]{1,0:T(8,128)(2,1)S(1)} %get-tuple-element.90), channel_id=1, source_target_pairs={{0,24},{4,28},{1,25},{5,29},{2,26},{6,30},{3,27},{7,31},{8,16},{12... | collective-permute-start | bytes 1591304 | tf_op jit(solution)/shard_map/ppermute | solution.py:34
  64.7 27.8 %collective-permute-start.17 = (bf16[288,256]{1,0:T(8,128)(2,1)S(1)}, bf16[288,256]{1,0:T(8,128)(2,1)S(1)}, u32[]{:S(2)}, u32[]{:S(2)}) collective-permute-start(bf16[288,256]{1,0:T(8,128)(2,1)S(1)} %get-tuple-element.93), channel_id=1, source_target_pairs={{0,1},{4,5},{1,0},{5,4},{2,3},{6,7},{3,2},{7,6},{8,9},{12,13},{9,8... | collective-permute-start | bytes 442376 | tf_op jit(solution)/shard_map/ppermute | solution.py:34
  66.3 27.9 %collective-permute-start.18 = (bf16[288,256]{1,0:T(8,128)(2,1)S(1)}, bf16[288,256]{1,0:T(8,128)(2,1)S(1)}, u32[]{:S(2)}, u32[]{:S(2)}) collective-permute-start(bf16[288,256]{1,0:T(8,128)(2,1)S(1)} %get-tuple-element.94), channel_id=1, source_target_pairs={{0,2},{4,6},{1,3},{5,7},{2,0},{6,4},{3,1},{7,5},{8,10},{12,14},{9,... | collective-permute-start | bytes 442376 | tf_op jit(solution)/shard_map/ppermute | solution.py:34
  76.1 18.1 %collective-permute-start.19 = (bf16[288,256]{1,0:T(8,128)(2,1)S(1)}, bf16[288,256]{1,0:T(8,128)(2,1)S(1)}, u32[]{:S(2)}, u32[]{:S(2)}) collective-permute-start(bf16[288,256]{1,0:T(8,128)(2,1)S(1)} %get-tuple-element.95), channel_id=1, source_target_pairs={{0,3},{4,7},{1,2},{5,6},{2,1},{6,5},{3,0},{7,4},{8,11},{12,15},{9,... | collective-permute-start | bytes 442376 | tf_op jit(solution)/shard_map/ppermute | solution.py:34
  89.8 6.8 %collective-permute-start.20 = (bf16[80,896]{1,0:T(8,128)(2,1)S(1)}, bf16[80,896]{1,0:T(8,128)(2,1)S(1)}, u32[]{:S(2)}, u32[]{:S(2)}) collective-permute-start(bf16[80,896]{1,0:T(8,128)(2,1)S(1)} %get-tuple-element.96), channel_id=1, source_target_pairs={{0,1},{4,5},{1,0},{5,4},{2,3},{6,7},{3,2},{7,6},{8,9},{12,13},{9,8... | collective-permute-start | bytes 430088 | tf_op jit(solution)/shard_map/ppermute | solution.py:34
  91.4 13.1 %collective-permute-start.21 = (bf16[80,896]{1,0:T(8,128)(2,1)S(1)}, bf16[80,896]{1,0:T(8,128)(2,1)S(1)}, u32[]{:S(2)}, u32[]{:S(2)}) collective-permute-start(bf16[80,896]{1,0:T(8,128)(2,1)S(1)} %get-tuple-element.98), channel_id=1, source_target_pairs={{0,2},{4,6},{1,3},{5,7},{2,0},{6,4},{3,1},{7,5},{8,10},{12,14},{9,... | collective-permute-start | bytes 430088 | tf_op jit(solution)/shard_map/ppermute | solution.py:34
  92.6 10.2 %collective-permute-start.22 = (bf16[80,896]{1,0:T(8,128)(2,1)S(1)}, bf16[80,896]{1,0:T(8,128)(2,1)S(1)}, u32[]{:S(2)}, u32[]{:S(2)}) collective-permute-start(bf16[80,896]{1,0:T(8,128)(2,1)S(1)} %get-tuple-element.99), channel_id=1, source_target_pairs={{0,3},{4,7},{1,2},{5,6},{2,1},{6,5},{3,0},{7,4},{8,11},{12,15},{9,... | collective-permute-start | bytes 430088 | tf_op jit(solution)/shard_map/ppermute | solution.py:34
  96.8 9.2 %collective-permute-start.24 = (bf16[72,256]{1,0:T(8,128)(2,1)S(1)}, bf16[72,256]{1,0:T(8,128)(2,1)S(1)}, u32[]{:S(2)}, u32[]{:S(2)}) collective-permute-start(bf16[72,256]{1,0:T(8,128)(2,1)S(1)} %get-tuple-element.106), channel_id=1, source_target_pairs={{0,8},{4,12},{1,9},{5,13},{2,10},{6,14},{3,11},{7,15},{8,0},{12,4}... | collective-permute-start | bytes 110600 | tf_op jit(solution)/shard_map/ppermute | solution.py:34
  98.1 7.9 %collective-permute-start.25 = (bf16[72,256]{1,0:T(8,128)(2,1)S(1)}, bf16[72,256]{1,0:T(8,128)(2,1)S(1)}, u32[]{:S(2)}, u32[]{:S(2)}) collective-permute-start(bf16[72,256]{1,0:T(8,128)(2,1)S(1)} %get-tuple-element.107), channel_id=1, source_target_pairs={{0,16},{4,20},{1,17},{5,21},{2,18},{6,22},{3,19},{7,23},{8,24},{12... | collective-permute-start | bytes 110600 | tf_op jit(solution)/shard_map/ppermute | solution.py:34
  98.9 7.1 %collective-permute-start.26 = (bf16[72,256]{1,0:T(8,128)(2,1)S(1)}, bf16[72,256]{1,0:T(8,128)(2,1)S(1)}, u32[]{:S(2)}, u32[]{:S(2)}) collective-permute-start(bf16[72,256]{1,0:T(8,128)(2,1)S(1)} %get-tuple-element.108), channel_id=1, source_target_pairs={{0,24},{4,28},{1,25},{5,29},{2,26},{6,30},{3,27},{7,31},{8,16},{12... | collective-permute-start | bytes 110600 | tf_op jit(solution)/shard_map/ppermute | solution.py:34
  (12 other events, 16.4 us)

commit v4 on v3

--- a/solution.py
+++ b/solution.py
@@ -95,10 +95,11 @@
     own_chunk[...] = feats[0]
 
 
-def project_chunk(image_proj, text_proj, shards):
+def project_chunk(image_proj, text_proj, shards, from_arguments):
     rows, width = shards[0].shape
     rows = 2 * rows
     anywhere = pl.BlockSpec(memory_space=pl.ANY)
+    hbm = pl.BlockSpec(memory_space=pltpu.HBM)
     vmem = pl.BlockSpec(memory_space=pltpu.VMEM)
     return pl.pallas_call(
         project_kernel,
@@ -108,7 +109,7 @@
             jax.ShapeDtypeStruct((rows, 128), F32),
             jax.ShapeDtypeStruct((rows, width), BF16),
         ],
-        in_specs=[anywhere] * 6,
+        in_specs=[hbm] * 2 + [hbm if from_arguments else anywhere] * 2 + [anywhere] * 2,
         out_specs=[vmem] * 4,
         scratch_shapes=[
             pltpu.VMEM((2, rows, width), BF16),
@@ -156,7 +157,7 @@
     own_inverses, refs = refs[: side - 1], refs[side - 1 :]
     other_halves, refs = refs[: side - 1], refs[side - 1 :]
     firsts, refs = refs[:side], refs[side:]
-    lates, refs = refs[:side], refs[side:]
+    own_late, late_message, refs = refs[0], refs[1], refs[2:]
     stats, projs, last, feats, units, inverses, other_half, dy, grad, piece, sems = refs
     rows, width = dy.shape
     chunk_rows = rows // side
@@ -246,7 +247,11 @@
                 source = i * chunk + shard_of(column, core, mp_size) * out_rows
                 target = (2 * i + core) * out_rows
                 piece[target : target + out_rows, :] = grad[source : source + out_rows, first_width:]
-        store_for(column, unit_column, piece, lates)
+        half = side // 2 * chunk
+        for t in range(side):
+            target = own_late if t < side // 2 else late_message
+            place = pl.ds(t * chunk % half, chunk)
+            store_for(column, unit_column, piece, {t: target.at[place, :]})
 
 
 def shard_of(column, core, mp_size):
@@ -254,7 +259,7 @@
 
 
 def store_for(index, own_index, piece, outs):
-    for t, out in enumerate(outs):
+    for t, out in outs.items():
 
         @pl.when(jnp.bitwise_xor(own_index, t) == index)
         def _():
@@ -283,16 +288,18 @@
     operands = [image_proj, text_proj, *last_shards]
     operands += [x for column in zip(*projected) for x in column]
     needed = 4 * width * width + 12 * rows * width + 4 * chunk_rows * width
-    needed += 4 * width * (width + late_width) + 24 * chunk_rows * rows + 14 * 1024 * 1024
+    needed += 4 * width * (width + late_width) + 24 * chunk_rows * rows + 7 * 1024 * 1024
     return pl.pallas_call(
         functools.partial(block_kernel, side, layout.mp, first_width),
         out_shape=[jax.ShapeDtypeStruct((chunk, first_width), F32)]
         + [jax.ShapeDtypeStruct((chunk + 8, first_width), BF16)] * (side - 1)
-        + [jax.ShapeDtypeStruct((chunk, late_width), F32)]
-        + [jax.ShapeDtypeStruct((chunk, late_width), BF16)] * (side - 1)
+        + [jax.ShapeDtypeStruct((width // 2, late_width), F32)]
+        + [jax.ShapeDtypeStruct((width // 2, late_width), BF16)]
         + [jax.ShapeDtypeStruct((8, 384), F32)],
-        in_specs=[pl.BlockSpec(memory_space=pltpu.SMEM)] + [anywhere] * len(operands),
-        out_specs=[vmem] * (2 * side + 1),
+        in_specs=[pl.BlockSpec(memory_space=pltpu.SMEM)]
+        + [pl.BlockSpec(memory_space=pltpu.HBM)] * 2
+        + [anywhere] * (len(operands) - 2),
+        out_specs=[vmem] * (side + 3),
         scratch_shapes=[
             pltpu.VMEM((2, width, width), BF16),
             pltpu.VMEM((2, chunk_rows, width), BF16),
@@ -336,7 +343,7 @@
         for core in range(2):
             source = shard_of(column, core, mp_size) * out_rows
             piece[core * out_rows : (core + 1) * out_rows, :] = total[source : source + out_rows, :]
-        store_for(column, unit_column, piece, outs)
+        store_for(column, unit_column, piece, dict(enumerate(outs)))
 
 
 def first_pieces(layout, own, own_stats, arrived):
@@ -357,15 +364,38 @@
     )(own, own_stats, *arrived)
 
 
+def halve_kernel(own, arrived, keep, message):
+    half = keep.shape[0]
+    keep[...] = own[:half, :] + arrived[:half, :].astype(F32)
+    message[...] = (own[half:, :] + arrived[half:, :].astype(F32)).astype(BF16)
+
+
+def halve(own, arrived):
+    rows, width = own.shape
+    vmem = pl.BlockSpec(memory_space=pltpu.VMEM)
+    return pl.pallas_call(
+        halve_kernel,
+        out_shape=[
+            jax.ShapeDtypeStruct((rows // 2, width), F32),
+            jax.ShapeDtypeStruct((rows // 2, width), BF16),
+        ],
+        in_specs=[vmem] * 2,
+        out_specs=[vmem] * 2,
+        compiler_params=pltpu.CompilerParams(vmem_limit_bytes=12 * 1024 * 1024),
+        name="halve",
+    )(own, arrived)
+
+
 def late_kernel(side, mp_size, own, *refs):
-    arrived, outs, total = refs[: side - 1], refs[side - 1 : 2 * side - 1], refs[-1]
+    arrived, outs, total = refs[:1], refs[1:-1], refs[-1]
     chunk = own.shape[0]
     total[...] = arrived_sum(own, arrived, chunk)
     dp_index, mp_index = lax.axis_index("dp"), lax.axis_index("mp")
     unit_row = (dp_index // 2 * mp_size + mp_index) // side
     rows = chunk // side
     for row in range(side):
-        store_for(row, unit_row, total.at[row * rows : (row + 1) * rows, :], outs)
+        piece = total.at[row * rows : (row + 1) * rows, :]
+        store_for(row, unit_row, piece, dict(enumerate(outs)))
 
 
 def late_pieces(layout, own, arrived):
@@ -377,12 +407,12 @@
         functools.partial(late_kernel, side, layout.mp),
         out_shape=[jax.ShapeDtypeStruct((rows, width), F32)]
         + [jax.ShapeDtypeStruct((rows, width), BF16)] * (side - 1),
-        in_specs=[vmem] * side,
+        in_specs=[vmem] * 2,
         out_specs=[vmem] * side,
         scratch_shapes=[pltpu.VMEM((chunk, width), F32)],
         compiler_params=pltpu.CompilerParams(vmem_limit_bytes=12 * 1024 * 1024),
         name="late",
-    )(own, *arrived)
+    )(own, arrived)
 
 
 def per_device(layout, image_feats, text_feats, image_proj, text_proj, log_scale, logit_bias):
@@ -401,7 +431,8 @@
         swapped[t] = layout.sibling(images[t]), layout.sibling(texts[t])
 
     def project_next(t):
-        projected[t] = project_chunk(image_proj, text_proj, [images[t], texts[t], *swapped[t]])
+        shards = [images[t], texts[t], *swapped[t]]
+        projected[t] = project_chunk(image_proj, text_proj, shards, t == 0)
 
     last = side - 1
     bit = side // 2
@@ -413,18 +444,20 @@
     sources = [t for t in images if t]
     images[1] = layout.along_row(image_feats, 1)
     texts[1] = layout.along_column(text_feats, 1)
+    swap(0)
+    project_next(0)
+    images, texts, projected = lax.optimization_barrier((images, texts, projected))
     for t in sources:
         images[t ^ 1] = layout.along_row(images[t], 1)
         texts[t ^ 1] = layout.along_column(texts[t], 1)
-    images[0], texts[0], texts[1] = lax.optimization_barrier((image_feats, text_feats, texts[1]))
-    for t in range(last):
+    for t in range(1, last):
         swap(t)
         project_next(t)
     images[last], texts[last], projected = lax.optimization_barrier(
         (images[last], texts[last], projected)
     )
     swap(last)
-    first_width = width - 256
+    first_width = width - width // 3
     results = block_grads(
         layout,
         first_width,
@@ -434,16 +467,21 @@
         [images[last], texts[last], *swapped[last]],
         [projected[t] for t in range(last)],
     )
-    firsts, lates, stats = list(results[:side]), list(results[side : 2 * side]), results[-1]
+    firsts, (late, message, stats) = list(results[:side]), results[side:]
 
     firsts[1:] = [layout.along_column(firsts[t], t) for t in range(1, side)]
-    lates[1:] = [layout.along_row(lates[t], t) for t in range(1, side)]
+    bit = side // 2
+    arrived = layout.along_row(message, bit)
+    while bit > 1:
+        late, message = halve(late, arrived)
+        bit //= 2
+        arrived = layout.along_row(message, bit)
     *firsts, stats = first_pieces(layout, firsts[0], stats, firsts[1:])
 
     firsts[1:] = [layout.along_row(firsts[t], t) for t in range(1, side)]
-    lates, firsts[1] = lax.optimization_barrier((lates, firsts[1]))
-    lates = list(late_pieces(layout, lates[0], lates[1:]))
+    lates = list(late_pieces(layout, late, arrived))
     lates[1:] = [layout.along_column(lates[t], t) for t in range(1, side)]
+    firsts, lates = lax.optimization_barrier((firsts, lates))
     last_rows = 2 * out_rows
     first_sum = tree_sum([x[:last_rows].astype(F32) for x in firsts])
     late_sum = tree_sum([x.astype(F32) for x in lates])

time: 109 us -> 96.6 us (0.89)
  waiting for transfers between devices: 37.9 us -> 31.6 us
  local copies, waits for them, and re-layouts: 10.3 us -> 6.02 us
  Pallas kernels: 28.9 us -> 27.7 us
    ppermute x28 -> x27, waiting for transfers between devices: 37.9 us -> 31.6 us  [send(): return lax.ppermute(value, AXES, pairs)]
    unnamed x16 -> x10, local copies, waits for them, and re-layouts: 9.7 us -> 5.43 us
    pallas_call x1, Pallas kernels: 19.9 us -> 18.6 us  [block_grads(): pl.pallas_call(functools.partial(block_kernel, side, layout.mp, first_wid...]
    ppermute x28 -> x27, starting transfers between devices: 27.9 us -> 27.8 us  [send(): return lax.ppermute(value, AXES, pairs)]
  transfers between devices with their start and end apart: 28 -> 27, of which waited for: 11 -> 12; matrix products, arithmetic and copies ran while one was open for 1% -> 1% of each run, Pallas kernels for 8% -> 9%
where the time goes in v4:
time: 96.6 us; the launch traced here: 96.4 us
  waiting for transfers between devices  31.6 us (33%)
  starting transfers between devices  27.8 us (29%)
  Pallas kernels  27.7 us (29%)
  local copies, waits for them, and re-layouts  6.02 us (6%)
  between operations  2.13 us (2%)
  other arithmetic  1.12 us (1%)
    ppermute x27, waiting for transfers between devices, send(): return lax.ppermute(value, AXES, pairs)  31.6 us
    ppermute x27, starting transfers between devices, send(): return lax.ppermute(value, AXES, pairs)  27.8 us
    pallas_call x1, Pallas kernels, block_grads(): pl.pallas_call(functools.partial(block_kernel, side, layout.mp, first_wid...  18.6 us
    pallas_call x3, Pallas kernels, project_chunk(): pl.pallas_call(project_kernel, out_shape=[jax.ShapeDtypeStruct((rows, wid...  8.31 us
    unnamed x10, local copies, waits for them, and re-layouts  5.43 us
  transfers between devices with their start and end apart: 27, of which 12 were waited for; matrix products, arithmetic and copies ran while one was open for 1% of the time, Pallas kernels for 9%

profile of v4, /device:TPU:0, one launch (start us, length us, event | category | flops | bytes accessed | tf_op | source)
XLA Modules:
  0.0 96.4 jit_solution(9586891613994828943)
XLA Ops:
  1.2 3.0 %collective-permute-start = (bf16[128,1152]{1,0:T(8,128)(2,1)}, bf16[128,1152]{1,0:T(8,128)(2,1)S(1)}, u32[]{:S(2)}, u32[]{:S(2)}) collective-permute-start(bf16[128,1152]{1,0:T(8,128)(2,1)} %refs_0_.1), channel_id=1, source_target_pairs={{0,1},{4,5},{1,0},{5,4},{2,3},{6,7},{3,2},{7,6},{8,9},{12,13},{9,8... | collective-permute-start | bytes 884744 | tf_op jit(solution)/shard_map/ppermute | solution.py:34
  4.2 2.6 %collective-permute-start.1 = (bf16[128,1152]{1,0:T(8,128)(2,1)}, bf16[128,1152]{1,0:T(8,128)(2,1)S(1)}, u32[]{:S(2)}, u32[]{:S(2)}) collective-permute-start(bf16[128,1152]{1,0:T(8,128)(2,1)} %refs_0_.1), channel_id=1, source_target_pairs={{0,2},{4,6},{1,3},{5,7},{2,0},{6,4},{3,1},{7,5},{8,10},{12,14},{9,... | collective-permute-start | bytes 884744 | tf_op jit(solution)/shard_map/ppermute | solution.py:34
  6.8 1.5 %collective-permute-start.2 = (bf16[128,1152]{1,0:T(8,128)(2,1)}, bf16[128,1152]{1,0:T(8,128)(2,1)S(1)}, u32[]{:S(2)}, u32[]{:S(2)}) collective-permute-start(bf16[128,1152]{1,0:T(8,128)(2,1)} %refs_1_.1), channel_id=1, source_target_pairs={{0,8},{4,12},{1,9},{5,13},{2,10},{6,14},{3,11},{7,15},{8,0},{12,4}... | collective-permute-start | bytes 884744 | tf_op jit(solution)/shard_map/ppermute | solution.py:34
  8.3 1.5 %collective-permute-start.3 = (bf16[128,1152]{1,0:T(8,128)(2,1)}, bf16[128,1152]{1,0:T(8,128)(2,1)S(1)}, u32[]{:S(2)}, u32[]{:S(2)}) collective-permute-start(bf16[128,1152]{1,0:T(8,128)(2,1)} %refs_1_.1), channel_id=1, source_target_pairs={{0,16},{4,20},{1,17},{5,21},{2,18},{6,22},{3,19},{7,23},{8,24},{12... | collective-permute-start | bytes 884744 | tf_op jit(solution)/shard_map/ppermute | solution.py:34
  9.8 1.7 %copy-done = bf16[1152,1152]{1,0:T(8,128)(2,1)S(1)} copy-done((bf16[1152,1152]{1,0:T(8,128)(2,1)S(1)}, bf16[1152,1152]{1,0:T(8,128)(2,1)}, u32[]{:S(2)}) %copy-start) | copy-done | bytes 2654232
  11.6 1.7 %copy-done.2 = bf16[1152,1152]{1,0:T(8,128)(2,1)S(1)} copy-done((bf16[1152,1152]{1,0:T(8,128)(2,1)S(1)}, bf16[1152,1152]{1,0:T(8,128)(2,1)}, u32[]{:S(2)}) %copy-start.2) | copy-done | bytes 2654232
  15.3 2.8 %project.3 = (bf16[256,1152]{1,0:T(8,128)(2,1)S(1)}, f32[256,1152]{1,0:T(8,128)S(1)}, f32[256,128]{1,0:T(8,128)S(1)}, bf16[256,1152]{1,0:T(8,128)(2,1)S(1)}) custom-call(bf16[1152,1152]{1,0:T(8,128)(2,1)S(1)} %copy-done, bf16[1152,1152]{1,0:T(8,128)(2,1)S(1)} %copy-done.2, bf16[128,1152]{1,0:T(8,128)(2,1)S(1)} %copy-done.3, bf16[128,1152]{1,0:T(8,128)(2,1)S(1)} %copy-done.4, ...), custom_call_target="tpu_custom_call" | custom-call | flops 1358954496 | bytes 8847360 | tf_op jit(solution)/shard_map/project/pallas_call | solution.py:104
  18.0 2.4 %collective-permute-done.1.refs_0_ = bf16[128,1152]{1,0:T(8,128)(2,1)S(1)} collective-permute-done((bf16[128,1152]{1,0:T(8,128)(2,1)}, bf16[128,1152]{1,0:T(8,128)(2,1)S(1)}, u32[]{:S(2)}, u32[]{:S(2)}) %collective-permute-start.1) | collective-permute-done | bytes 294944 | tf_op jit(solution)/shard_map/ppermute | solution.py:34
  22.0 1.5 %collective-permute-start.7 = (bf16[128,1152]{1,0:T(8,128)(2,1)S(1)}, bf16[128,1152]{1,0:T(8,128)(2,1)S(1)}, u32[]{:S(2)}, u32[]{:S(2)}) collective-permute-start(bf16[128,1152]{1,0:T(8,128)(2,1)S(1)} %collective-permute-done.3.refs_1_), channel_id=1, source_target_pairs={{0,8},{4,12},{1,9},{5,13},{2,10},{6,14},{3,11},{7,15},{8,0},{12,4}... | collective-permute-start | bytes 884744 | tf_op jit(solution)/shard_map/ppermute | solution.py:34
  23.5 2.8 %project.5 = (bf16[256,1152]{1,0:T(8,128)(2,1)S(1)}, f32[256,1152]{1,0:T(8,128)S(1)}, f32[256,128]{1,0:T(8,128)S(1)}, bf16[256,1152]{1,0:T(8,128)(2,1)S(1)}) custom-call(bf16[1152,1152]{1,0:T(8,128)(2,1)S(1)} %copy-done, bf16[1152,1152]{1,0:T(8,128)(2,1)S(1)} %copy-done.2, bf16[128,1152]{1,0:T(8,128)(2,1)S(1)} %collective-permute-done.1.refs_0_, ...), custom_call_target="tpu_custom_call" | custom-call | flops 1358954496 | bytes 8847360 | tf_op jit(solution)/shard_map/project/pallas_call | solution.py:104
  26.3 2.8 %project.4 = (bf16[256,1152]{1,0:T(8,128)(2,1)S(1)}, f32[256,1152]{1,0:T(8,128)S(1)}, f32[256,128]{1,0:T(8,128)S(1)}, bf16[256,1152]{1,0:T(8,128)(2,1)S(1)}) custom-call(bf16[1152,1152]{1,0:T(8,128)(2,1)S(1)} %copy-done, bf16[1152,1152]{1,0:T(8,128)(2,1)S(1)} %copy-done.2, bf16[128,1152]{1,0:T(8,128)(2,1)S(1)} %collective-permute-done.refs_0_, ...), custom_call_target="tpu_custom_call" | custom-call | flops 1358954496 | bytes 8847360 | tf_op jit(solution)/shard_map/project/pallas_call | solution.py:104
  29.1 1.3 %collective-permute-done.6.refs_0_ = bf16[128,1152]{1,0:T(8,128)(2,1)S(1)} collective-permute-done((bf16[128,1152]{1,0:T(8,128)(2,1)S(1)}, bf16[128,1152]{1,0:T(8,128)(2,1)S(1)}, u32[]{:S(2)}, u32[]{:S(2)}) %collective-permute-start.6) | collective-permute-done | bytes 294944 | tf_op jit(solution)/shard_map/ppermute | solution.py:34
  33.1 18.6 %block.1 = (f32[288,768]{1,0:T(8,128)S(1)}, bf16[296,768]{1,0:T(8,128)(2,1)S(1)}, bf16[296,768]{1,0:T(8,128)(2,1)S(1)}, bf16[296,768]{1,0:T(8,128)(2,1)S(1)}, f3...) custom-call(f32[2]{0:T(128)S(1)} %pad_maximum_fusion.1.scalars, ...), custom_call_target="tpu_custom_call" | custom-call | flops 8908701696 | bytes 19464192 | tf_op jit(solution)/shard_map/block/pallas_call | solution.py:292
  51.7 2.2 %collective-permute-start.20 = (bf16[576,384]{1,0:T(8,128)(2,1)S(1)}, bf16[576,384]{1,0:T(8,128)(2,1)S(1)}, u32[]{:S(2)}, u32[]{:S(2)}) collective-permute-start(bf16[576,384]{1,0:T(8,128)(2,1)S(1)} %get-tuple-element.110), channel_id=1, source_target_pairs={{0,2},{4,6},{1,3},{5,7},{2,0},{6,4},{3,1},{7,5},{8,10},{12,14},{9,... | collective-permute-start | bytes 1327112 | tf_op jit(solution)/shard_map/ppermute | solution.py:34
  53.9 1.5 %collective-permute-start.14 = (bf16[296,768]{1,0:T(8,128)(2,1)S(1)}, bf16[296,768]{1,0:T(8,128)(2,1)S(1)}, u32[]{:S(2)}, u32[]{:S(2)}) collective-permute-start(bf16[296,768]{1,0:T(8,128)(2,1)S(1)} %get-tuple-element.101), channel_id=1, source_target_pairs={{0,8},{4,12},{1,9},{5,13},{2,10},{6,14},{3,11},{7,15},{8,0},{12,4}... | collective-permute-start | bytes 1363976 | tf_op jit(solution)/shard_map/ppermute | solution.py:34
  55.4 1.5 %collective-permute-start.15 = (bf16[296,768]{1,0:T(8,128)(2,1)S(1)}, bf16[296,768]{1,0:T(8,128)(2,1)S(1)}, u32[]{:S(2)}, u32[]{:S(2)}) collective-permute-start(bf16[296,768]{1,0:T(8,128)(2,1)S(1)} %get-tuple-element.102), channel_id=1, source_target_pairs={{0,16},{4,20},{1,17},{5,21},{2,18},{6,22},{3,19},{7,23},{8,24},{12... | collective-permute-start | bytes 1363976 | tf_op jit(solution)/shard_map/ppermute | solution.py:34
  57.4 17.0 %collective-permute-done.20.arrived = bf16[576,384]{1,0:T(8,128)(2,1)S(1)} collective-permute-done((bf16[576,384]{1,0:T(8,128)(2,1)S(1)}, bf16[576,384]{1,0:T(8,128)(2,1)S(1)}, u32[]{:S(2)}, u32[]{:S(2)}) %collective-permute-start.20) | collective-permute-done | bytes 442400 | tf_op jit(solution)/shard_map/ppermute | solution.py:34
  74.6 2.5 %collective-permute-done.15.refs_1_ = bf16[296,768]{1,0:T(8,128)(2,1)S(1)} collective-permute-done((bf16[296,768]{1,0:T(8,128)(2,1)S(1)}, bf16[296,768]{1,0:T(8,128)(2,1)S(1)}, u32[]{:S(2)}, u32[]{:S(2)}) %collective-permute-start.15) | collective-permute-done | bytes 454688 | tf_op jit(solution)/shard_map/ppermute | solution.py:34
  78.6 1.0 %collective-permute-start.18 = (bf16[80,768]{1,0:T(8,128)(2,1)S(1)}, bf16[80,768]{1,0:T(8,128)(2,1)S(1)}, u32[]{:S(2)}, u32[]{:S(2)}) collective-permute-start(bf16[80,768]{1,0:T(8,128)(2,1)S(1)} %get-tuple-element.107), channel_id=1, source_target_pairs={{0,2},{4,6},{1,3},{5,7},{2,0},{6,4},{3,1},{7,5},{8,10},{12,14},{9,... | collective-permute-start | bytes 368648 | tf_op jit(solution)/shard_map/ppermute | solution.py:34
  79.6 2.4 %collective-permute-start.19 = (bf16[80,768]{1,0:T(8,128)(2,1)S(1)}, bf16[80,768]{1,0:T(8,128)(2,1)S(1)}, u32[]{:S(2)}, u32[]{:S(2)}) collective-permute-start(bf16[80,768]{1,0:T(8,128)(2,1)S(1)} %get-tuple-element.108), channel_id=1, source_target_pairs={{0,3},{4,7},{1,2},{5,6},{2,1},{6,5},{3,0},{7,4},{8,11},{12,15},{9,... | collective-permute-start | bytes 368648 | tf_op jit(solution)/shard_map/ppermute | solution.py:34
  82.1 2.9 %collective-permute-done.21.refs_0_ = bf16[288,384]{1,0:T(8,128)(2,1)S(1)} collective-permute-done((bf16[288,384]{1,0:T(8,128)(2,1)S(1)}, bf16[288,384]{1,0:T(8,128)(2,1)S(1)}, u32[]{:S(2)}, u32[]{:S(2)}) %collective-permute-start.21) | collective-permute-done | bytes 221216 | tf_op jit(solution)/shard_map/ppermute | solution.py:34
  85.1 1.6 %collective-permute-start.22 = (bf16[72,384]{1,0:T(8,128)(2,1)S(1)}, bf16[72,384]{1,0:T(8,128)(2,1)S(1)}, u32[]{:S(2)}, u32[]{:S(2)}) collective-permute-start(bf16[72,384]{1,0:T(8,128)(2,1)S(1)} %get-tuple-element.114), channel_id=1, source_target_pairs={{0,8},{4,12},{1,9},{5,13},{2,10},{6,14},{3,11},{7,15},{8,0},{12,4}... | collective-permute-start | bytes 165896 | tf_op jit(solution)/shard_map/ppermute | solution.py:34
  86.7 1.8 %collective-permute-start.23 = (bf16[72,384]{1,0:T(8,128)(2,1)S(1)}, bf16[72,384]{1,0:T(8,128)(2,1)S(1)}, u32[]{:S(2)}, u32[]{:S(2)}) collective-permute-start(bf16[72,384]{1,0:T(8,128)(2,1)S(1)} %get-tuple-element.115), channel_id=1, source_target_pairs={{0,16},{4,20},{1,17},{5,21},{2,18},{6,22},{3,19},{7,23},{8,24},{12... | collective-permute-start | bytes 165896 | tf_op jit(solution)/shard_map/ppermute | solution.py:34
  90.9 2.7 %collective-permute-done.24 = bf16[72,384]{1,0:T(8,128)(2,1)S(1)} collective-permute-done((bf16[72,384]{1,0:T(8,128)(2,1)S(1)}, bf16[72,384]{1,0:T(8,128)(2,1)S(1)}, u32[]{:S(2)}, u32[]{:S(2)}) %collective-permute-start.24) | collective-permute-done | bytes 55328 | tf_op jit(solution)/shard_map/ppermute | solution.py:34
  (58 shorter events, 12.9 us)
Async XLA Ops:
  0.6 7.7 %collective-permute-start.4 = (bf16[128,1152]{1,0:T(8,128)(2,1)}, bf16[128,1152]{1,0:T(8,128)(2,1)S(1)}, u32[]{:S(2)}, u32[]{:S(2)}) collective-permute-start(bf16[128,1152]{1,0:T(8,128)(2,1)} %refs_0_.1), channel_id=1, source_target_pairs={{0,4},{4,0},{1,5},{5,1},{2,6},{6,2},{3,7},{7,3},{8,12},{12,8},{9,1... | collective-permute-start | bytes 884744 | tf_op jit(solution)/shard_map/ppermute | solution.py:34
  1.1 8.7 %collective-permute-start.5 = (bf16[128,1152]{1,0:T(8,128)(2,1)}, bf16[128,1152]{1,0:T(8,128)(2,1)S(1)}, u32[]{:S(2)}, u32[]{:S(2)}) collective-permute-start(bf16[128,1152]{1,0:T(8,128)(2,1)} %refs_1_.1), channel_id=1, source_target_pairs={{0,4},{4,0},{1,5},{5,1},{2,6},{6,2},{3,7},{7,3},{8,12},{12,8},{9,1... | collective-permute-start | bytes 884744 | tf_op jit(solution)/shard_map/ppermute | solution.py:34
  1.2 16.8 %collective-permute-start = (bf16[128,1152]{1,0:T(8,128)(2,1)}, bf16[128,1152]{1,0:T(8,128)(2,1)S(1)}, u32[]{:S(2)}, u32[]{:S(2)}) collective-permute-start(bf16[128,1152]{1,0:T(8,128)(2,1)} %refs_0_.1), channel_id=1, source_target_pairs={{0,1},{4,5},{1,0},{5,4},{2,3},{6,7},{3,2},{7,6},{8,9},{12,13},{9,8... | collective-permute-start | bytes 884744 | tf_op jit(solution)/shard_map/ppermute | solution.py:34
  4.2 16.2 %collective-permute-start.1 = (bf16[128,1152]{1,0:T(8,128)(2,1)}, bf16[128,1152]{1,0:T(8,128)(2,1)S(1)}, u32[]{:S(2)}, u32[]{:S(2)}) collective-permute-start(bf16[128,1152]{1,0:T(8,128)(2,1)} %refs_0_.1), channel_id=1, source_target_pairs={{0,2},{4,6},{1,3},{5,7},{2,0},{6,4},{3,1},{7,5},{8,10},{12,14},{9,... | collective-permute-start | bytes 884744 | tf_op jit(solution)/shard_map/ppermute | solution.py:34
  6.8 13.6 %collective-permute-start.2 = (bf16[128,1152]{1,0:T(8,128)(2,1)}, bf16[128,1152]{1,0:T(8,128)(2,1)S(1)}, u32[]{:S(2)}, u32[]{:S(2)}) collective-permute-start(bf16[128,1152]{1,0:T(8,128)(2,1)} %refs_1_.1), channel_id=1, source_target_pairs={{0,8},{4,12},{1,9},{5,13},{2,10},{6,14},{3,11},{7,15},{8,0},{12,4}... | collective-permute-start | bytes 884744 | tf_op jit(solution)/shard_map/ppermute | solution.py:34
  8.3 12.1 %collective-permute-start.3 = (bf16[128,1152]{1,0:T(8,128)(2,1)}, bf16[128,1152]{1,0:T(8,128)(2,1)S(1)}, u32[]{:S(2)}, u32[]{:S(2)}) collective-permute-start(bf16[128,1152]{1,0:T(8,128)(2,1)} %refs_1_.1), channel_id=1, source_target_pairs={{0,16},{4,20},{1,17},{5,21},{2,18},{6,22},{3,19},{7,23},{8,24},{12... | collective-permute-start | bytes 884744 | tf_op jit(solution)/shard_map/ppermute | solution.py:34
  20.4 3.1 %collective-permute-start.11 = (bf16[128,1152]{1,0:T(8,128)(2,1)S(1)}, bf16[128,1152]{1,0:T(8,128)(2,1)S(1)}, u32[]{:S(2)}, u32[]{:S(2)}) collective-permute-start(bf16[128,1152]{1,0:T(8,128)(2,1)S(1)} %collective-permute-done.3.refs_1_), channel_id=1, source_target_pairs={{0,4},{4,0},{1,5},{5,1},{2,6},{6,2},{3,7},{7,3},{8,12},{12,8},{9,1... | collective-permute-start | bytes 884744 | tf_op jit(solution)/shard_map/ppermute | solution.py:34
  21.0 5.4 %collective-permute-start.8 = (bf16[128,1152]{1,0:T(8,128)(2,1)S(1)}, bf16[128,1152]{1,0:T(8,128)(2,1)S(1)}, u32[]{:S(2)}, u32[]{:S(2)}) collective-permute-start(bf16[128,1152]{1,0:T(8,128)(2,1)S(1)} %collective-permute-done.refs_0_), channel_id=1, source_target_pairs={{0,4},{4,0},{1,5},{5,1},{2,6},{6,2},{3,7},{7,3},{8,12},{12,8},{9,1... | collective-permute-start | bytes 884744 | tf_op jit(solution)/shard_map/ppermute | solution.py:34
  21.0 5.3 %collective-permute-start.9 = (bf16[128,1152]{1,0:T(8,128)(2,1)S(1)}, bf16[128,1152]{1,0:T(8,128)(2,1)S(1)}, u32[]{:S(2)}, u32[]{:S(2)}) collective-permute-start(bf16[128,1152]{1,0:T(8,128)(2,1)S(1)} %collective-permute-done.2.refs_1_), channel_id=1, source_target_pairs={{0,4},{4,0},{1,5},{5,1},{2,6},{6,2},{3,7},{7,3},{8,12},{12,8},{9,1... | collective-permute-start | bytes 884744 | tf_op jit(solution)/shard_map/ppermute | solution.py:34
  21.5 9.0 %collective-permute-start.6 = (bf16[128,1152]{1,0:T(8,128)(2,1)S(1)}, bf16[128,1152]{1,0:T(8,128)(2,1)S(1)}, u32[]{:S(2)}, u32[]{:S(2)}) collective-permute-start(bf16[128,1152]{1,0:T(8,128)(2,1)S(1)} %collective-permute-done.1.refs_0_), channel_id=1, source_target_pairs={{0,1},{4,5},{1,0},{5,4},{2,3},{6,7},{3,2},{7,6},{8,9},{12,13},{9,8... | collective-permute-start | bytes 884744 | tf_op jit(solution)/shard_map/ppermute | solution.py:34
  22.0 9.1 %collective-permute-start.7 = (bf16[128,1152]{1,0:T(8,128)(2,1)S(1)}, bf16[128,1152]{1,0:T(8,128)(2,1)S(1)}, u32[]{:S(2)}, u32[]{:S(2)}) collective-permute-start(bf16[128,1152]{1,0:T(8,128)(2,1)S(1)} %collective-permute-done.3.refs_1_), channel_id=1, source_target_pairs={{0,8},{4,12},{1,9},{5,13},{2,10},{6,14},{3,11},{7,15},{8,0},{12,4}... | collective-permute-start | bytes 884744 | tf_op jit(solution)/shard_map/ppermute | solution.py:34
  31.1 1.9 %collective-permute-start.12 = (bf16[128,1152]{1,0:T(8,128)(2,1)S(1)}, bf16[128,1152]{1,0:T(8,128)(2,1)S(1)}, u32[]{:S(2)}, u32[]{:S(2)}) collective-permute-start(bf16[128,1152]{1,0:T(8,128)(2,1)S(1)} %collective-permute-done.6.refs_0_), channel_id=1, source_target_pairs={{0,4},{4,0},{1,5},{5,1},{2,6},{6,2},{3,7},{7,3},{8,12},{12,8},{9,1... | collective-permute-start | bytes 884744 | tf_op jit(solution)/shard_map/ppermute | solution.py:34
  31.1 2.0 %collective-permute-start.13 = (bf16[128,1152]{1,0:T(8,128)(2,1)S(1)}, bf16[128,1152]{1,0:T(8,128)(2,1)S(1)}, u32[]{:S(2)}, u32[]{:S(2)}) collective-permute-start(bf16[128,1152]{1,0:T(8,128)(2,1)S(1)} %collective-permute-done.7.refs_1_), channel_id=1, source_target_pairs={{0,4},{4,0},{1,5},{5,1},{2,6},{6,2},{3,7},{7,3},{8,12},{12,8},{9,1... | collective-permute-start | bytes 884744 | tf_op jit(solution)/shard_map/ppermute | solution.py:34
  51.7 22.7 %collective-permute-start.20 = (bf16[576,384]{1,0:T(8,128)(2,1)S(1)}, bf16[576,384]{1,0:T(8,128)(2,1)S(1)}, u32[]{:S(2)}, u32[]{:S(2)}) collective-permute-start(bf16[576,384]{1,0:T(8,128)(2,1)S(1)} %get-tuple-element.110), channel_id=1, source_target_pairs={{0,2},{4,6},{1,3},{5,7},{2,0},{6,4},{3,1},{7,5},{8,10},{12,14},{9,... | collective-permute-start | bytes 1327112 | tf_op jit(solution)/shard_map/ppermute | solution.py:34
  53.9 20.7 %collective-permute-start.14 = (bf16[296,768]{1,0:T(8,128)(2,1)S(1)}, bf16[296,768]{1,0:T(8,128)(2,1)S(1)}, u32[]{:S(2)}, u32[]{:S(2)}) collective-permute-start(bf16[296,768]{1,0:T(8,128)(2,1)S(1)} %get-tuple-element.101), channel_id=1, source_target_pairs={{0,8},{4,12},{1,9},{5,13},{2,10},{6,14},{3,11},{7,15},{8,0},{12,4}... | collective-permute-start | bytes 1363976 | tf_op jit(solution)/shard_map/ppermute | solution.py:34
  55.4 21.7 %collective-permute-start.15 = (bf16[296,768]{1,0:T(8,128)(2,1)S(1)}, bf16[296,768]{1,0:T(8,128)(2,1)S(1)}, u32[]{:S(2)}, u32[]{:S(2)}) collective-permute-start(bf16[296,768]{1,0:T(8,128)(2,1)S(1)} %get-tuple-element.102), channel_id=1, source_target_pairs={{0,16},{4,20},{1,17},{5,21},{2,18},{6,22},{3,19},{7,23},{8,24},{12... | collective-permute-start | bytes 1363976 | tf_op jit(solution)/shard_map/ppermute | solution.py:34
  56.9 20.1 %collective-permute-start.16 = (bf16[296,768]{1,0:T(8,128)(2,1)S(1)}, bf16[296,768]{1,0:T(8,128)(2,1)S(1)}, u32[]{:S(2)}, u32[]{:S(2)}) collective-permute-start(bf16[296,768]{1,0:T(8,128)(2,1)S(1)} %get-tuple-element.103), channel_id=1, source_target_pairs={{0,24},{4,28},{1,25},{5,29},{2,26},{6,30},{3,27},{7,31},{8,16},{12... | collective-permute-start | bytes 1363976 | tf_op jit(solution)/shard_map/ppermute | solution.py:34
  74.5 10.5 %collective-permute-start.21 = (bf16[288,384]{1,0:T(8,128)(2,1)S(1)}, bf16[288,384]{1,0:T(8,128)(2,1)S(1)}, u32[]{:S(2)}, u32[]{:S(2)}) collective-permute-start(bf16[288,384]{1,0:T(8,128)(2,1)S(1)} %get-tuple-element.112), channel_id=1, source_target_pairs={{0,1},{4,5},{1,0},{5,4},{2,3},{6,7},{3,2},{7,6},{8,9},{12,13},{9,8... | collective-permute-start | bytes 663560 | tf_op jit(solution)/shard_map/ppermute | solution.py:34
  77.6 10.9 %collective-permute-start.17 = (bf16[80,768]{1,0:T(8,128)(2,1)S(1)}, bf16[80,768]{1,0:T(8,128)(2,1)S(1)}, u32[]{:S(2)}, u32[]{:S(2)}) collective-permute-start(bf16[80,768]{1,0:T(8,128)(2,1)S(1)} %get-tuple-element.106), channel_id=1, source_target_pairs={{0,1},{4,5},{1,0},{5,4},{2,3},{6,7},{3,2},{7,6},{8,9},{12,13},{9,8... | collective-permute-start | bytes 368648 | tf_op jit(solution)/shard_map/ppermute | solution.py:34
  78.6 10.9 %collective-permute-start.18 = (bf16[80,768]{1,0:T(8,128)(2,1)S(1)}, bf16[80,768]{1,0:T(8,128)(2,1)S(1)}, u32[]{:S(2)}, u32[]{:S(2)}) collective-permute-start(bf16[80,768]{1,0:T(8,128)(2,1)S(1)} %get-tuple-element.107), channel_id=1, source_target_pairs={{0,2},{4,6},{1,3},{5,7},{2,0},{6,4},{3,1},{7,5},{8,10},{12,14},{9,... | collective-permute-start | bytes 368648 | tf_op jit(solution)/shard_map/ppermute | solution.py:34
  79.6 10.5 %collective-permute-start.19 = (bf16[80,768]{1,0:T(8,128)(2,1)S(1)}, bf16[80,768]{1,0:T(8,128)(2,1)S(1)}, u32[]{:S(2)}, u32[]{:S(2)}) collective-permute-start(bf16[80,768]{1,0:T(8,128)(2,1)S(1)} %get-tuple-element.108), channel_id=1, source_target_pairs={{0,3},{4,7},{1,2},{5,6},{2,1},{6,5},{3,0},{7,4},{8,11},{12,15},{9,... | collective-permute-start | bytes 368648 | tf_op jit(solution)/shard_map/ppermute | solution.py:34
  85.1 5.0 %collective-permute-start.22 = (bf16[72,384]{1,0:T(8,128)(2,1)S(1)}, bf16[72,384]{1,0:T(8,128)(2,1)S(1)}, u32[]{:S(2)}, u32[]{:S(2)}) collective-permute-start(bf16[72,384]{1,0:T(8,128)(2,1)S(1)} %get-tuple-element.114), channel_id=1, source_target_pairs={{0,8},{4,12},{1,9},{5,13},{2,10},{6,14},{3,11},{7,15},{8,0},{12,4}... | collective-permute-start | bytes 165896 | tf_op jit(solution)/shard_map/ppermute | solution.py:34
  86.7 4.2 %collective-permute-start.23 = (bf16[72,384]{1,0:T(8,128)(2,1)S(1)}, bf16[72,384]{1,0:T(8,128)(2,1)S(1)}, u32[]{:S(2)}, u32[]{:S(2)}) collective-permute-start(bf16[72,384]{1,0:T(8,128)(2,1)S(1)} %get-tuple-element.115), channel_id=1, source_target_pairs={{0,16},{4,20},{1,17},{5,21},{2,18},{6,22},{3,19},{7,23},{8,24},{12... | collective-permute-start | bytes 165896 | tf_op jit(solution)/shard_map/ppermute | solution.py:34
  88.5 5.1 %collective-permute-start.24 = (bf16[72,384]{1,0:T(8,128)(2,1)S(1)}, bf16[72,384]{1,0:T(8,128)(2,1)S(1)}, u32[]{:S(2)}, u32[]{:S(2)}) collective-permute-start(bf16[72,384]{1,0:T(8,128)(2,1)S(1)} %get-tuple-element.116), channel_id=1, source_target_pairs={{0,24},{4,28},{1,25},{5,29},{2,26},{6,30},{3,27},{7,31},{8,16},{12... | collective-permute-start | bytes 165896 | tf_op jit(solution)/shard_map/ppermute | solution.py:34
  (8 other events, 16.8 us)

commit v5 on v4

--- a/solution.py
+++ b/solution.py
@@ -130,19 +130,18 @@
 
 def pair_terms(cosine, scale, bias, masked):
     logits = scale * cosine + bias
-    small = jnp.exp(-jnp.abs(logits))
-    inverse_sum = 1.0 / (1.0 + small)
-    large_side = logits >= 0.0
-    pair_grads = jnp.where(large_side, inverse_sum, small * inverse_sum)
-    tops = jnp.maximum(logits, 0.0)
+    raised = jnp.exp(logits)
+    total = 1.0 + raised
+    inverse = 1.0 / total
+    losses = jnp.log(total) + (raised - (total - 1.0)) * inverse
+    pair_grads = raised * inverse
     if masked:
         equal = lax.broadcasted_iota(jnp.int32, cosine.shape, 0) == lax.broadcasted_iota(
             jnp.int32, cosine.shape, 1
         )
-        lower = jnp.where(large_side, small * inverse_sum, inverse_sum)
-        pair_grads = jnp.where(equal, -lower, pair_grads)
-        tops = jnp.where(equal, jnp.maximum(-logits, 0.0), tops)
-    return tops + jnp.log1p(small), pair_grads
+        losses = jnp.where(equal, jnp.log1p(jnp.exp(-logits)), losses)
+        pair_grads = jnp.where(equal, -inverse, pair_grads)
+    return losses, pair_grads
 
 
 def lane_sums(values):
@@ -150,13 +149,13 @@
     return sum(total[:, j : j + 128] for j in range(0, total.shape[1], 128))
 
 
-def block_kernel(side, mp_size, first_width, scalars, image_proj, text_proj, *refs):
+def block_kernel(side, mp_size, groups, scalars, image_proj, text_proj, *refs):
     last_shards, refs = refs[:4], refs[4:]
     own_chunks, refs = refs[: side - 1], refs[side - 1 :]
     own_units, refs = refs[: side - 1], refs[side - 1 :]
     own_inverses, refs = refs[: side - 1], refs[side - 1 :]
     other_halves, refs = refs[: side - 1], refs[side - 1 :]
-    firsts, refs = refs[:side], refs[side:]
+    firsts, refs = refs[: side * len(groups)], refs[side * len(groups) :]
     own_late, late_message, refs = refs[0], refs[1], refs[2:]
     stats, projs, last, feats, units, inverses, other_half, dy, grad, piece, sems = refs
     rows, width = dy.shape
@@ -197,12 +196,17 @@
     for copy in other_copies + unit_copies:
         copy.wait()
 
-    def tile(place, with_partners):
-        unit = units[place, :]
-        cosine = lax.dot_general(
-            unit.astype(BF16), other_half[...], (((1,), (1,)), ((), ())), preferred_element_type=F32
+    def cosines(i):
+        half = units[i * chunk_rows : (i + 1) * chunk_rows, :].astype(BF16)
+        return lax.dot_general(
+            half, other_half[...], (((1,), (1,)), ((), ())), preferred_element_type=F32
         )
-        if with_partners:
+
+    total = None
+    cosine = cosines(0)
+    for i in range(side):
+        following = cosines(i + 1) if i + 1 < side else None
+        if i == 0:
             terms = [
                 pair_terms(cosine[:, :chunk_rows], scale, bias, True),
                 pair_terms(cosine[:, chunk_rows:], scale, bias, False),
@@ -211,19 +215,16 @@
         else:
             losses, pair_grads = pair_terms(cosine, scale, bias, False)
         half_grads = pair_grads.astype(BF16)
-        sums = jnp.concatenate(
-            [lane_sums(losses), lane_sums(pair_grads * cosine) * scale, lane_sums(pair_grads)], axis=1
-        )
-        stats[0:1, :] = sums if with_partners else stats[0:1, :] + sums
+        sums = [lane_sums(losses), lane_sums(pair_grads * cosine) * scale, lane_sums(pair_grads)]
+        sums = jnp.concatenate(sums, axis=1)
+        total = sums if total is None else total + sums
         inner = jnp.sum(half_grads.astype(F32) * cosine, axis=-1, keepdims=True)
         grads = jnp.dot(half_grads, other_half[...], preferred_element_type=F32)
-        dy[place, :] = ((grads - unit * inner) * (scale * inverses[place, 0:1])).astype(BF16)
-
-    tile(pl.ds(0, chunk_rows), True)
-
-    @pl.loop(1, side)
-    def _(i):
-        tile(pl.ds(pl.multiple_of(i * chunk_rows, chunk_rows), chunk_rows), False)
+        place = slice(i * chunk_rows, (i + 1) * chunk_rows)
+        grads = (grads - units[place, :] * inner) * (scale * inverses[place, 0:1])
+        dy[place, :] = grads.astype(BF16)
+        cosine = following
+    stats[0:1, :] = total
 
     for copy in feat_copies:
         copy.wait()
@@ -235,11 +236,14 @@
     sums = stats[0:1, :]
     stats[...] = jnp.broadcast_to(sums, stats.shape)
     chunk = width // side
-    for t in range(side):
-        first = pl.multiple_of(jnp.bitwise_xor(unit_row, t) * chunk, chunk)
-        firsts[t][:chunk, :] = grad[pl.ds(first, chunk), :first_width].astype(firsts[t].dtype)
-        if t:
-            firsts[t][chunk:, :] = stat_rows(sums, first_width).astype(BF16)
+    for g, (begin, end) in enumerate(groups):
+        for t in range(side):
+            out = firsts[side * g + t]
+            first = pl.multiple_of(jnp.bitwise_xor(unit_row, t) * chunk, chunk)
+            out[:chunk, :] = grad[pl.ds(first, chunk), begin:end].astype(out.dtype)
+            if t and g == 0:
+                out[chunk:, :] = stat_rows(sums, end - begin).astype(BF16)
+    first_width = groups[-1][1]
     out_rows = chunk // (2 * side)
     for column in range(side):
         for i in range(side):
@@ -277,29 +281,34 @@
     return parts
 
 
-def block_grads(layout, first_width, scalars, image_proj, text_proj, last_shards, projected):
+def block_grads(layout, groups, scalars, image_proj, text_proj, last_shards, projected):
     side = layout.side
     chunk_rows, width = projected[0][0].shape
     rows = side * chunk_rows
     chunk = width // side
     anywhere = pl.BlockSpec(memory_space=pl.ANY)
     vmem = pl.BlockSpec(memory_space=pltpu.VMEM)
+    first_width = groups[-1][1]
     late_width = width - first_width
     operands = [image_proj, text_proj, *last_shards]
     operands += [x for column in zip(*projected) for x in column]
+    out_shape = []
+    for begin, end in groups:
+        out_shape.append(jax.ShapeDtypeStruct((chunk, end - begin), F32))
+        message = jax.ShapeDtypeStruct((chunk if begin else chunk + 8, end - begin), BF16)
+        out_shape += [message] * (side - 1)
     needed = 4 * width * width + 12 * rows * width + 4 * chunk_rows * width
     needed += 4 * width * (width + late_width) + 24 * chunk_rows * rows + 7 * 1024 * 1024
     return pl.pallas_call(
-        functools.partial(block_kernel, side, layout.mp, first_width),
-        out_shape=[jax.ShapeDtypeStruct((chunk, first_width), F32)]
-        + [jax.ShapeDtypeStruct((chunk + 8, first_width), BF16)] * (side - 1)
+        functools.partial(block_kernel, side, layout.mp, groups),
+        out_shape=out_shape
         + [jax.ShapeDtypeStruct((width // 2, late_width), F32)]
         + [jax.ShapeDtypeStruct((width // 2, late_width), BF16)]
         + [jax.ShapeDtypeStruct((8, 384), F32)],
         in_specs=[pl.BlockSpec(memory_space=pltpu.SMEM)]
         + [pl.BlockSpec(memory_space=pltpu.HBM)] * 2
         + [anywhere] * (len(operands) - 2),
-        out_specs=[vmem] * (side + 3),
+        out_specs=[vmem] * (len(out_shape) + 3),
         scratch_shapes=[
             pltpu.VMEM((2, width, width), BF16),
             pltpu.VMEM((2, chunk_rows, width), BF16),
@@ -326,19 +335,22 @@
     return tree_sum([own[:rows, :]] + [x[:rows, :].astype(F32) for x in arrived])
 
 
-def first_kernel(side, mp_size, own, own_stats, *refs):
-    arrived, outs = refs[: side - 1], refs[side - 1 : 2 * side - 1]
-    stats, total, piece = refs[2 * side - 1 :]
+def first_kernel(side, mp_size, has_stats, own, *refs):
+    own_stats, refs = (refs[0], refs[1:]) if has_stats else (None, refs)
+    arrived, outs, refs = refs[: side - 1], refs[side - 1 : 2 * side - 1], refs[2 * side - 1 :]
+    total, piece = refs[-2:]
     chunk, width = own.shape
     out_rows = chunk // (2 * side)
     total[...] = arrived_sum(own, arrived, chunk)
-    parts = [x[chunk:, :384].astype(F32) for x in arrived]
-    sums = tree_sum([own_stats[0:1, :]] + [x[0:1] + x[1:2] + x[2:3] for x in parts])
-    stats[...] = jnp.broadcast_to(sums, stats.shape)
+    if piece.shape[0] > 2 * out_rows:
+        piece[2 * out_rows :, :] = jnp.zeros((piece.shape[0] - 2 * out_rows, width), F32)
+    if has_stats:
+        parts = [x[chunk:, :384].astype(F32) for x in arrived]
+        sums = tree_sum([own_stats[0:1, :]] + [x[0:1] + x[1:2] + x[2:3] for x in parts])
+        refs[0][...] = jnp.broadcast_to(sums, refs[0].shape)
+        piece[piece.shape[0] - 8 :, :] = stat_rows(sums, width)
     dp_index, mp_index = lax.axis_index("dp"), lax.axis_index("mp")
     unit_column = lax.rem(dp_index // 2 * mp_size + mp_index, side)
-    piece[2 * out_rows :, :] = jnp.zeros((piece.shape[0] - 2 * out_rows, width), F32)
-    piece[piece.shape[0] - 8 :, :] = stat_rows(sums, width)
     for column in range(side):
         for core in range(2):
             source = shard_of(column, core, mp_size) * out_rows
@@ -349,19 +361,23 @@
 def first_pieces(layout, own, own_stats, arrived):
     side = layout.side
     chunk, width = own.shape
-    rows = (2 * (chunk // (2 * side)) + 7) // 8 * 8 + 8
+    has_stats = own_stats is not None
+    rows = (2 * (chunk // (2 * side)) + 7) // 8 * 8 + (8 if has_stats else 0)
     vmem = pl.BlockSpec(memory_space=pltpu.VMEM)
+    out_shape = [jax.ShapeDtypeStruct((rows, width), F32)]
+    out_shape += [jax.ShapeDtypeStruct((rows, width), BF16)] * (side - 1)
+    operands = [own, *([own_stats] if has_stats else []), *arrived]
+    if has_stats:
+        out_shape.append(jax.ShapeDtypeStruct((8, 384), F32))
     return pl.pallas_call(
-        functools.partial(first_kernel, side, layout.mp),
-        out_shape=[jax.ShapeDtypeStruct((rows, width), F32)]
-        + [jax.ShapeDtypeStruct((rows, width), BF16)] * (side - 1)
-        + [jax.ShapeDtypeStruct((8, 384), F32)],
-        in_specs=[vmem] * (side + 1),
-        out_specs=[vmem] * (side + 1),
+        functools.partial(first_kernel, side, layout.mp, has_stats),
+        out_shape=out_shape,
+        in_specs=[vmem] * len(operands),
+        out_specs=[vmem] * len(out_shape),
         scratch_shapes=[pltpu.VMEM((chunk, width), F32), pltpu.VMEM((rows, width), F32)],
         compiler_params=pltpu.CompilerParams(vmem_limit_bytes=12 * 1024 * 1024),
         name="first",
-    )(own, own_stats, *arrived)
+    )(*operands)
 
 
 def halve_kernel(own, arrived, keep, message):
@@ -457,36 +473,44 @@
         (images[last], texts[last], projected)
     )
     swap(last)
-    first_width = width - width // 3
+    groups = ((0, 512), (512, 896))
     results = block_grads(
         layout,
-        first_width,
+        groups,
         scalars,
         image_proj,
         text_proj,
         [images[last], texts[last], *swapped[last]],
         [projected[t] for t in range(last)],
     )
-    firsts, (late, message, stats) = list(results[:side]), results[side:]
-
-    firsts[1:] = [layout.along_column(firsts[t], t) for t in range(1, side)]
+    count = side * len(groups)
+    firsts = [list(results[g : g + side]) for g in range(0, count, side)]
+    late, message, stats = results[count:]
+
     bit = side // 2
     arrived = layout.along_row(message, bit)
+    for g, group in enumerate(firsts):
+        if g:
+            group[1:], firsts[g - 1][1] = lax.optimization_barrier((group[1:], firsts[g - 1][1]))
+        group[1:] = [layout.along_column(group[t], t) for t in range(1, side)]
     while bit > 1:
         late, message = halve(late, arrived)
         bit //= 2
         arrived = layout.along_row(message, bit)
-    *firsts, stats = first_pieces(layout, firsts[0], stats, firsts[1:])
-
-    firsts[1:] = [layout.along_row(firsts[t], t) for t in range(1, side)]
+
+    for g, group in enumerate(firsts):
+        own_stats = None if g else stats
+        pieces = list(first_pieces(layout, group[0], own_stats, group[1:]))
+        if not g:
+            stats = pieces.pop()
+        group[:] = [pieces[0]] + [layout.along_row(pieces[t], t) for t in range(1, side)]
     lates = list(late_pieces(layout, late, arrived))
     lates[1:] = [layout.along_column(lates[t], t) for t in range(1, side)]
     firsts, lates = lax.optimization_barrier((firsts, lates))
     last_rows = 2 * out_rows
-    first_sum = tree_sum([x[:last_rows].astype(F32) for x in firsts])
-    late_sum = tree_sum([x.astype(F32) for x in lates])
-    total = jnp.concatenate([first_sum, late_sum], axis=1)
-    parts = [x[-8:-5, :384].astype(F32) for x in firsts[1:]]
+    sums = [tree_sum([x[:last_rows].astype(F32) for x in group]) for group in [*firsts, lates]]
+    total = jnp.concatenate(sums, axis=1)
+    parts = [x[-8:-5, :384].astype(F32) for x in firsts[0][1:]]
     stat_total = tree_sum([stats[0]] + [x[0] + x[1] + x[2] for x in parts])
 
     upper, lower = total[:out_rows], total[out_rows:]

time: 96.6 us -> 93.9 us (0.972)
  waiting for transfers between devices: 31.6 us -> 24.9 us
  starting transfers between devices: 27.8 us -> 33.7 us
  Pallas kernels: 27.7 us -> 25.6 us
    ppermute x27 -> x33, waiting for transfers between devices: 31.6 us -> 24.9 us  [send(): return lax.ppermute(value, AXES, pairs)]
    ppermute x27 -> x33, starting transfers between devices: 27.8 us -> 33.7 us  [send(): return lax.ppermute(value, AXES, pairs)]
    pallas_call x2 -> x3, Pallas kernels: 19.2 us -> 17.2 us  [the longest x1 16.5 us: block_grads(): pl.pallas_call(functools.partial(block_kernel, side, layout.mp, groups),...]
  transfers between devices with their start and end apart: 27 -> 33, of which waited for: 12 -> 12; matrix products, arithmetic and copies ran while one was open for 1% -> 1% of each run, Pallas kernels for 9% -> 10%
where the time goes in v5:
time: 93.9 us; the launch traced here: 93.6 us
  starting transfers between devices  33.7 us (36%)
  Pallas kernels  25.6 us (27%)
  waiting for transfers between devices  24.9 us (27%)
  local copies, waits for them, and re-layouts  6.02 us (6%)
  between operations  2.19 us (2%)
  other arithmetic  1.15 us (1%)
    ppermute x33, starting transfers between devices, send(): return lax.ppermute(value, AXES, pairs)  33.7 us
    ppermute x33, waiting for transfers between devices, send(): return lax.ppermute(value, AXES, pairs)  24.9 us
    pallas_call x1, Pallas kernels, block_grads(): pl.pallas_call(functools.partial(block_kernel, side, layout.mp, groups),...  16.5 us
    pallas_call x3, Pallas kernels, project_chunk(): pl.pallas_call(project_kernel, out_shape=[jax.ShapeDtypeStruct((rows, wid...  8.31 us
    unnamed x10, local copies, waits for them, and re-layouts  5.43 us
  transfers between devices with their start and end apart: 33, of which 12 were waited for; matrix products, arithmetic and copies ran while one was open for 1% of the time, Pallas kernels for 10%

profile of v5, /device:TPU:0, one launch (start us, length us, event | category | flops | bytes accessed | tf_op | source)
XLA Modules:
  0.0 93.6 jit_solution(12650335919962717881)
XLA Ops:
  1.2 3.0 %collective-permute-start = (bf16[128,1152]{1,0:T(8,128)(2,1)}, bf16[128,1152]{1,0:T(8,128)(2,1)S(1)}, u32[]{:S(2)}, u32[]{:S(2)}) collective-permute-start(bf16[128,1152]{1,0:T(8,128)(2,1)} %refs_0_.1), channel_id=1, source_target_pairs={{0,1},{4,5},{1,0},{5,4},{2,3},{6,7},{3,2},{7,6},{8,9},{12,13},{9,8... | collective-permute-start | bytes 884744 | tf_op jit(solution)/shard_map/ppermute | solution.py:34
  4.2 2.6 %collective-permute-start.1 = (bf16[128,1152]{1,0:T(8,128)(2,1)}, bf16[128,1152]{1,0:T(8,128)(2,1)S(1)}, u32[]{:S(2)}, u32[]{:S(2)}) collective-permute-start(bf16[128,1152]{1,0:T(8,128)(2,1)} %refs_0_.1), channel_id=1, source_target_pairs={{0,2},{4,6},{1,3},{5,7},{2,0},{6,4},{3,1},{7,5},{8,10},{12,14},{9,... | collective-permute-start | bytes 884744 | tf_op jit(solution)/shard_map/ppermute | solution.py:34
  8.3 1.5 %collective-permute-start.3 = (bf16[128,1152]{1,0:T(8,128)(2,1)}, bf16[128,1152]{1,0:T(8,128)(2,1)S(1)}, u32[]{:S(2)}, u32[]{:S(2)}) collective-permute-start(bf16[128,1152]{1,0:T(8,128)(2,1)} %refs_1_.1), channel_id=1, source_target_pairs={{0,16},{4,20},{1,17},{5,21},{2,18},{6,22},{3,19},{7,23},{8,24},{12... | collective-permute-start | bytes 884744 | tf_op jit(solution)/shard_map/ppermute | solution.py:34
  9.8 1.7 %copy-done = bf16[1152,1152]{1,0:T(8,128)(2,1)S(1)} copy-done((bf16[1152,1152]{1,0:T(8,128)(2,1)S(1)}, bf16[1152,1152]{1,0:T(8,128)(2,1)}, u32[]{:S(2)}) %copy-start) | copy-done | bytes 2654232
  11.6 1.7 %copy-done.2 = bf16[1152,1152]{1,0:T(8,128)(2,1)S(1)} copy-done((bf16[1152,1152]{1,0:T(8,128)(2,1)S(1)}, bf16[1152,1152]{1,0:T(8,128)(2,1)}, u32[]{:S(2)}) %copy-start.2) | copy-done | bytes 2654232
  15.3 2.8 %project.3 = (bf16[256,1152]{1,0:T(8,128)(2,1)S(1)}, f32[256,1152]{1,0:T(8,128)S(1)}, f32[256,128]{1,0:T(8,128)S(1)}, bf16[256,1152]{1,0:T(8,128)(2,1)S(1)}) custom-call(bf16[1152,1152]{1,0:T(8,128)(2,1)S(1)} %copy-done, bf16[1152,1152]{1,0:T(8,128)(2,1)S(1)} %copy-done.2, bf16[128,1152]{1,0:T(8,128)(2,1)S(1)} %copy-done.3, bf16[128,1152]{1,0:T(8,128)(2,1)S(1)} %copy-done.4, ...), custom_call_target="tpu_custom_call" | custom-call | flops 1358954496 | bytes 8847360 | tf_op jit(solution)/shard_map/project/pallas_call | solution.py:104
  18.0 2.4 %collective-permute-done.1.refs_0_ = bf16[128,1152]{1,0:T(8,128)(2,1)S(1)} collective-permute-done((bf16[128,1152]{1,0:T(8,128)(2,1)}, bf16[128,1152]{1,0:T(8,128)(2,1)S(1)}, u32[]{:S(2)}, u32[]{:S(2)}) %collective-permute-start.1) | collective-permute-done | bytes 294944 | tf_op jit(solution)/shard_map/ppermute | solution.py:34
  22.0 1.5 %collective-permute-start.7 = (bf16[128,1152]{1,0:T(8,128)(2,1)S(1)}, bf16[128,1152]{1,0:T(8,128)(2,1)S(1)}, u32[]{:S(2)}, u32[]{:S(2)}) collective-permute-start(bf16[128,1152]{1,0:T(8,128)(2,1)S(1)} %collective-permute-done.3.refs_1_), channel_id=1, source_target_pairs={{0,8},{4,12},{1,9},{5,13},{2,10},{6,14},{3,11},{7,15},{8,0},{12,4}... | collective-permute-start | bytes 884744 | tf_op jit(solution)/shard_map/ppermute | solution.py:34
  23.5 2.8 %project.5 = (bf16[256,1152]{1,0:T(8,128)(2,1)S(1)}, f32[256,1152]{1,0:T(8,128)S(1)}, f32[256,128]{1,0:T(8,128)S(1)}, bf16[256,1152]{1,0:T(8,128)(2,1)S(1)}) custom-call(bf16[1152,1152]{1,0:T(8,128)(2,1)S(1)} %copy-done, bf16[1152,1152]{1,0:T(8,128)(2,1)S(1)} %copy-done.2, bf16[128,1152]{1,0:T(8,128)(2,1)S(1)} %collective-permute-done.1.refs_0_, ...), custom_call_target="tpu_custom_call" | custom-call | flops 1358954496 | bytes 8847360 | tf_op jit(solution)/shard_map/project/pallas_call | solution.py:104
  26.3 2.8 %project.4 = (bf16[256,1152]{1,0:T(8,128)(2,1)S(1)}, f32[256,1152]{1,0:T(8,128)S(1)}, f32[256,128]{1,0:T(8,128)S(1)}, bf16[256,1152]{1,0:T(8,128)(2,1)S(1)}) custom-call(bf16[1152,1152]{1,0:T(8,128)(2,1)S(1)} %copy-done, bf16[1152,1152]{1,0:T(8,128)(2,1)S(1)} %copy-done.2, bf16[128,1152]{1,0:T(8,128)(2,1)S(1)} %collective-permute-done.refs_0_, ...), custom_call_target="tpu_custom_call" | custom-call | flops 1358954496 | bytes 8847360 | tf_op jit(solution)/shard_map/project/pallas_call | solution.py:104
  33.1 16.5 %block.1 = (f32[288,512]{1,0:T(8,128)S(1)}, bf16[296,512]{1,0:T(8,128)(2,1)S(1)}, bf16[296,512]{1,0:T(8,128)(2,1)S(1)}, bf16[296,512]{1,0:T(8,128)(2,1)S(1)}, f3...) custom-call(f32[2]{0:T(128)S(1)} %pad_maximum_fusion.1.scalars, ...), custom_call_target="tpu_custom_call" | custom-call | flops 8908701696 | bytes 19464192 | tf_op jit(solution)/shard_map/block/pallas_call | solution.py:302
  49.6 1.6 %collective-permute-start.14 = (bf16[296,512]{1,0:T(8,128)(2,1)S(1)}, bf16[296,512]{1,0:T(8,128)(2,1)S(1)}, u32[]{:S(2)}, u32[]{:S(2)}) collective-permute-start(bf16[296,512]{1,0:T(8,128)(2,1)S(1)} %get-tuple-element.120), channel_id=1, source_target_pairs={{0,8},{4,12},{1,9},{5,13},{2,10},{6,14},{3,11},{7,15},{8,0},{12,4}... | collective-permute-start | bytes 909320 | tf_op jit(solution)/shard_map/ppermute | solution.py:34
  51.2 1.5 %collective-permute-start.15 = (bf16[296,512]{1,0:T(8,128)(2,1)S(1)}, bf16[296,512]{1,0:T(8,128)(2,1)S(1)}, u32[]{:S(2)}, u32[]{:S(2)}) collective-permute-start(bf16[296,512]{1,0:T(8,128)(2,1)S(1)} %get-tuple-element.122), channel_id=1, source_target_pairs={{0,16},{4,20},{1,17},{5,21},{2,18},{6,22},{3,19},{7,23},{8,24},{12... | collective-permute-start | bytes 909320 | tf_op jit(solution)/shard_map/ppermute | solution.py:34
  52.7 2.1 %collective-permute-start.26 = (bf16[576,256]{1,0:T(8,128)(2,1)S(1)}, bf16[576,256]{1,0:T(8,128)(2,1)S(1)}, u32[]{:S(2)}, u32[]{:S(2)}) collective-permute-start(bf16[576,256]{1,0:T(8,128)(2,1)S(1)} %get-tuple-element.138), channel_id=1, source_target_pairs={{0,2},{4,6},{1,3},{5,7},{2,0},{6,4},{3,1},{7,5},{8,10},{12,14},{9,... | collective-permute-start | bytes 884744 | tf_op jit(solution)/shard_map/ppermute | solution.py:34
  55.3 4.4 %collective-permute-done.14.refs_1_ = bf16[296,512]{1,0:T(8,128)(2,1)S(1)} collective-permute-done((bf16[296,512]{1,0:T(8,128)(2,1)S(1)}, bf16[296,512]{1,0:T(8,128)(2,1)S(1)}, u32[]{:S(2)}, u32[]{:S(2)}) %collective-permute-start.14) | collective-permute-done | bytes 303136 | tf_op jit(solution)/shard_map/ppermute | solution.py:34
  59.7 1.5 %collective-permute-start.20 = (bf16[288,384]{1,0:T(8,128)(2,1)S(1)}, bf16[288,384]{1,0:T(8,128)(2,1)S(1)}, u32[]{:S(2)}, u32[]{:S(2)}) collective-permute-start(bf16[288,384]{1,0:T(8,128)(2,1)S(1)} %get-tuple-element.130), channel_id=1, source_target_pairs={{0,8},{4,12},{1,9},{5,13},{2,10},{6,14},{3,11},{7,15},{8,0},{12,4}... | collective-permute-start | bytes 663560 | tf_op jit(solution)/shard_map/ppermute | solution.py:34
  61.2 1.5 %collective-permute-start.21 = (bf16[288,384]{1,0:T(8,128)(2,1)S(1)}, bf16[288,384]{1,0:T(8,128)(2,1)S(1)}, u32[]{:S(2)}, u32[]{:S(2)}) collective-permute-start(bf16[288,384]{1,0:T(8,128)(2,1)S(1)} %get-tuple-element.131), channel_id=1, source_target_pairs={{0,16},{4,20},{1,17},{5,21},{2,18},{6,22},{3,19},{7,23},{8,24},{12... | collective-permute-start | bytes 663560 | tf_op jit(solution)/shard_map/ppermute | solution.py:34
  62.7 5.7 %collective-permute-done.26.arrived = bf16[576,256]{1,0:T(8,128)(2,1)S(1)} collective-permute-done((bf16[576,256]{1,0:T(8,128)(2,1)S(1)}, bf16[576,256]{1,0:T(8,128)(2,1)S(1)}, u32[]{:S(2)}, u32[]{:S(2)}) %collective-permute-start.26) | collective-permute-done | bytes 294944 | tf_op jit(solution)/shard_map/ppermute | solution.py:34
  69.5 2.0 %collective-permute-start.17 = (bf16[80,512]{1,0:T(8,128)(2,1)S(1)}, bf16[80,512]{1,0:T(8,128)(2,1)S(1)}, u32[]{:S(2)}, u32[]{:S(2)}) collective-permute-start(bf16[80,512]{1,0:T(8,128)(2,1)S(1)} %get-tuple-element.126), channel_id=1, source_target_pairs={{0,1},{4,5},{1,0},{5,4},{2,3},{6,7},{3,2},{7,6},{8,9},{12,13},{9,8... | collective-permute-start | bytes 245768 | tf_op jit(solution)/shard_map/ppermute | solution.py:34
  71.5 3.1 %collective-permute-done.27.refs_0_ = bf16[288,256]{1,0:T(8,128)(2,1)S(1)} collective-permute-done((bf16[288,256]{1,0:T(8,128)(2,1)S(1)}, bf16[288,256]{1,0:T(8,128)(2,1)S(1)}, u32[]{:S(2)}, u32[]{:S(2)}) %collective-permute-start.27) | collective-permute-done | bytes 147488 | tf_op jit(solution)/shard_map/ppermute | solution.py:34
  79.1 1.7 %collective-permute-start.24 = (bf16[72,384]{1,0:T(8,128)(2,1)S(1)}, bf16[72,384]{1,0:T(8,128)(2,1)S(1)}, u32[]{:S(2)}, u32[]{:S(2)}) collective-permute-start(bf16[72,384]{1,0:T(8,128)(2,1)S(1)} %get-tuple-element.135), channel_id=1, source_target_pairs={{0,2},{4,6},{1,3},{5,7},{2,0},{6,4},{3,1},{7,5},{8,10},{12,14},{9,... | collective-permute-start | bytes 165896 | tf_op jit(solution)/shard_map/ppermute | solution.py:34
  80.8 2.8 %collective-permute-done.18 = bf16[80,512]{1,0:T(8,128)(2,1)S(1)} collective-permute-done((bf16[80,512]{1,0:T(8,128)(2,1)S(1)}, bf16[80,512]{1,0:T(8,128)(2,1)S(1)}, u32[]{:S(2)}, u32[]{:S(2)}) %collective-permute-start.18) | collective-permute-done | bytes 81952 | tf_op jit(solution)/shard_map/ppermute | solution.py:34
  83.6 2.3 %collective-permute-start.25 = (bf16[72,384]{1,0:T(8,128)(2,1)S(1)}, bf16[72,384]{1,0:T(8,128)(2,1)S(1)}, u32[]{:S(2)}, u32[]{:S(2)}) collective-permute-start(bf16[72,384]{1,0:T(8,128)(2,1)S(1)} %get-tuple-element.136), channel_id=1, source_target_pairs={{0,3},{4,7},{1,2},{5,6},{2,1},{6,5},{3,0},{7,4},{8,11},{12,15},{9,... | collective-permute-start | bytes 165896 | tf_op jit(solution)/shard_map/ppermute | solution.py:34
  86.9 2.9 %collective-permute-done.29 = bf16[72,256]{1,0:T(8,128)(2,1)S(1)} collective-permute-done((bf16[72,256]{1,0:T(8,128)(2,1)S(1)}, bf16[72,256]{1,0:T(8,128)(2,1)S(1)}, u32[]{:S(2)}, u32[]{:S(2)}) %collective-permute-start.29) | collective-permute-done | bytes 36896 | tf_op jit(solution)/shard_map/ppermute | solution.py:34
  (73 shorter events, 19.1 us)
Async XLA Ops:
  0.6 7.7 %collective-permute-start.4 = (bf16[128,1152]{1,0:T(8,128)(2,1)}, bf16[128,1152]{1,0:T(8,128)(2,1)S(1)}, u32[]{:S(2)}, u32[]{:S(2)}) collective-permute-start(bf16[128,1152]{1,0:T(8,128)(2,1)} %refs_0_.1), channel_id=1, source_target_pairs={{0,4},{4,0},{1,5},{5,1},{2,6},{6,2},{3,7},{7,3},{8,12},{12,8},{9,1... | collective-permute-start | bytes 884744 | tf_op jit(solution)/shard_map/ppermute | solution.py:34
  1.1 8.7 %collective-permute-start.5 = (bf16[128,1152]{1,0:T(8,128)(2,1)}, bf16[128,1152]{1,0:T(8,128)(2,1)S(1)}, u32[]{:S(2)}, u32[]{:S(2)}) collective-permute-start(bf16[128,1152]{1,0:T(8,128)(2,1)} %refs_1_.1), channel_id=1, source_target_pairs={{0,4},{4,0},{1,5},{5,1},{2,6},{6,2},{3,7},{7,3},{8,12},{12,8},{9,1... | collective-permute-start | bytes 884744 | tf_op jit(solution)/shard_map/ppermute | solution.py:34
  1.2 16.8 %collective-permute-start = (bf16[128,1152]{1,0:T(8,128)(2,1)}, bf16[128,1152]{1,0:T(8,128)(2,1)S(1)}, u32[]{:S(2)}, u32[]{:S(2)}) collective-permute-start(bf16[128,1152]{1,0:T(8,128)(2,1)} %refs_0_.1), channel_id=1, source_target_pairs={{0,1},{4,5},{1,0},{5,4},{2,3},{6,7},{3,2},{7,6},{8,9},{12,13},{9,8... | collective-permute-start | bytes 884744 | tf_op jit(solution)/shard_map/ppermute | solution.py:34
  4.2 16.2 %collective-permute-start.1 = (bf16[128,1152]{1,0:T(8,128)(2,1)}, bf16[128,1152]{1,0:T(8,128)(2,1)S(1)}, u32[]{:S(2)}, u32[]{:S(2)}) collective-permute-start(bf16[128,1152]{1,0:T(8,128)(2,1)} %refs_0_.1), channel_id=1, source_target_pairs={{0,2},{4,6},{1,3},{5,7},{2,0},{6,4},{3,1},{7,5},{8,10},{12,14},{9,... | collective-permute-start | bytes 884744 | tf_op jit(solution)/shard_map/ppermute | solution.py:34
  6.8 13.6 %collective-permute-start.2 = (bf16[128,1152]{1,0:T(8,128)(2,1)}, bf16[128,1152]{1,0:T(8,128)(2,1)S(1)}, u32[]{:S(2)}, u32[]{:S(2)}) collective-permute-start(bf16[128,1152]{1,0:T(8,128)(2,1)} %refs_1_.1), channel_id=1, source_target_pairs={{0,8},{4,12},{1,9},{5,13},{2,10},{6,14},{3,11},{7,15},{8,0},{12,4}... | collective-permute-start | bytes 884744 | tf_op jit(solution)/shard_map/ppermute | solution.py:34
  8.3 12.1 %collective-permute-start.3 = (bf16[128,1152]{1,0:T(8,128)(2,1)}, bf16[128,1152]{1,0:T(8,128)(2,1)S(1)}, u32[]{:S(2)}, u32[]{:S(2)}) collective-permute-start(bf16[128,1152]{1,0:T(8,128)(2,1)} %refs_1_.1), channel_id=1, source_target_pairs={{0,16},{4,20},{1,17},{5,21},{2,18},{6,22},{3,19},{7,23},{8,24},{12... | collective-permute-start | bytes 884744 | tf_op jit(solution)/shard_map/ppermute | solution.py:34
  21.0 5.4 %collective-permute-start.8 = (bf16[128,1152]{1,0:T(8,128)(2,1)S(1)}, bf16[128,1152]{1,0:T(8,128)(2,1)S(1)}, u32[]{:S(2)}, u32[]{:S(2)}) collective-permute-start(bf16[128,1152]{1,0:T(8,128)(2,1)S(1)} %collective-permute-done.refs_0_), channel_id=1, source_target_pairs={{0,4},{4,0},{1,5},{5,1},{2,6},{6,2},{3,7},{7,3},{8,12},{12,8},{9,1... | collective-permute-start | bytes 884744 | tf_op jit(solution)/shard_map/ppermute | solution.py:34
  21.5 9.0 %collective-permute-start.6 = (bf16[128,1152]{1,0:T(8,128)(2,1)S(1)}, bf16[128,1152]{1,0:T(8,128)(2,1)S(1)}, u32[]{:S(2)}, u32[]{:S(2)}) collective-permute-start(bf16[128,1152]{1,0:T(8,128)(2,1)S(1)} %collective-permute-done.1.refs_0_), channel_id=1, source_target_pairs={{0,1},{4,5},{1,0},{5,4},{2,3},{6,7},{3,2},{7,6},{8,9},{12,13},{9,8... | collective-permute-start | bytes 884744 | tf_op jit(solution)/shard_map/ppermute | solution.py:34
  22.0 9.1 %collective-permute-start.7 = (bf16[128,1152]{1,0:T(8,128)(2,1)S(1)}, bf16[128,1152]{1,0:T(8,128)(2,1)S(1)}, u32[]{:S(2)}, u32[]{:S(2)}) collective-permute-start(bf16[128,1152]{1,0:T(8,128)(2,1)S(1)} %collective-permute-done.3.refs_1_), channel_id=1, source_target_pairs={{0,8},{4,12},{1,9},{5,13},{2,10},{6,14},{3,11},{7,15},{8,0},{12,4}... | collective-permute-start | bytes 884744 | tf_op jit(solution)/shard_map/ppermute | solution.py:34
  49.6 10.1 %collective-permute-start.14 = (bf16[296,512]{1,0:T(8,128)(2,1)S(1)}, bf16[296,512]{1,0:T(8,128)(2,1)S(1)}, u32[]{:S(2)}, u32[]{:S(2)}) collective-permute-start(bf16[296,512]{1,0:T(8,128)(2,1)S(1)} %get-tuple-element.120), channel_id=1, source_target_pairs={{0,8},{4,12},{1,9},{5,13},{2,10},{6,14},{3,11},{7,15},{8,0},{12,4}... | collective-permute-start | bytes 909320 | tf_op jit(solution)/shard_map/ppermute | solution.py:34
  51.2 17.4 %collective-permute-start.15 = (bf16[296,512]{1,0:T(8,128)(2,1)S(1)}, bf16[296,512]{1,0:T(8,128)(2,1)S(1)}, u32[]{:S(2)}, u32[]{:S(2)}) collective-permute-start(bf16[296,512]{1,0:T(8,128)(2,1)S(1)} %get-tuple-element.122), channel_id=1, source_target_pairs={{0,16},{4,20},{1,17},{5,21},{2,18},{6,22},{3,19},{7,23},{8,24},{12... | collective-permute-start | bytes 909320 | tf_op jit(solution)/shard_map/ppermute | solution.py:34
  52.7 15.7 %collective-permute-start.26 = (bf16[576,256]{1,0:T(8,128)(2,1)S(1)}, bf16[576,256]{1,0:T(8,128)(2,1)S(1)}, u32[]{:S(2)}, u32[]{:S(2)}) collective-permute-start(bf16[576,256]{1,0:T(8,128)(2,1)S(1)} %get-tuple-element.138), channel_id=1, source_target_pairs={{0,2},{4,6},{1,3},{5,7},{2,0},{6,4},{3,1},{7,5},{8,10},{12,14},{9,... | collective-permute-start | bytes 884744 | tf_op jit(solution)/shard_map/ppermute | solution.py:34
  54.8 14.3 %collective-permute-start.16 = (bf16[296,512]{1,0:T(8,128)(2,1)S(1)}, bf16[296,512]{1,0:T(8,128)(2,1)S(1)}, u32[]{:S(2)}, u32[]{:S(2)}) collective-permute-start(bf16[296,512]{1,0:T(8,128)(2,1)S(1)} %get-tuple-element.123), channel_id=1, source_target_pairs={{0,24},{4,28},{1,25},{5,29},{2,26},{6,30},{3,27},{7,31},{8,16},{12... | collective-permute-start | bytes 909320 | tf_op jit(solution)/shard_map/ppermute | solution.py:34
  59.7 16.1 %collective-permute-start.20 = (bf16[288,384]{1,0:T(8,128)(2,1)S(1)}, bf16[288,384]{1,0:T(8,128)(2,1)S(1)}, u32[]{:S(2)}, u32[]{:S(2)}) collective-permute-start(bf16[288,384]{1,0:T(8,128)(2,1)S(1)} %get-tuple-element.130), channel_id=1, source_target_pairs={{0,8},{4,12},{1,9},{5,13},{2,10},{6,14},{3,11},{7,15},{8,0},{12,4}... | collective-permute-start | bytes 663560 | tf_op jit(solution)/shard_map/ppermute | solution.py:34
  61.2 16.1 %collective-permute-start.21 = (bf16[288,384]{1,0:T(8,128)(2,1)S(1)}, bf16[288,384]{1,0:T(8,128)(2,1)S(1)}, u32[]{:S(2)}, u32[]{:S(2)}) collective-permute-start(bf16[288,384]{1,0:T(8,128)(2,1)S(1)} %get-tuple-element.131), channel_id=1, source_target_pairs={{0,16},{4,20},{1,17},{5,21},{2,18},{6,22},{3,19},{7,23},{8,24},{12... | collective-permute-start | bytes 663560 | tf_op jit(solution)/shard_map/ppermute | solution.py:34
  68.4 6.1 %collective-permute-start.27 = (bf16[288,256]{1,0:T(8,128)(2,1)S(1)}, bf16[288,256]{1,0:T(8,128)(2,1)S(1)}, u32[]{:S(2)}, u32[]{:S(2)}) collective-permute-start(bf16[288,256]{1,0:T(8,128)(2,1)S(1)} %get-tuple-element.140), channel_id=1, source_target_pairs={{0,1},{4,5},{1,0},{5,4},{2,3},{6,7},{3,2},{7,6},{8,9},{12,13},{9,8... | collective-permute-start | bytes 442376 | tf_op jit(solution)/shard_map/ppermute | solution.py:34
  68.5 9.2 %collective-permute-start.22 = (bf16[288,384]{1,0:T(8,128)(2,1)S(1)}, bf16[288,384]{1,0:T(8,128)(2,1)S(1)}, u32[]{:S(2)}, u32[]{:S(2)}) collective-permute-start(bf16[288,384]{1,0:T(8,128)(2,1)S(1)} %get-tuple-element.132), channel_id=1, source_target_pairs={{0,24},{4,28},{1,25},{5,29},{2,26},{6,30},{3,27},{7,31},{8,16},{12... | collective-permute-start | bytes 663560 | tf_op jit(solution)/shard_map/ppermute | solution.py:34
  69.5 9.6 %collective-permute-start.17 = (bf16[80,512]{1,0:T(8,128)(2,1)S(1)}, bf16[80,512]{1,0:T(8,128)(2,1)S(1)}, u32[]{:S(2)}, u32[]{:S(2)}) collective-permute-start(bf16[80,512]{1,0:T(8,128)(2,1)S(1)} %get-tuple-element.126), channel_id=1, source_target_pairs={{0,1},{4,5},{1,0},{5,4},{2,3},{6,7},{3,2},{7,6},{8,9},{12,13},{9,8... | collective-permute-start | bytes 245768 | tf_op jit(solution)/shard_map/ppermute | solution.py:34
  74.6 9.0 %collective-permute-start.18 = (bf16[80,512]{1,0:T(8,128)(2,1)S(1)}, bf16[80,512]{1,0:T(8,128)(2,1)S(1)}, u32[]{:S(2)}, u32[]{:S(2)}) collective-permute-start(bf16[80,512]{1,0:T(8,128)(2,1)S(1)} %get-tuple-element.127), channel_id=1, source_target_pairs={{0,2},{4,6},{1,3},{5,7},{2,0},{6,4},{3,1},{7,5},{8,10},{12,14},{9,... | collective-permute-start | bytes 245768 | tf_op jit(solution)/shard_map/ppermute | solution.py:34
  75.8 10.1 %collective-permute-start.19 = (bf16[80,512]{1,0:T(8,128)(2,1)S(1)}, bf16[80,512]{1,0:T(8,128)(2,1)S(1)}, u32[]{:S(2)}, u32[]{:S(2)}) collective-permute-start(bf16[80,512]{1,0:T(8,128)(2,1)S(1)} %get-tuple-element.128), channel_id=1, source_target_pairs={{0,3},{4,7},{1,2},{5,6},{2,1},{6,5},{3,0},{7,4},{8,11},{12,15},{9,... | collective-permute-start | bytes 245768 | tf_op jit(solution)/shard_map/ppermute | solution.py:34
  77.3 8.6 %collective-permute-start.28 = (bf16[72,256]{1,0:T(8,128)(2,1)S(1)}, bf16[72,256]{1,0:T(8,128)(2,1)S(1)}, u32[]{:S(2)}, u32[]{:S(2)}) collective-permute-start(bf16[72,256]{1,0:T(8,128)(2,1)S(1)} %get-tuple-element.142), channel_id=1, source_target_pairs={{0,8},{4,12},{1,9},{5,13},{2,10},{6,14},{3,11},{7,15},{8,0},{12,4}... | collective-permute-start | bytes 110600 | tf_op jit(solution)/shard_map/ppermute | solution.py:34
  78.0 12.8 %collective-permute-start.23 = (bf16[72,384]{1,0:T(8,128)(2,1)S(1)}, bf16[72,384]{1,0:T(8,128)(2,1)S(1)}, u32[]{:S(2)}, u32[]{:S(2)}) collective-permute-start(bf16[72,384]{1,0:T(8,128)(2,1)S(1)} %get-tuple-element.134), channel_id=1, source_target_pairs={{0,1},{4,5},{1,0},{5,4},{2,3},{6,7},{3,2},{7,6},{8,9},{12,13},{9,8... | collective-permute-start | bytes 165896 | tf_op jit(solution)/shard_map/ppermute | solution.py:34
  79.1 11.7 %collective-permute-start.24 = (bf16[72,384]{1,0:T(8,128)(2,1)S(1)}, bf16[72,384]{1,0:T(8,128)(2,1)S(1)}, u32[]{:S(2)}, u32[]{:S(2)}) collective-permute-start(bf16[72,384]{1,0:T(8,128)(2,1)S(1)} %get-tuple-element.135), channel_id=1, source_target_pairs={{0,2},{4,6},{1,3},{5,7},{2,0},{6,4},{3,1},{7,5},{8,10},{12,14},{9,... | collective-permute-start | bytes 165896 | tf_op jit(solution)/shard_map/ppermute | solution.py:34
  83.6 7.3 %collective-permute-start.25 = (bf16[72,384]{1,0:T(8,128)(2,1)S(1)}, bf16[72,384]{1,0:T(8,128)(2,1)S(1)}, u32[]{:S(2)}, u32[]{:S(2)}) collective-permute-start(bf16[72,384]{1,0:T(8,128)(2,1)S(1)} %get-tuple-element.136), channel_id=1, source_target_pairs={{0,3},{4,7},{1,2},{5,6},{2,1},{6,5},{3,0},{7,4},{8,11},{12,15},{9,... | collective-permute-start | bytes 165896 | tf_op jit(solution)/shard_map/ppermute | solution.py:34
  (14 other events, 37.9 us)

commit v6 on v5

--- a/solution.py
+++ b/solution.py
@@ -38,6 +38,9 @@
 
     def along_row(self, value, t):
         return self.send(value, lambda r, c, core: (r, c ^ t, core))
+
+    def exchange(self, value, row_bits, column_bits):
+        return self.send(value, lambda r, c, core: (r ^ row_bits, c ^ column_bits, core))
 
     def sibling(self, value):
         return self.send(value, lambda r, c, core: (r, c, 1 - core))
@@ -149,15 +152,15 @@
     return sum(total[:, j : j + 128] for j in range(0, total.shape[1], 128))
 
 
-def block_kernel(side, mp_size, groups, scalars, image_proj, text_proj, *refs):
+def block_kernel(side, mp_size, scalars, image_proj, text_proj, *refs):
     last_shards, refs = refs[:4], refs[4:]
     own_chunks, refs = refs[: side - 1], refs[side - 1 :]
     own_units, refs = refs[: side - 1], refs[side - 1 :]
     own_inverses, refs = refs[: side - 1], refs[side - 1 :]
     other_halves, refs = refs[: side - 1], refs[side - 1 :]
-    firsts, refs = refs[: side * len(groups)], refs[side * len(groups) :]
-    own_late, late_message, refs = refs[0], refs[1], refs[2:]
-    stats, projs, last, feats, units, inverses, other_half, dy, grad, piece, sems = refs
+    orders = part_orders(side)
+    results, refs = refs[: 2 * len(orders)], refs[2 * len(orders) :]
+    stats, projs, last, feats, units, inverses, other_half, dy, grad, pieces, moving, sems = refs
     rows, width = dy.shape
     chunk_rows = rows // side
     rest = rows - chunk_rows
@@ -236,38 +239,54 @@
     sums = stats[0:1, :]
     stats[...] = jnp.broadcast_to(sums, stats.shape)
     chunk = width // side
-    for g, (begin, end) in enumerate(groups):
-        for t in range(side):
-            out = firsts[side * g + t]
-            first = pl.multiple_of(jnp.bitwise_xor(unit_row, t) * chunk, chunk)
-            out[:chunk, :] = grad[pl.ds(first, chunk), begin:end].astype(out.dtype)
-            if t and g == 0:
-                out[chunk:, :] = stat_rows(sums, end - begin).astype(BF16)
-    first_width = groups[-1][1]
     out_rows = chunk // (2 * side)
-    for column in range(side):
-        for i in range(side):
-            for core in range(2):
-                source = i * chunk + shard_of(column, core, mp_size) * out_rows
-                target = (2 * i + core) * out_rows
-                piece[target : target + out_rows, :] = grad[source : source + out_rows, first_width:]
-        half = side // 2 * chunk
-        for t in range(side):
-            target = own_late if t < side // 2 else late_message
-            place = pl.ds(t * chunk % half, chunk)
-            store_for(column, unit_column, piece, {t: target.at[place, :]})
+    piece_rows = pieces.shape[0] // side**2
+    for unit in range(side**2):
+        row, column = divmod(unit, side)
+        for core in range(2):
+            source = row * chunk + shard_of(column, core, mp_size) * out_rows
+            target = unit * piece_rows + core * out_rows
+            pieces[target : target + out_rows, :] = grad[source : source + out_rows, :]
+        if piece_rows > 2 * out_rows:
+            target = unit * piece_rows + 2 * out_rows
+            pieces[target : (unit + 1) * piece_rows, :] = jnp.zeros(
+                (piece_rows - 2 * out_rows, width), F32
+            )
+    half = side**2 // 2
+    part_width = width // len(orders)
+    moving[half * piece_rows :, :] = stat_rows(sums, part_width)
+    for g, order in enumerate(orders):
+        own, message = results[2 * g : 2 * g + 2]
+        columns = slice(g * part_width, (g + 1) * part_width)
+        for p in range(2 * half):
+            row, column = relative_unit(order, p)
+            unit = jnp.bitwise_xor(unit_row, row) * side + jnp.bitwise_xor(unit_column, column)
+            block = pieces[pl.ds(pl.multiple_of(unit * piece_rows, 8), piece_rows), columns]
+            target = p % half * piece_rows
+            (own if p < half else moving)[target : target + piece_rows, :] = block
+        message[...] = moving[: message.shape[0], :].astype(BF16)
+
+
+def part_orders(side):
+    bits = [1 << i for i in range(side.bit_length() - 1)]
+    rows, columns = [(b, 0) for b in bits], [(0, b) for b in bits]
+    return [
+        rows + columns[::-1],
+        [rows[-1], columns[0]] + rows[:-1] + columns[1:],
+        [columns[0]] + rows + columns[1:],
+    ]
+
+
+def relative_unit(order, position):
+    row = column = 0
+    for i, step in enumerate(reversed(order)):
+        if position >> i & 1:
+            row, column = row | step[0], column | step[1]
+    return row, column
 
 
 def shard_of(column, core, mp_size):
     return column // mp_size * 2 * mp_size + core * mp_size + column % mp_size
-
-
-def store_for(index, own_index, piece, outs):
-    for t, out in outs.items():
-
-        @pl.when(jnp.bitwise_xor(own_index, t) == index)
-        def _():
-            out[...] = piece[...].astype(out.dtype)
 
 
 def stat_rows(sums, width):
@@ -281,34 +300,32 @@
     return parts
 
 
-def block_grads(layout, groups, scalars, image_proj, text_proj, last_shards, projected):
+def block_grads(layout, scalars, image_proj, text_proj, last_shards, projected):
     side = layout.side
     chunk_rows, width = projected[0][0].shape
     rows = side * chunk_rows
-    chunk = width // side
     anywhere = pl.BlockSpec(memory_space=pl.ANY)
     vmem = pl.BlockSpec(memory_space=pltpu.VMEM)
-    first_width = groups[-1][1]
-    late_width = width - first_width
     operands = [image_proj, text_proj, *last_shards]
     operands += [x for column in zip(*projected) for x in column]
+    parts = len(part_orders(side))
+    part_width = width // parts
+    piece_rows = (width // layout.units + 7) // 8 * 8
+    half_rows = layout.units // 2 * piece_rows
     out_shape = []
-    for begin, end in groups:
-        out_shape.append(jax.ShapeDtypeStruct((chunk, end - begin), F32))
-        message = jax.ShapeDtypeStruct((chunk if begin else chunk + 8, end - begin), BF16)
-        out_shape += [message] * (side - 1)
-    needed = 4 * width * width + 12 * rows * width + 4 * chunk_rows * width
-    needed += 4 * width * (width + late_width) + 24 * chunk_rows * rows + 7 * 1024 * 1024
+    for g in range(parts):
+        out_shape.append(jax.ShapeDtypeStruct((half_rows, part_width), F32))
+        out_shape.append(jax.ShapeDtypeStruct((half_rows if g else half_rows + 8, part_width), BF16))
+    out_shape.append(jax.ShapeDtypeStruct((8, part_width), F32))
+    needed = 6 * width * width + 14 * rows * width + 16 * half_rows * width
+    needed += 12 * chunk_rows * rows + 2 * 1024 * 1024
     return pl.pallas_call(
-        functools.partial(block_kernel, side, layout.mp, groups),
-        out_shape=out_shape
-        + [jax.ShapeDtypeStruct((width // 2, late_width), F32)]
-        + [jax.ShapeDtypeStruct((width // 2, late_width), BF16)]
-        + [jax.ShapeDtypeStruct((8, 384), F32)],
+        functools.partial(block_kernel, side, layout.mp),
+        out_shape=out_shape,
         in_specs=[pl.BlockSpec(memory_space=pltpu.SMEM)]
         + [pl.BlockSpec(memory_space=pltpu.HBM)] * 2
         + [anywhere] * (len(operands) - 2),
-        out_specs=[vmem] * (len(out_shape) + 3),
+        out_specs=[vmem] * len(out_shape),
         scratch_shapes=[
             pltpu.VMEM((2, width, width), BF16),
             pltpu.VMEM((2, chunk_rows, width), BF16),
@@ -318,7 +335,8 @@
             pltpu.VMEM((rows, width), BF16),
             pltpu.VMEM((rows, width), BF16),
             pltpu.VMEM((width, width), F32),
-            pltpu.VMEM((chunk, late_width), F32),
+            pltpu.VMEM((2 * half_rows, width), F32),
+            pltpu.VMEM((half_rows + 8, part_width), F32),
             pltpu.SemaphoreType.DMA((len(operands),)),
         ],
         compiler_params=pltpu.CompilerParams(vmem_limit_bytes=min(needed, 60 * 1024 * 1024)),
@@ -331,104 +349,39 @@
     )(scalars, *operands)
 
 
-def arrived_sum(own, arrived, rows):
-    return tree_sum([own[:rows, :]] + [x[:rows, :].astype(F32) for x in arrived])
-
-
-def first_kernel(side, mp_size, has_stats, own, *refs):
-    own_stats, refs = (refs[0], refs[1:]) if has_stats else (None, refs)
-    arrived, outs, refs = refs[: side - 1], refs[side - 1 : 2 * side - 1], refs[2 * side - 1 :]
-    total, piece = refs[-2:]
-    chunk, width = own.shape
-    out_rows = chunk // (2 * side)
-    total[...] = arrived_sum(own, arrived, chunk)
-    if piece.shape[0] > 2 * out_rows:
-        piece[2 * out_rows :, :] = jnp.zeros((piece.shape[0] - 2 * out_rows, width), F32)
-    if has_stats:
-        parts = [x[chunk:, :384].astype(F32) for x in arrived]
-        sums = tree_sum([own_stats[0:1, :]] + [x[0:1] + x[1:2] + x[2:3] for x in parts])
-        refs[0][...] = jnp.broadcast_to(sums, refs[0].shape)
-        piece[piece.shape[0] - 8 :, :] = stat_rows(sums, width)
-    dp_index, mp_index = lax.axis_index("dp"), lax.axis_index("mp")
-    unit_column = lax.rem(dp_index // 2 * mp_size + mp_index, side)
-    for column in range(side):
-        for core in range(2):
-            source = shard_of(column, core, mp_size) * out_rows
-            piece[core * out_rows : (core + 1) * out_rows, :] = total[source : source + out_rows, :]
-        store_for(column, unit_column, piece, dict(enumerate(outs)))
-
-
-def first_pieces(layout, own, own_stats, arrived):
-    side = layout.side
-    chunk, width = own.shape
-    has_stats = own_stats is not None
-    rows = (2 * (chunk // (2 * side)) + 7) // 8 * 8 + (8 if has_stats else 0)
+def halve_kernel(own, arrived, *refs):
+    rows, half = own.shape[0], own.shape[0] // 2
+    total = arrived[...].astype(F32)
+    keep, message = refs[-2], refs[-1]
+    moved = own[half:, :] + total[half:rows, :]
+    keep[...] = own[:half, :] + total[:half, :]
+    if len(refs) > 2:
+        own_stats, stats = refs[0], refs[1]
+        parts = total[rows:, :]
+        sums = own_stats[0:1, :] + (parts[0:1, :] + parts[1:2, :] + parts[2:3, :])
+        stats[...] = jnp.broadcast_to(sums, stats.shape)
+        moved = jnp.concatenate([moved, stat_rows(sums, own.shape[1])], axis=0)
+    message[...] = moved.astype(BF16)
+
+
+def halve(own, arrived, *own_stats):
+    rows, width = own.shape
+    half = rows // 2
     vmem = pl.BlockSpec(memory_space=pltpu.VMEM)
-    out_shape = [jax.ShapeDtypeStruct((rows, width), F32)]
-    out_shape += [jax.ShapeDtypeStruct((rows, width), BF16)] * (side - 1)
-    operands = [own, *([own_stats] if has_stats else []), *arrived]
-    if has_stats:
-        out_shape.append(jax.ShapeDtypeStruct((8, 384), F32))
-    return pl.pallas_call(
-        functools.partial(first_kernel, side, layout.mp, has_stats),
-        out_shape=out_shape,
-        in_specs=[vmem] * len(operands),
-        out_specs=[vmem] * len(out_shape),
-        scratch_shapes=[pltpu.VMEM((chunk, width), F32), pltpu.VMEM((rows, width), F32)],
-        compiler_params=pltpu.CompilerParams(vmem_limit_bytes=12 * 1024 * 1024),
-        name="first",
-    )(*operands)
-
-
-def halve_kernel(own, arrived, keep, message):
-    half = keep.shape[0]
-    keep[...] = own[:half, :] + arrived[:half, :].astype(F32)
-    message[...] = (own[half:, :] + arrived[half:, :].astype(F32)).astype(BF16)
-
-
-def halve(own, arrived):
-    rows, width = own.shape
-    vmem = pl.BlockSpec(memory_space=pltpu.VMEM)
+    stats = [jax.ShapeDtypeStruct(x.shape, F32) for x in own_stats]
+    out_shape = [
+        *stats,
+        jax.ShapeDtypeStruct((half, width), F32),
+        jax.ShapeDtypeStruct((half + 8 * len(stats), width), BF16),
+    ]
     return pl.pallas_call(
         halve_kernel,
-        out_shape=[
-            jax.ShapeDtypeStruct((rows // 2, width), F32),
-            jax.ShapeDtypeStruct((rows // 2, width), BF16),
-        ],
-        in_specs=[vmem] * 2,
-        out_specs=[vmem] * 2,
+        out_shape=out_shape,
+        in_specs=[vmem] * (2 + len(stats)),
+        out_specs=[vmem] * len(out_shape),
         compiler_params=pltpu.CompilerParams(vmem_limit_bytes=12 * 1024 * 1024),
         name="halve",
-    )(own, arrived)
-
-
-def late_kernel(side, mp_size, own, *refs):
-    arrived, outs, total = refs[:1], refs[1:-1], refs[-1]
-    chunk = own.shape[0]
-    total[...] = arrived_sum(own, arrived, chunk)
-    dp_index, mp_index = lax.axis_index("dp"), lax.axis_index("mp")
-    unit_row = (dp_index // 2 * mp_size + mp_index) // side
-    rows = chunk // side
-    for row in range(side):
-        piece = total.at[row * rows : (row + 1) * rows, :]
-        store_for(row, unit_row, piece, dict(enumerate(outs)))
-
-
-def late_pieces(layout, own, arrived):
-    side = layout.side
-    chunk, width = own.shape
-    rows = chunk // side
-    vmem = pl.BlockSpec(memory_space=pltpu.VMEM)
-    return pl.pallas_call(
-        functools.partial(late_kernel, side, layout.mp),
-        out_shape=[jax.ShapeDtypeStruct((rows, width), F32)]
-        + [jax.ShapeDtypeStruct((rows, width), BF16)] * (side - 1),
-        in_specs=[vmem] * 2,
-        out_specs=[vmem] * side,
-        scratch_shapes=[pltpu.VMEM((chunk, width), F32)],
-        compiler_params=pltpu.CompilerParams(vmem_limit_bytes=12 * 1024 * 1024),
-        name="late",
-    )(own, arrived)
+    )(own, arrived, *own_stats)
 
 
 def per_device(layout, image_feats, text_feats, image_proj, text_proj, log_scale, logit_bias):
@@ -473,45 +426,33 @@
         (images[last], texts[last], projected)
     )
     swap(last)
-    groups = ((0, 512), (512, 896))
     results = block_grads(
         layout,
-        groups,
         scalars,
         image_proj,
         text_proj,
         [images[last], texts[last], *swapped[last]],
         [projected[t] for t in range(last)],
     )
-    count = side * len(groups)
-    firsts = [list(results[g : g + side]) for g in range(0, count, side)]
-    late, message, stats = results[count:]
-
-    bit = side // 2
-    arrived = layout.along_row(message, bit)
-    for g, group in enumerate(firsts):
-        if g:
-            group[1:], firsts[g - 1][1] = lax.optimization_barrier((group[1:], firsts[g - 1][1]))
-        group[1:] = [layout.along_column(group[t], t) for t in range(1, side)]
-    while bit > 1:
-        late, message = halve(late, arrived)
-        bit //= 2
-        arrived = layout.along_row(message, bit)
-
-    for g, group in enumerate(firsts):
-        own_stats = None if g else stats
-        pieces = list(first_pieces(layout, group[0], own_stats, group[1:]))
-        if not g:
-            stats = pieces.pop()
-        group[:] = [pieces[0]] + [layout.along_row(pieces[t], t) for t in range(1, side)]
-    lates = list(late_pieces(layout, late, arrived))
-    lates[1:] = [layout.along_column(lates[t], t) for t in range(1, side)]
-    firsts, lates = lax.optimization_barrier((firsts, lates))
+    orders = part_orders(side)
+    owns, messages = list(results[0:-1:2]), list(results[1:-1:2])
+    stats = [results[-1]]
+
+    steps = len(orders[0])
+    for step in range(steps):
+        arrived = [
+            layout.exchange(message, *order[step]) for message, order in zip(messages, orders)
+        ]
+        if step + 1 < steps:
+            for g in range(len(orders)):
+                *some, owns[g], messages[g] = halve(owns[g], arrived[g], *([] if g else stats))
+                stats = some if g == 0 else stats
     last_rows = 2 * out_rows
-    sums = [tree_sum([x[:last_rows].astype(F32) for x in group]) for group in [*firsts, lates]]
-    total = jnp.concatenate(sums, axis=1)
-    parts = [x[-8:-5, :384].astype(F32) for x in firsts[0][1:]]
-    stat_total = tree_sum([stats[0]] + [x[0] + x[1] + x[2] for x in parts])
+    total = jnp.concatenate(
+        [own[:last_rows] + x[:last_rows].astype(F32) for own, x in zip(owns, arrived)], axis=1
+    )
+    parts = arrived[0][owns[0].shape[0] :].astype(F32)
+    stat_total = stats[0][0] + (parts[0] + parts[1] + parts[2])
 
     upper, lower = total[:out_rows], total[out_rows:]
     keep, give = jnp.where(is_image, upper, lower), jnp.where(is_image, lower, upper)

time: 93.9 us -> 86.5 us (0.921)
  starting transfers between devices: 33.7 us -> 29.7 us
  waiting for transfers between devices: 24.9 us -> 22.2 us
    ppermute x33 -> x28, starting transfers between devices: 33.7 us -> 29.7 us  [send(): return lax.ppermute(value, AXES, pairs)]
    ppermute x33 -> x28, waiting for transfers between devices: 24.9 us -> 22.2 us  [send(): return lax.ppermute(value, AXES, pairs)]
    pallas_call x5 -> x10, Pallas kernels: 17.3 us -> 16.7 us  [the longest x1 16.2 us: block_grads(): pl.pallas_call(functools.partial(block_kernel, side, layout.mp), out_shap...]
  transfers between devices with their start and end apart: 33 -> 28, of which waited for: 12 -> 14; matrix products, arithmetic and copies ran while one was open for 1% -> 1% of each run, Pallas kernels for 10% -> 10%
where the time goes in v6:
time: 86.5 us; the launch traced here: 86.2 us
  starting transfers between devices  29.7 us (34%)
  Pallas kernels  25 us (29%)
  waiting for transfers between devices  22.2 us (26%)
  local copies, waits for them, and re-layouts  6.02 us (7%)
  between operations  2.13 us (2%)
  other arithmetic  1.09 us (1%)
    ppermute x28, starting transfers between devices, send(): return lax.ppermute(value, AXES, pairs)  29.7 us
    ppermute x28, waiting for transfers between devices, send(): return lax.ppermute(value, AXES, pairs)  22.2 us
    pallas_call x1, Pallas kernels, block_grads(): pl.pallas_call(functools.partial(block_kernel, side, layout.mp), out_shap...  16.2 us
    pallas_call x3, Pallas kernels, project_chunk(): pl.pallas_call(project_kernel, out_shape=[jax.ShapeDtypeStruct((rows, wid...  8.31 us
    unnamed x10, local copies, waits for them, and re-layouts  5.43 us
  transfers between devices with their start and end apart: 28, of which 14 were waited for; matrix products, arithmetic and copies ran while one was open for 1% of the time, Pallas kernels for 10%

profile of v6, /device:TPU:0, one launch (start us, length us, event | category | flops | bytes accessed | tf_op | source)
XLA Modules:
  0.0 86.2 jit_solution(13912137281880603818)
XLA Ops:
  1.2 3.0 %collective-permute-start = (bf16[128,1152]{1,0:T(8,128)(2,1)}, bf16[128,1152]{1,0:T(8,128)(2,1)S(1)}, u32[]{:S(2)}, u32[]{:S(2)}) collective-permute-start(bf16[128,1152]{1,0:T(8,128)(2,1)} %refs_0_.1), channel_id=1, source_target_pairs={{0,1},{4,5},{1,0},{5,4},{2,3},{6,7},{3,2},{7,6},{8,9},{12,13},{9,8... | collective-permute-start | bytes 884744 | tf_op jit(solution)/shard_map/ppermute | solution.py:34
  4.2 2.6 %collective-permute-start.1 = (bf16[128,1152]{1,0:T(8,128)(2,1)}, bf16[128,1152]{1,0:T(8,128)(2,1)S(1)}, u32[]{:S(2)}, u32[]{:S(2)}) collective-permute-start(bf16[128,1152]{1,0:T(8,128)(2,1)} %refs_0_.1), channel_id=1, source_target_pairs={{0,2},{4,6},{1,3},{5,7},{2,0},{6,4},{3,1},{7,5},{8,10},{12,14},{9,... | collective-permute-start | bytes 884744 | tf_op jit(solution)/shard_map/ppermute | solution.py:34
  6.8 1.5 %collective-permute-start.2 = (bf16[128,1152]{1,0:T(8,128)(2,1)}, bf16[128,1152]{1,0:T(8,128)(2,1)S(1)}, u32[]{:S(2)}, u32[]{:S(2)}) collective-permute-start(bf16[128,1152]{1,0:T(8,128)(2,1)} %refs_1_.1), channel_id=1, source_target_pairs={{0,8},{4,12},{1,9},{5,13},{2,10},{6,14},{3,11},{7,15},{8,0},{12,4}... | collective-permute-start | bytes 884744 | tf_op jit(solution)/shard_map/ppermute | solution.py:34
  8.3 1.5 %collective-permute-start.3 = (bf16[128,1152]{1,0:T(8,128)(2,1)}, bf16[128,1152]{1,0:T(8,128)(2,1)S(1)}, u32[]{:S(2)}, u32[]{:S(2)}) collective-permute-start(bf16[128,1152]{1,0:T(8,128)(2,1)} %refs_1_.1), channel_id=1, source_target_pairs={{0,16},{4,20},{1,17},{5,21},{2,18},{6,22},{3,19},{7,23},{8,24},{12... | collective-permute-start | bytes 884744 | tf_op jit(solution)/shard_map/ppermute | solution.py:34
  9.8 1.7 %copy-done = bf16[1152,1152]{1,0:T(8,128)(2,1)S(1)} copy-done((bf16[1152,1152]{1,0:T(8,128)(2,1)S(1)}, bf16[1152,1152]{1,0:T(8,128)(2,1)}, u32[]{:S(2)}) %copy-start) | copy-done | bytes 2654232
  11.6 1.7 %copy-done.2 = bf16[1152,1152]{1,0:T(8,128)(2,1)S(1)} copy-done((bf16[1152,1152]{1,0:T(8,128)(2,1)S(1)}, bf16[1152,1152]{1,0:T(8,128)(2,1)}, u32[]{:S(2)}) %copy-start.2) | copy-done | bytes 2654232
  15.3 2.8 %project.3 = (bf16[256,1152]{1,0:T(8,128)(2,1)S(1)}, f32[256,1152]{1,0:T(8,128)S(1)}, f32[256,128]{1,0:T(8,128)S(1)}, bf16[256,1152]{1,0:T(8,128)(2,1)S(1)}) custom-call(bf16[1152,1152]{1,0:T(8,128)(2,1)S(1)} %copy-done, bf16[1152,1152]{1,0:T(8,128)(2,1)S(1)} %copy-done.2, bf16[128,1152]{1,0:T(8,128)(2,1)S(1)} %copy-done.3, bf16[128,1152]{1,0:T(8,128)(2,1)S(1)} %copy-done.4, ...), custom_call_target="tpu_custom_call" | custom-call | flops 1358954496 | bytes 8847360 | tf_op jit(solution)/shard_map/project/pallas_call | solution.py:107
  18.0 2.4 %collective-permute-done.1.refs_0_ = bf16[128,1152]{1,0:T(8,128)(2,1)S(1)} collective-permute-done((bf16[128,1152]{1,0:T(8,128)(2,1)}, bf16[128,1152]{1,0:T(8,128)(2,1)S(1)}, u32[]{:S(2)}, u32[]{:S(2)}) %collective-permute-start.1) | collective-permute-done | bytes 294944 | tf_op jit(solution)/shard_map/ppermute | solution.py:34
  22.0 1.5 %collective-permute-start.7 = (bf16[128,1152]{1,0:T(8,128)(2,1)S(1)}, bf16[128,1152]{1,0:T(8,128)(2,1)S(1)}, u32[]{:S(2)}, u32[]{:S(2)}) collective-permute-start(bf16[128,1152]{1,0:T(8,128)(2,1)S(1)} %collective-permute-done.3.refs_1_), channel_id=1, source_target_pairs={{0,8},{4,12},{1,9},{5,13},{2,10},{6,14},{3,11},{7,15},{8,0},{12,4}... | collective-permute-start | bytes 884744 | tf_op jit(solution)/shard_map/ppermute | solution.py:34
  23.5 2.8 %project.5 = (bf16[256,1152]{1,0:T(8,128)(2,1)S(1)}, f32[256,1152]{1,0:T(8,128)S(1)}, f32[256,128]{1,0:T(8,128)S(1)}, bf16[256,1152]{1,0:T(8,128)(2,1)S(1)}) custom-call(bf16[1152,1152]{1,0:T(8,128)(2,1)S(1)} %copy-done, bf16[1152,1152]{1,0:T(8,128)(2,1)S(1)} %copy-done.2, bf16[128,1152]{1,0:T(8,128)(2,1)S(1)} %collective-permute-done.1.refs_0_, ...), custom_call_target="tpu_custom_call" | custom-call | flops 1358954496 | bytes 8847360 | tf_op jit(solution)/shard_map/project/pallas_call | solution.py:107
  26.3 2.8 %project.4 = (bf16[256,1152]{1,0:T(8,128)(2,1)S(1)}, f32[256,1152]{1,0:T(8,128)S(1)}, f32[256,128]{1,0:T(8,128)S(1)}, bf16[256,1152]{1,0:T(8,128)(2,1)S(1)}) custom-call(bf16[1152,1152]{1,0:T(8,128)(2,1)S(1)} %copy-done, bf16[1152,1152]{1,0:T(8,128)(2,1)S(1)} %copy-done.2, bf16[128,1152]{1,0:T(8,128)(2,1)S(1)} %collective-permute-done.refs_0_, ...), custom_call_target="tpu_custom_call" | custom-call | flops 1358954496 | bytes 8847360 | tf_op jit(solution)/shard_map/project/pallas_call | solution.py:107
  29.1 1.3 %collective-permute-done.6.refs_0_ = bf16[128,1152]{1,0:T(8,128)(2,1)S(1)} collective-permute-done((bf16[128,1152]{1,0:T(8,128)(2,1)S(1)}, bf16[128,1152]{1,0:T(8,128)(2,1)S(1)}, u32[]{:S(2)}, u32[]{:S(2)}) %collective-permute-start.6) | collective-permute-done | bytes 294944 | tf_op jit(solution)/shard_map/ppermute | solution.py:34
  33.1 16.2 %block.1 = (f32[576,384]{1,0:T(8,128)S(1)}, bf16[584,384]{1,0:T(8,128)(2,1)S(1)}, f32[576,384]{1,0:T(8,128)S(1)}, bf16[576,384]{1,0:T(8,128)(2,1)S(1)}, f32[576,...) custom-call(f32[2]{0:T(128)S(1)} %pad_maximum_fusion.1.scalars, ...), custom_call_target="tpu_custom_call" | custom-call | flops 8908701696 | bytes 19464192 | tf_op jit(solution)/shard_map/block/pallas_call | solution.py:322
  49.3 1.6 %collective-permute-start.19 = (bf16[576,384]{1,0:T(8,128)(2,1)S(1)}, bf16[576,384]{1,0:T(8,128)(2,1)S(1)}, u32[]{:S(2)}, u32[]{:S(2)}) collective-permute-start(bf16[576,384]{1,0:T(8,128)(2,1)S(1)} %get-tuple-element.114), channel_id=1, source_target_pairs={{0,16},{4,20},{1,17},{5,21},{2,18},{6,22},{3,19},{7,23},{8,24},{12... | collective-permute-start | bytes 1327112 | tf_op jit(solution)/shard_map/ppermute | solution.py:34
  50.9 1.5 %collective-permute-start.14 = (bf16[584,384]{1,0:T(8,128)(2,1)S(1)}, bf16[584,384]{1,0:T(8,128)(2,1)S(1)}, u32[]{:S(2)}, u32[]{:S(2)}) collective-permute-start(bf16[584,384]{1,0:T(8,128)(2,1)S(1)} %get-tuple-element.102), channel_id=1, source_target_pairs={{0,8},{4,12},{1,9},{5,13},{2,10},{6,14},{3,11},{7,15},{8,0},{12,4}... | collective-permute-start | bytes 1345544 | tf_op jit(solution)/shard_map/ppermute | solution.py:34
  53.5 8.1 %collective-permute-done.19.arrived = bf16[576,384]{1,0:T(8,128)(2,1)S(1)} collective-permute-done((bf16[576,384]{1,0:T(8,128)(2,1)S(1)}, bf16[576,384]{1,0:T(8,128)(2,1)S(1)}, u32[]{:S(2)}, u32[]{:S(2)}) %collective-permute-start.19) | collective-permute-done | bytes 442400 | tf_op jit(solution)/shard_map/ppermute | solution.py:34
  63.0 1.5 %collective-permute-start.15 = (bf16[296,384]{1,0:T(8,128)(2,1)S(1)}, bf16[296,384]{1,0:T(8,128)(2,1)S(1)}, u32[]{:S(2)}, u32[]{:S(2)}) collective-permute-start(bf16[296,384]{1,0:T(8,128)(2,1)S(1)} %get-tuple-element.105), channel_id=1, source_target_pairs={{0,16},{4,20},{1,17},{5,21},{2,18},{6,22},{3,19},{7,23},{8,24},{12... | collective-permute-start | bytes 681992 | tf_op jit(solution)/shard_map/ppermute | solution.py:34
  64.6 1.6 %collective-permute-start.24 = (bf16[288,384]{1,0:T(8,128)(2,1)S(1)}, bf16[288,384]{1,0:T(8,128)(2,1)S(1)}, u32[]{:S(2)}, u32[]{:S(2)}) collective-permute-start(bf16[288,384]{1,0:T(8,128)(2,1)S(1)} %get-tuple-element.124), channel_id=1, source_target_pairs={{0,8},{4,12},{1,9},{5,13},{2,10},{6,14},{3,11},{7,15},{8,0},{12,4}... | collective-permute-start | bytes 663560 | tf_op jit(solution)/shard_map/ppermute | solution.py:34
  66.2 2.6 %collective-permute-done.20.arrived = bf16[288,384]{1,0:T(8,128)(2,1)S(1)} collective-permute-done((bf16[288,384]{1,0:T(8,128)(2,1)S(1)}, bf16[288,384]{1,0:T(8,128)(2,1)S(1)}, u32[]{:S(2)}, u32[]{:S(2)}) %collective-permute-start.20) | collective-permute-done | bytes 221216 | tf_op jit(solution)/shard_map/ppermute | solution.py:34
  70.0 2.2 %collective-permute-start.16 = (bf16[152,384]{1,0:T(8,128)(2,1)S(1)}, bf16[152,384]{1,0:T(8,128)(2,1)S(1)}, u32[]{:S(2)}, u32[]{:S(2)}) collective-permute-start(bf16[152,384]{1,0:T(8,128)(2,1)S(1)} %get-tuple-element.108), channel_id=1, source_target_pairs={{0,2},{4,6},{1,3},{5,7},{2,0},{6,4},{3,1},{7,5},{8,10},{12,14},{9,... | collective-permute-start | bytes 350216 | tf_op jit(solution)/shard_map/ppermute | solution.py:34
  72.3 1.6 %collective-permute-start.25 = (bf16[144,384]{1,0:T(8,128)(2,1)S(1)}, bf16[144,384]{1,0:T(8,128)(2,1)S(1)}, u32[]{:S(2)}, u32[]{:S(2)}) collective-permute-start(bf16[144,384]{1,0:T(8,128)(2,1)S(1)} %get-tuple-element.126), channel_id=1, source_target_pairs={{0,16},{4,20},{1,17},{5,21},{2,18},{6,22},{3,19},{7,23},{8,24},{12... | collective-permute-start | bytes 331784 | tf_op jit(solution)/shard_map/ppermute | solution.py:34
  73.9 1.9 %collective-permute-start.22 = (bf16[72,384]{1,0:T(8,128)(2,1)S(1)}, bf16[72,384]{1,0:T(8,128)(2,1)S(1)}, u32[]{:S(2)}, u32[]{:S(2)}) collective-permute-start(bf16[72,384]{1,0:T(8,128)(2,1)S(1)} %get-tuple-element.120), channel_id=1, source_target_pairs={{0,2},{4,6},{1,3},{5,7},{2,0},{6,4},{3,1},{7,5},{8,10},{12,14},{9,... | collective-permute-start | bytes 165896 | tf_op jit(solution)/shard_map/ppermute | solution.py:34
  75.8 1.3 %collective-permute-done.25.arrived = bf16[144,384]{1,0:T(8,128)(2,1)S(1)} collective-permute-done((bf16[144,384]{1,0:T(8,128)(2,1)S(1)}, bf16[144,384]{1,0:T(8,128)(2,1)S(1)}, u32[]{:S(2)}, u32[]{:S(2)}) %collective-permute-start.25) | collective-permute-done | bytes 110624 | tf_op jit(solution)/shard_map/ppermute | solution.py:34
  80.6 2.3 %collective-permute-done.26 = bf16[72,384]{1,0:T(8,128)(2,1)S(1)} collective-permute-done((bf16[72,384]{1,0:T(8,128)(2,1)S(1)}, bf16[72,384]{1,0:T(8,128)(2,1)S(1)}, u32[]{:S(2)}, u32[]{:S(2)}) %collective-permute-start.26) | collective-permute-done | bytes 55328 | tf_op jit(solution)/shard_map/ppermute | solution.py:34
  (67 shorter events, 16.2 us)
Async XLA Ops:
  0.6 7.7 %collective-permute-start.4 = (bf16[128,1152]{1,0:T(8,128)(2,1)}, bf16[128,1152]{1,0:T(8,128)(2,1)S(1)}, u32[]{:S(2)}, u32[]{:S(2)}) collective-permute-start(bf16[128,1152]{1,0:T(8,128)(2,1)} %refs_0_.1), channel_id=1, source_target_pairs={{0,4},{4,0},{1,5},{5,1},{2,6},{6,2},{3,7},{7,3},{8,12},{12,8},{9,1... | collective-permute-start | bytes 884744 | tf_op jit(solution)/shard_map/ppermute | solution.py:34
  1.1 8.7 %collective-permute-start.5 = (bf16[128,1152]{1,0:T(8,128)(2,1)}, bf16[128,1152]{1,0:T(8,128)(2,1)S(1)}, u32[]{:S(2)}, u32[]{:S(2)}) collective-permute-start(bf16[128,1152]{1,0:T(8,128)(2,1)} %refs_1_.1), channel_id=1, source_target_pairs={{0,4},{4,0},{1,5},{5,1},{2,6},{6,2},{3,7},{7,3},{8,12},{12,8},{9,1... | collective-permute-start | bytes 884744 | tf_op jit(solution)/shard_map/ppermute | solution.py:34
  1.2 16.8 %collective-permute-start = (bf16[128,1152]{1,0:T(8,128)(2,1)}, bf16[128,1152]{1,0:T(8,128)(2,1)S(1)}, u32[]{:S(2)}, u32[]{:S(2)}) collective-permute-start(bf16[128,1152]{1,0:T(8,128)(2,1)} %refs_0_.1), channel_id=1, source_target_pairs={{0,1},{4,5},{1,0},{5,4},{2,3},{6,7},{3,2},{7,6},{8,9},{12,13},{9,8... | collective-permute-start | bytes 884744 | tf_op jit(solution)/shard_map/ppermute | solution.py:34
  4.2 16.2 %collective-permute-start.1 = (bf16[128,1152]{1,0:T(8,128)(2,1)}, bf16[128,1152]{1,0:T(8,128)(2,1)S(1)}, u32[]{:S(2)}, u32[]{:S(2)}) collective-permute-start(bf16[128,1152]{1,0:T(8,128)(2,1)} %refs_0_.1), channel_id=1, source_target_pairs={{0,2},{4,6},{1,3},{5,7},{2,0},{6,4},{3,1},{7,5},{8,10},{12,14},{9,... | collective-permute-start | bytes 884744 | tf_op jit(solution)/shard_map/ppermute | solution.py:34
  6.8 13.6 %collective-permute-start.2 = (bf16[128,1152]{1,0:T(8,128)(2,1)}, bf16[128,1152]{1,0:T(8,128)(2,1)S(1)}, u32[]{:S(2)}, u32[]{:S(2)}) collective-permute-start(bf16[128,1152]{1,0:T(8,128)(2,1)} %refs_1_.1), channel_id=1, source_target_pairs={{0,8},{4,12},{1,9},{5,13},{2,10},{6,14},{3,11},{7,15},{8,0},{12,4}... | collective-permute-start | bytes 884744 | tf_op jit(solution)/shard_map/ppermute | solution.py:34
  8.3 12.1 %collective-permute-start.3 = (bf16[128,1152]{1,0:T(8,128)(2,1)}, bf16[128,1152]{1,0:T(8,128)(2,1)S(1)}, u32[]{:S(2)}, u32[]{:S(2)}) collective-permute-start(bf16[128,1152]{1,0:T(8,128)(2,1)} %refs_1_.1), channel_id=1, source_target_pairs={{0,16},{4,20},{1,17},{5,21},{2,18},{6,22},{3,19},{7,23},{8,24},{12... | collective-permute-start | bytes 884744 | tf_op jit(solution)/shard_map/ppermute | solution.py:34
  20.4 3.1 %collective-permute-start.11 = (bf16[128,1152]{1,0:T(8,128)(2,1)S(1)}, bf16[128,1152]{1,0:T(8,128)(2,1)S(1)}, u32[]{:S(2)}, u32[]{:S(2)}) collective-permute-start(bf16[128,1152]{1,0:T(8,128)(2,1)S(1)} %collective-permute-done.3.refs_1_), channel_id=1, source_target_pairs={{0,4},{4,0},{1,5},{5,1},{2,6},{6,2},{3,7},{7,3},{8,12},{12,8},{9,1... | collective-permute-start | bytes 884744 | tf_op jit(solution)/shard_map/ppermute | solution.py:34
  21.0 5.4 %collective-permute-start.8 = (bf16[128,1152]{1,0:T(8,128)(2,1)S(1)}, bf16[128,1152]{1,0:T(8,128)(2,1)S(1)}, u32[]{:S(2)}, u32[]{:S(2)}) collective-permute-start(bf16[128,1152]{1,0:T(8,128)(2,1)S(1)} %collective-permute-done.refs_0_), channel_id=1, source_target_pairs={{0,4},{4,0},{1,5},{5,1},{2,6},{6,2},{3,7},{7,3},{8,12},{12,8},{9,1... | collective-permute-start | bytes 884744 | tf_op jit(solution)/shard_map/ppermute | solution.py:34
  21.0 5.3 %collective-permute-start.9 = (bf16[128,1152]{1,0:T(8,128)(2,1)S(1)}, bf16[128,1152]{1,0:T(8,128)(2,1)S(1)}, u32[]{:S(2)}, u32[]{:S(2)}) collective-permute-start(bf16[128,1152]{1,0:T(8,128)(2,1)S(1)} %collective-permute-done.2.refs_1_), channel_id=1, source_target_pairs={{0,4},{4,0},{1,5},{5,1},{2,6},{6,2},{3,7},{7,3},{8,12},{12,8},{9,1... | collective-permute-start | bytes 884744 | tf_op jit(solution)/shard_map/ppermute | solution.py:34
  21.5 9.0 %collective-permute-start.6 = (bf16[128,1152]{1,0:T(8,128)(2,1)S(1)}, bf16[128,1152]{1,0:T(8,128)(2,1)S(1)}, u32[]{:S(2)}, u32[]{:S(2)}) collective-permute-start(bf16[128,1152]{1,0:T(8,128)(2,1)S(1)} %collective-permute-done.1.refs_0_), channel_id=1, source_target_pairs={{0,1},{4,5},{1,0},{5,4},{2,3},{6,7},{3,2},{7,6},{8,9},{12,13},{9,8... | collective-permute-start | bytes 884744 | tf_op jit(solution)/shard_map/ppermute | solution.py:34
  22.0 9.1 %collective-permute-start.7 = (bf16[128,1152]{1,0:T(8,128)(2,1)S(1)}, bf16[128,1152]{1,0:T(8,128)(2,1)S(1)}, u32[]{:S(2)}, u32[]{:S(2)}) collective-permute-start(bf16[128,1152]{1,0:T(8,128)(2,1)S(1)} %collective-permute-done.3.refs_1_), channel_id=1, source_target_pairs={{0,8},{4,12},{1,9},{5,13},{2,10},{6,14},{3,11},{7,15},{8,0},{12,4}... | collective-permute-start | bytes 884744 | tf_op jit(solution)/shard_map/ppermute | solution.py:34
  31.1 2.0 %collective-permute-start.13 = (bf16[128,1152]{1,0:T(8,128)(2,1)S(1)}, bf16[128,1152]{1,0:T(8,128)(2,1)S(1)}, u32[]{:S(2)}, u32[]{:S(2)}) collective-permute-start(bf16[128,1152]{1,0:T(8,128)(2,1)S(1)} %collective-permute-done.7.refs_1_), channel_id=1, source_target_pairs={{0,4},{4,0},{1,5},{5,1},{2,6},{6,2},{3,7},{7,3},{8,12},{12,8},{9,1... | collective-permute-start | bytes 884744 | tf_op jit(solution)/shard_map/ppermute | solution.py:34
  49.3 12.3 %collective-permute-start.19 = (bf16[576,384]{1,0:T(8,128)(2,1)S(1)}, bf16[576,384]{1,0:T(8,128)(2,1)S(1)}, u32[]{:S(2)}, u32[]{:S(2)}) collective-permute-start(bf16[576,384]{1,0:T(8,128)(2,1)S(1)} %get-tuple-element.114), channel_id=1, source_target_pairs={{0,16},{4,20},{1,17},{5,21},{2,18},{6,22},{3,19},{7,23},{8,24},{12... | collective-permute-start | bytes 1327112 | tf_op jit(solution)/shard_map/ppermute | solution.py:34
  50.9 12.1 %collective-permute-start.14 = (bf16[584,384]{1,0:T(8,128)(2,1)S(1)}, bf16[584,384]{1,0:T(8,128)(2,1)S(1)}, u32[]{:S(2)}, u32[]{:S(2)}) collective-permute-start(bf16[584,384]{1,0:T(8,128)(2,1)S(1)} %get-tuple-element.102), channel_id=1, source_target_pairs={{0,8},{4,12},{1,9},{5,13},{2,10},{6,14},{3,11},{7,15},{8,0},{12,4}... | collective-permute-start | bytes 1345544 | tf_op jit(solution)/shard_map/ppermute | solution.py:34
  52.4 12.2 %collective-permute-start.23 = (bf16[576,384]{1,0:T(8,128)(2,1)S(1)}, bf16[576,384]{1,0:T(8,128)(2,1)S(1)}, u32[]{:S(2)}, u32[]{:S(2)}) collective-permute-start(bf16[576,384]{1,0:T(8,128)(2,1)S(1)} %get-tuple-element.122), channel_id=1, source_target_pairs={{0,1},{4,5},{1,0},{5,4},{2,3},{6,7},{3,2},{7,6},{8,9},{12,13},{9,8... | collective-permute-start | bytes 1327112 | tf_op jit(solution)/shard_map/ppermute | solution.py:34
  61.7 7.1 %collective-permute-start.20 = (bf16[288,384]{1,0:T(8,128)(2,1)S(1)}, bf16[288,384]{1,0:T(8,128)(2,1)S(1)}, u32[]{:S(2)}, u32[]{:S(2)}) collective-permute-start(bf16[288,384]{1,0:T(8,128)(2,1)S(1)} %get-tuple-element.116), channel_id=1, source_target_pairs={{0,1},{4,5},{1,0},{5,4},{2,3},{6,7},{3,2},{7,6},{8,9},{12,13},{9,8... | collective-permute-start | bytes 663560 | tf_op jit(solution)/shard_map/ppermute | solution.py:34
  63.0 7.0 %collective-permute-start.15 = (bf16[296,384]{1,0:T(8,128)(2,1)S(1)}, bf16[296,384]{1,0:T(8,128)(2,1)S(1)}, u32[]{:S(2)}, u32[]{:S(2)}) collective-permute-start(bf16[296,384]{1,0:T(8,128)(2,1)S(1)} %get-tuple-element.105), channel_id=1, source_target_pairs={{0,16},{4,20},{1,17},{5,21},{2,18},{6,22},{3,19},{7,23},{8,24},{12... | collective-permute-start | bytes 681992 | tf_op jit(solution)/shard_map/ppermute | solution.py:34
  64.6 7.6 %collective-permute-start.24 = (bf16[288,384]{1,0:T(8,128)(2,1)S(1)}, bf16[288,384]{1,0:T(8,128)(2,1)S(1)}, u32[]{:S(2)}, u32[]{:S(2)}) collective-permute-start(bf16[288,384]{1,0:T(8,128)(2,1)S(1)} %get-tuple-element.124), channel_id=1, source_target_pairs={{0,8},{4,12},{1,9},{5,13},{2,10},{6,14},{3,11},{7,15},{8,0},{12,4}... | collective-permute-start | bytes 663560 | tf_op jit(solution)/shard_map/ppermute | solution.py:34
  68.8 5.1 %collective-permute-start.21 = (bf16[144,384]{1,0:T(8,128)(2,1)S(1)}, bf16[144,384]{1,0:T(8,128)(2,1)S(1)}, u32[]{:S(2)}, u32[]{:S(2)}) collective-permute-start(bf16[144,384]{1,0:T(8,128)(2,1)S(1)} %get-tuple-element.118), channel_id=1, source_target_pairs={{0,8},{4,12},{1,9},{5,13},{2,10},{6,14},{3,11},{7,15},{8,0},{12,4}... | collective-permute-start | bytes 331784 | tf_op jit(solution)/shard_map/ppermute | solution.py:34
  70.0 9.0 %collective-permute-start.16 = (bf16[152,384]{1,0:T(8,128)(2,1)S(1)}, bf16[152,384]{1,0:T(8,128)(2,1)S(1)}, u32[]{:S(2)}, u32[]{:S(2)}) collective-permute-start(bf16[152,384]{1,0:T(8,128)(2,1)S(1)} %get-tuple-element.108), channel_id=1, source_target_pairs={{0,2},{4,6},{1,3},{5,7},{2,0},{6,4},{3,1},{7,5},{8,10},{12,14},{9,... | collective-permute-start | bytes 350216 | tf_op jit(solution)/shard_map/ppermute | solution.py:34
  72.3 4.8 %collective-permute-start.25 = (bf16[144,384]{1,0:T(8,128)(2,1)S(1)}, bf16[144,384]{1,0:T(8,128)(2,1)S(1)}, u32[]{:S(2)}, u32[]{:S(2)}) collective-permute-start(bf16[144,384]{1,0:T(8,128)(2,1)S(1)} %get-tuple-element.126), channel_id=1, source_target_pairs={{0,16},{4,20},{1,17},{5,21},{2,18},{6,22},{3,19},{7,23},{8,24},{12... | collective-permute-start | bytes 331784 | tf_op jit(solution)/shard_map/ppermute | solution.py:34
  73.9 6.7 %collective-permute-start.22 = (bf16[72,384]{1,0:T(8,128)(2,1)S(1)}, bf16[72,384]{1,0:T(8,128)(2,1)S(1)}, u32[]{:S(2)}, u32[]{:S(2)}) collective-permute-start(bf16[72,384]{1,0:T(8,128)(2,1)S(1)} %get-tuple-element.120), channel_id=1, source_target_pairs={{0,2},{4,6},{1,3},{5,7},{2,0},{6,4},{3,1},{7,5},{8,10},{12,14},{9,... | collective-permute-start | bytes 165896 | tf_op jit(solution)/shard_map/ppermute | solution.py:34
  77.2 5.8 %collective-permute-start.26 = (bf16[72,384]{1,0:T(8,128)(2,1)S(1)}, bf16[72,384]{1,0:T(8,128)(2,1)S(1)}, u32[]{:S(2)}, u32[]{:S(2)}) collective-permute-start(bf16[72,384]{1,0:T(8,128)(2,1)S(1)} %get-tuple-element.128), channel_id=1, source_target_pairs={{0,2},{4,6},{1,3},{5,7},{2,0},{6,4},{3,1},{7,5},{8,10},{12,14},{9,... | collective-permute-start | bytes 165896 | tf_op jit(solution)/shard_map/ppermute | solution.py:34
  79.1 4.5 %collective-permute-start.17 = (bf16[80,384]{1,0:T(8,128)(2,1)S(1)}, bf16[80,384]{1,0:T(8,128)(2,1)S(1)}, u32[]{:S(2)}, u32[]{:S(2)}) collective-permute-start(bf16[80,384]{1,0:T(8,128)(2,1)S(1)} %get-tuple-element.111), channel_id=1, source_target_pairs={{0,1},{4,5},{1,0},{5,4},{2,3},{6,7},{3,2},{7,6},{8,9},{12,13},{9,8... | collective-permute-start | bytes 184328 | tf_op jit(solution)/shard_map/ppermute | solution.py:34
  (9 other events, 18.7 us)

commit v7 on v6

--- a/solution.py
+++ b/solution.py
@@ -57,13 +57,16 @@
     return lax.rem(lax.axis_index("dp"), 2)
 
 
-def load_projections(image_proj, text_proj, projs, sems):
+def by_role(image_proj, text_proj, body):
     core = this_core()
-    own = pltpu.make_async_copy(image_proj, projs.at[core], sems.at[0])
-    other = pltpu.make_async_copy(text_proj, projs.at[1 - core], sems.at[1])
-    own.start()
-    other.start()
-    return [own, other]
+
+    @pl.when(core == 0)
+    def _():
+        body(image_proj, text_proj)
+
+    @pl.when(core == 1)
+    def _():
+        body(text_proj, image_proj)
 
 
 def load_chunk(shards, feats, sems):
@@ -85,16 +88,18 @@
 
 
 def project_kernel(image_proj, text_proj, *refs):
-    shards, (own_chunk, own_unit, own_inverse, other_half, feats, projs, sems) = refs[:4], refs[4:]
-    copies = load_chunk(shards, feats, sems.at[pl.ds(2, 4)])
-    copies += load_projections(image_proj, text_proj, projs, sems.at[pl.ds(0, 2)])
-    for copy in copies:
+    shards, (own_chunk, own_unit, own_inverse, other_half, feats, sems) = refs[:4], refs[4:]
+    for copy in load_chunk(shards, feats, sems):
         copy.wait()
-    unit, _ = project(feats[1], projs[1])
-    other_half[...] = unit.astype(BF16)
-    unit, inverse = project(feats[0], projs[0])
-    own_unit[...] = unit
-    own_inverse[...] = jnp.broadcast_to(inverse, own_inverse.shape)
+
+    def body(own_proj, other_proj):
+        unit, _ = project(feats[1], other_proj[...])
+        other_half[...] = unit.astype(BF16)
+        unit, inverse = project(feats[0], own_proj[...])
+        own_unit[...] = unit
+        own_inverse[...] = jnp.broadcast_to(inverse, own_inverse.shape)
+
+    by_role(image_proj, text_proj, body)
     own_chunk[...] = feats[0]
 
 
@@ -112,12 +117,11 @@
             jax.ShapeDtypeStruct((rows, 128), F32),
             jax.ShapeDtypeStruct((rows, width), BF16),
         ],
-        in_specs=[hbm] * 2 + [hbm if from_arguments else anywhere] * 2 + [anywhere] * 2,
+        in_specs=[vmem] * 2 + [hbm if from_arguments else anywhere] * 2 + [anywhere] * 2,
         out_specs=[vmem] * 4,
         scratch_shapes=[
             pltpu.VMEM((2, rows, width), BF16),
-            pltpu.VMEM((2, width, width), BF16),
-            pltpu.SemaphoreType.DMA((6,)),
+            pltpu.SemaphoreType.DMA((4,)),
         ],
         compiler_params=pltpu.CompilerParams(
             vmem_limit_bytes=4 * width * width + 24 * rows * width + 4 * 1024 * 1024
@@ -160,7 +164,7 @@
     other_halves, refs = refs[: side - 1], refs[side - 1 :]
     orders = part_orders(side)
     results, refs = refs[: 2 * len(orders)], refs[2 * len(orders) :]
-    stats, projs, last, feats, units, inverses, other_half, dy, grad, pieces, moving, sems = refs
+    stats, last, feats, units, inverses, other_half, dy, grad, pieces, moving, sems = refs
     rows, width = dy.shape
     chunk_rows = rows // side
     rest = rows - chunk_rows
@@ -169,7 +173,7 @@
     unit_row, unit_column = unit_index // side, lax.rem(unit_index, side)
     scale, bias = scalars[0], scalars[1]
 
-    count = 6
+    count = 4
 
     def start(source, target):
         nonlocal count
@@ -181,8 +185,7 @@
     def places(i):
         return pl.ds(i * chunk_rows, chunk_rows)
 
-    first_copies = load_chunk(last_shards, last, sems.at[pl.ds(2, 4)])
-    first_copies += load_projections(image_proj, text_proj, projs, sems.at[pl.ds(0, 2)])
+    first_copies = load_chunk(last_shards, last, sems.at[pl.ds(0, 4)])
     other_copies = [start(other_halves[i], other_half.at[places(i)]) for i in range(side - 1)]
     unit_copies = [start(own_units[i], units.at[places(i)]) for i in range(side - 1)]
     unit_copies += [start(own_inverses[i], inverses.at[places(i)]) for i in range(side - 1)]
@@ -190,11 +193,15 @@
 
     for copy in first_copies:
         copy.wait()
-    unit, _ = project(last[1], projs[1])
-    other_half[rest:, :] = unit.astype(BF16)
-    unit, inverse = project(last[0], projs[0])
-    units[rest:, :] = unit
-    inverses[rest:, :] = jnp.broadcast_to(inverse, (chunk_rows, 128))
+
+    def project_last(own_proj, other_proj):
+        unit, _ = project(last[1], other_proj[...])
+        other_half[rest:, :] = unit.astype(BF16)
+        unit, inverse = project(last[0], own_proj[...])
+        units[rest:, :] = unit
+        inverses[rest:, :] = jnp.broadcast_to(inverse, (chunk_rows, 128))
+
+    by_role(image_proj, text_proj, project_last)
     feats[rest:, :] = last[0]
     for copy in other_copies + unit_copies:
         copy.wait()
@@ -323,11 +330,10 @@
         functools.partial(block_kernel, side, layout.mp),
         out_shape=out_shape,
         in_specs=[pl.BlockSpec(memory_space=pltpu.SMEM)]
-        + [pl.BlockSpec(memory_space=pltpu.HBM)] * 2
+        + [vmem] * 2
         + [anywhere] * (len(operands) - 2),
         out_specs=[vmem] * len(out_shape),
         scratch_shapes=[
-            pltpu.VMEM((2, width, width), BF16),
             pltpu.VMEM((2, chunk_rows, width), BF16),
             pltpu.VMEM((rows, width), BF16),
             pltpu.VMEM((rows, width), F32),
@@ -337,7 +343,7 @@
             pltpu.VMEM((width, width), F32),
             pltpu.VMEM((2 * half_rows, width), F32),
             pltpu.VMEM((half_rows + 8, part_width), F32),
-            pltpu.SemaphoreType.DMA((len(operands),)),
+            pltpu.SemaphoreType.DMA((len(operands) - 2,)),
         ],
         compiler_params=pltpu.CompilerParams(vmem_limit_bytes=min(needed, 60 * 1024 * 1024)),
         cost_estimate=pl.CostEstimate(

time: 86.5 us -> 87.4 us (1.010)
  waiting for transfers between devices: 22.2 us -> 23.6 us
    pallas_call x3, Pallas kernels: 8.31 us -> 6.91 us  [project_chunk(): pl.pallas_call(project_kernel, out_shape=[jax.ShapeDtypeStruct((rows, wid...]
    ppermute x28, waiting for transfers between devices: 22.2 us -> 23.6 us  [send(): return lax.ppermute(value, AXES, pairs)]
    pallas_call x1, Pallas kernels: 16.2 us -> 17.1 us  [block_grads(): pl.pallas_call(functools.partial(block_kernel, side, layout.mp), out_shap...]
  transfers between devices with their start and end apart: 28 -> 28, of which waited for: 14 -> 15; matrix products, arithmetic and copies ran while one was open for 1% -> 1% of each run, Pallas kernels for 10% -> 9%
where the time goes in v7:
time: 87.4 us; the launch traced here: 87.1 us
  starting transfers between devices  29.8 us (34%)
  Pallas kernels  24.6 us (28%)
  waiting for transfers between devices  23.6 us (27%)
  local copies, waits for them, and re-layouts  6.02 us (7%)
  between operations  2.12 us (2%)
  other arithmetic  1.09 us (1%)
    ppermute x28, starting transfers between devices, send(): return lax.ppermute(value, AXES, pairs)  29.8 us
    ppermute x28, waiting for transfers between devices, send(): return lax.ppermute(value, AXES, pairs)  23.6 us
    pallas_call x1, Pallas kernels, block_grads(): pl.pallas_call(functools.partial(block_kernel, side, layout.mp), out_shap...  17.1 us
    pallas_call x3, Pallas kernels, project_chunk(): pl.pallas_call(project_kernel, out_shape=[jax.ShapeDtypeStruct((rows, wid...  6.91 us
    unnamed x10, local copies, waits for them, and re-layouts  5.43 us
  transfers between devices with their start and end apart: 28, of which 15 were waited for; matrix products, arithmetic and copies ran while one was open for 1% of the time, Pallas kernels for 9%

profile of v7, /device:TPU:0, one launch (start us, length us, event | category | flops | bytes accessed | tf_op | source)
XLA Modules:
  0.0 87.1 jit_solution(6422736009698019125)
XLA Ops:
  1.2 3.0 %collective-permute-start = (bf16[128,1152]{1,0:T(8,128)(2,1)}, bf16[128,1152]{1,0:T(8,128)(2,1)S(1)}, u32[]{:S(2)}, u32[]{:S(2)}) collective-permute-start(bf16[128,1152]{1,0:T(8,128)(2,1)} %refs_0_.1), channel_id=1, source_target_pairs={{0,1},{4,5},{1,0},{5,4},{2,3},{6,7},{3,2},{7,6},{8,9},{12,13},{9,8... | collective-permute-start | bytes 884744 | tf_op jit(solution)/shard_map/ppermute | solution.py:34
  4.2 2.6 %collective-permute-start.1 = (bf16[128,1152]{1,0:T(8,128)(2,1)}, bf16[128,1152]{1,0:T(8,128)(2,1)S(1)}, u32[]{:S(2)}, u32[]{:S(2)}) collective-permute-start(bf16[128,1152]{1,0:T(8,128)(2,1)} %refs_0_.1), channel_id=1, source_target_pairs={{0,2},{4,6},{1,3},{5,7},{2,0},{6,4},{3,1},{7,5},{8,10},{12,14},{9,... | collective-permute-start | bytes 884744 | tf_op jit(solution)/shard_map/ppermute | solution.py:34
  6.8 1.5 %collective-permute-start.2 = (bf16[128,1152]{1,0:T(8,128)(2,1)}, bf16[128,1152]{1,0:T(8,128)(2,1)S(1)}, u32[]{:S(2)}, u32[]{:S(2)}) collective-permute-start(bf16[128,1152]{1,0:T(8,128)(2,1)} %refs_1_.1), channel_id=1, source_target_pairs={{0,8},{4,12},{1,9},{5,13},{2,10},{6,14},{3,11},{7,15},{8,0},{12,4}... | collective-permute-start | bytes 884744 | tf_op jit(solution)/shard_map/ppermute | solution.py:34
  8.3 1.5 %collective-permute-start.3 = (bf16[128,1152]{1,0:T(8,128)(2,1)}, bf16[128,1152]{1,0:T(8,128)(2,1)S(1)}, u32[]{:S(2)}, u32[]{:S(2)}) collective-permute-start(bf16[128,1152]{1,0:T(8,128)(2,1)} %refs_1_.1), channel_id=1, source_target_pairs={{0,16},{4,20},{1,17},{5,21},{2,18},{6,22},{3,19},{7,23},{8,24},{12... | collective-permute-start | bytes 884744 | tf_op jit(solution)/shard_map/ppermute | solution.py:34
  9.8 1.7 %copy-done = bf16[1152,1152]{1,0:T(8,128)(2,1)S(1)} copy-done((bf16[1152,1152]{1,0:T(8,128)(2,1)S(1)}, bf16[1152,1152]{1,0:T(8,128)(2,1)}, u32[]{:S(2)}) %copy-start) | copy-done | bytes 2654232
  11.6 1.7 %copy-done.2 = bf16[1152,1152]{1,0:T(8,128)(2,1)S(1)} copy-done((bf16[1152,1152]{1,0:T(8,128)(2,1)S(1)}, bf16[1152,1152]{1,0:T(8,128)(2,1)}, u32[]{:S(2)}) %copy-start.2) | copy-done | bytes 2654232
  15.3 2.3 %project.3 = (bf16[256,1152]{1,0:T(8,128)(2,1)S(1)}, f32[256,1152]{1,0:T(8,128)S(1)}, f32[256,128]{1,0:T(8,128)S(1)}, bf16[256,1152]{1,0:T(8,128)(2,1)S(1)}) custom-call(bf16[1152,1152]{1,0:T(8,128)(2,1)S(1)} %copy-done, bf16[1152,1152]{1,0:T(8,128)(2,1)S(1)} %copy-done.2, bf16[128,1152]{1,0:T(8,128)(2,1)S(1)} %copy-done.3, bf16[128,1152]{1,0:T(8,128)(2,1)S(1)} %copy-done.4, ...), custom_call_target="tpu_custom_call" | custom-call | flops 1358954496 | bytes 8847360 | tf_op jit(solution)/shard_map/project/pallas_call | solution.py:112
  17.9 2.6 %collective-permute-done.1.refs_0_ = bf16[128,1152]{1,0:T(8,128)(2,1)S(1)} collective-permute-done((bf16[128,1152]{1,0:T(8,128)(2,1)}, bf16[128,1152]{1,0:T(8,128)(2,1)S(1)}, u32[]{:S(2)}, u32[]{:S(2)}) %collective-permute-start.1) | collective-permute-done | bytes 294944 | tf_op jit(solution)/shard_map/ppermute | solution.py:34
  22.0 1.5 %collective-permute-start.7 = (bf16[128,1152]{1,0:T(8,128)(2,1)S(1)}, bf16[128,1152]{1,0:T(8,128)(2,1)S(1)}, u32[]{:S(2)}, u32[]{:S(2)}) collective-permute-start(bf16[128,1152]{1,0:T(8,128)(2,1)S(1)} %collective-permute-done.3.refs_1_), channel_id=1, source_target_pairs={{0,8},{4,12},{1,9},{5,13},{2,10},{6,14},{3,11},{7,15},{8,0},{12,4}... | collective-permute-start | bytes 884744 | tf_op jit(solution)/shard_map/ppermute | solution.py:34
  23.5 2.3 %project.5 = (bf16[256,1152]{1,0:T(8,128)(2,1)S(1)}, f32[256,1152]{1,0:T(8,128)S(1)}, f32[256,128]{1,0:T(8,128)S(1)}, bf16[256,1152]{1,0:T(8,128)(2,1)S(1)}) custom-call(bf16[1152,1152]{1,0:T(8,128)(2,1)S(1)} %copy-done, bf16[1152,1152]{1,0:T(8,128)(2,1)S(1)} %copy-done.2, bf16[128,1152]{1,0:T(8,128)(2,1)S(1)} %collective-permute-done.1.refs_0_, ...), custom_call_target="tpu_custom_call" | custom-call | flops 1358954496 | bytes 8847360 | tf_op jit(solution)/shard_map/project/pallas_call | solution.py:112
  25.9 2.3 %project.4 = (bf16[256,1152]{1,0:T(8,128)(2,1)S(1)}, f32[256,1152]{1,0:T(8,128)S(1)}, f32[256,128]{1,0:T(8,128)S(1)}, bf16[256,1152]{1,0:T(8,128)(2,1)S(1)}) custom-call(bf16[1152,1152]{1,0:T(8,128)(2,1)S(1)} %copy-done, bf16[1152,1152]{1,0:T(8,128)(2,1)S(1)} %copy-done.2, bf16[128,1152]{1,0:T(8,128)(2,1)S(1)} %collective-permute-done.refs_0_, ...), custom_call_target="tpu_custom_call" | custom-call | flops 1358954496 | bytes 8847360 | tf_op jit(solution)/shard_map/project/pallas_call | solution.py:112
  28.2 2.3 %collective-permute-done.6.refs_0_ = bf16[128,1152]{1,0:T(8,128)(2,1)S(1)} collective-permute-done((bf16[128,1152]{1,0:T(8,128)(2,1)S(1)}, bf16[128,1152]{1,0:T(8,128)(2,1)S(1)}, u32[]{:S(2)}, u32[]{:S(2)}) %collective-permute-start.6) | collective-permute-done | bytes 294944 | tf_op jit(solution)/shard_map/ppermute | solution.py:34
  33.1 17.1 %block.1 = (f32[576,384]{1,0:T(8,128)S(1)}, bf16[584,384]{1,0:T(8,128)(2,1)S(1)}, f32[576,384]{1,0:T(8,128)S(1)}, bf16[576,384]{1,0:T(8,128)(2,1)S(1)}, f32[576,...) custom-call(f32[2]{0:T(128)S(1)} %pad_maximum_fusion.1.scalars, ...), custom_call_target="tpu_custom_call" | custom-call | flops 8908701696 | bytes 19464192 | tf_op jit(solution)/shard_map/block/pallas_call | solution.py:329
  50.2 1.6 %collective-permute-start.19 = (bf16[576,384]{1,0:T(8,128)(2,1)S(1)}, bf16[576,384]{1,0:T(8,128)(2,1)S(1)}, u32[]{:S(2)}, u32[]{:S(2)}) collective-permute-start(bf16[576,384]{1,0:T(8,128)(2,1)S(1)} %get-tuple-element.114), channel_id=1, source_target_pairs={{0,16},{4,20},{1,17},{5,21},{2,18},{6,22},{3,19},{7,23},{8,24},{12... | collective-permute-start | bytes 1327112 | tf_op jit(solution)/shard_map/ppermute | solution.py:34
  51.8 1.5 %collective-permute-start.14 = (bf16[584,384]{1,0:T(8,128)(2,1)S(1)}, bf16[584,384]{1,0:T(8,128)(2,1)S(1)}, u32[]{:S(2)}, u32[]{:S(2)}) collective-permute-start(bf16[584,384]{1,0:T(8,128)(2,1)S(1)} %get-tuple-element.102), channel_id=1, source_target_pairs={{0,8},{4,12},{1,9},{5,13},{2,10},{6,14},{3,11},{7,15},{8,0},{12,4}... | collective-permute-start | bytes 1345544 | tf_op jit(solution)/shard_map/ppermute | solution.py:34
  54.4 8.1 %collective-permute-done.19.arrived = bf16[576,384]{1,0:T(8,128)(2,1)S(1)} collective-permute-done((bf16[576,384]{1,0:T(8,128)(2,1)S(1)}, bf16[576,384]{1,0:T(8,128)(2,1)S(1)}, u32[]{:S(2)}, u32[]{:S(2)}) %collective-permute-start.19) | collective-permute-done | bytes 442400 | tf_op jit(solution)/shard_map/ppermute | solution.py:34
  63.9 1.5 %collective-permute-start.15 = (bf16[296,384]{1,0:T(8,128)(2,1)S(1)}, bf16[296,384]{1,0:T(8,128)(2,1)S(1)}, u32[]{:S(2)}, u32[]{:S(2)}) collective-permute-start(bf16[296,384]{1,0:T(8,128)(2,1)S(1)} %get-tuple-element.105), channel_id=1, source_target_pairs={{0,16},{4,20},{1,17},{5,21},{2,18},{6,22},{3,19},{7,23},{8,24},{12... | collective-permute-start | bytes 681992 | tf_op jit(solution)/shard_map/ppermute | solution.py:34
  65.5 1.6 %collective-permute-start.24 = (bf16[288,384]{1,0:T(8,128)(2,1)S(1)}, bf16[288,384]{1,0:T(8,128)(2,1)S(1)}, u32[]{:S(2)}, u32[]{:S(2)}) collective-permute-start(bf16[288,384]{1,0:T(8,128)(2,1)S(1)} %get-tuple-element.124), channel_id=1, source_target_pairs={{0,8},{4,12},{1,9},{5,13},{2,10},{6,14},{3,11},{7,15},{8,0},{12,4}... | collective-permute-start | bytes 663560 | tf_op jit(solution)/shard_map/ppermute | solution.py:34
  67.1 2.5 %collective-permute-done.20.arrived = bf16[288,384]{1,0:T(8,128)(2,1)S(1)} collective-permute-done((bf16[288,384]{1,0:T(8,128)(2,1)S(1)}, bf16[288,384]{1,0:T(8,128)(2,1)S(1)}, u32[]{:S(2)}, u32[]{:S(2)}) %collective-permute-start.20) | collective-permute-done | bytes 221216 | tf_op jit(solution)/shard_map/ppermute | solution.py:34
  71.0 2.2 %collective-permute-start.16 = (bf16[152,384]{1,0:T(8,128)(2,1)S(1)}, bf16[152,384]{1,0:T(8,128)(2,1)S(1)}, u32[]{:S(2)}, u32[]{:S(2)}) collective-permute-start(bf16[152,384]{1,0:T(8,128)(2,1)S(1)} %get-tuple-element.108), channel_id=1, source_target_pairs={{0,2},{4,6},{1,3},{5,7},{2,0},{6,4},{3,1},{7,5},{8,10},{12,14},{9,... | collective-permute-start | bytes 350216 | tf_op jit(solution)/shard_map/ppermute | solution.py:34
  73.2 1.6 %collective-permute-start.25 = (bf16[144,384]{1,0:T(8,128)(2,1)S(1)}, bf16[144,384]{1,0:T(8,128)(2,1)S(1)}, u32[]{:S(2)}, u32[]{:S(2)}) collective-permute-start(bf16[144,384]{1,0:T(8,128)(2,1)S(1)} %get-tuple-element.126), channel_id=1, source_target_pairs={{0,16},{4,20},{1,17},{5,21},{2,18},{6,22},{3,19},{7,23},{8,24},{12... | collective-permute-start | bytes 331784 | tf_op jit(solution)/shard_map/ppermute | solution.py:34
  74.8 1.9 %collective-permute-start.22 = (bf16[72,384]{1,0:T(8,128)(2,1)S(1)}, bf16[72,384]{1,0:T(8,128)(2,1)S(1)}, u32[]{:S(2)}, u32[]{:S(2)}) collective-permute-start(bf16[72,384]{1,0:T(8,128)(2,1)S(1)} %get-tuple-element.120), channel_id=1, source_target_pairs={{0,2},{4,6},{1,3},{5,7},{2,0},{6,4},{3,1},{7,5},{8,10},{12,14},{9,... | collective-permute-start | bytes 165896 | tf_op jit(solution)/shard_map/ppermute | solution.py:34
  80.3 1.3 %collective-permute-done.22 = bf16[72,384]{1,0:T(8,128)(2,1)S(1)} collective-permute-done((bf16[72,384]{1,0:T(8,128)(2,1)S(1)}, bf16[72,384]{1,0:T(8,128)(2,1)S(1)}, u32[]{:S(2)}, u32[]{:S(2)}) %collective-permute-start.22) | collective-permute-done | bytes 55328 | tf_op jit(solution)/shard_map/ppermute | solution.py:34
  81.6 2.3 %collective-permute-done.26 = bf16[72,384]{1,0:T(8,128)(2,1)S(1)} collective-permute-done((bf16[72,384]{1,0:T(8,128)(2,1)S(1)}, bf16[72,384]{1,0:T(8,128)(2,1)S(1)}, u32[]{:S(2)}, u32[]{:S(2)}) %collective-permute-start.26) | collective-permute-done | bytes 55328 | tf_op jit(solution)/shard_map/ppermute | solution.py:34
  (67 shorter events, 16.6 us)
Async XLA Ops:
  0.6 7.7 %collective-permute-start.4 = (bf16[128,1152]{1,0:T(8,128)(2,1)}, bf16[128,1152]{1,0:T(8,128)(2,1)S(1)}, u32[]{:S(2)}, u32[]{:S(2)}) collective-permute-start(bf16[128,1152]{1,0:T(8,128)(2,1)} %refs_0_.1), channel_id=1, source_target_pairs={{0,4},{4,0},{1,5},{5,1},{2,6},{6,2},{3,7},{7,3},{8,12},{12,8},{9,1... | collective-permute-start | bytes 884744 | tf_op jit(solution)/shard_map/ppermute | solution.py:34
  1.1 8.7 %collective-permute-start.5 = (bf16[128,1152]{1,0:T(8,128)(2,1)}, bf16[128,1152]{1,0:T(8,128)(2,1)S(1)}, u32[]{:S(2)}, u32[]{:S(2)}) collective-permute-start(bf16[128,1152]{1,0:T(8,128)(2,1)} %refs_1_.1), channel_id=1, source_target_pairs={{0,4},{4,0},{1,5},{5,1},{2,6},{6,2},{3,7},{7,3},{8,12},{12,8},{9,1... | collective-permute-start | bytes 884744 | tf_op jit(solution)/shard_map/ppermute | solution.py:34
  1.2 16.6 %collective-permute-start = (bf16[128,1152]{1,0:T(8,128)(2,1)}, bf16[128,1152]{1,0:T(8,128)(2,1)S(1)}, u32[]{:S(2)}, u32[]{:S(2)}) collective-permute-start(bf16[128,1152]{1,0:T(8,128)(2,1)} %refs_0_.1), channel_id=1, source_target_pairs={{0,1},{4,5},{1,0},{5,4},{2,3},{6,7},{3,2},{7,6},{8,9},{12,13},{9,8... | collective-permute-start | bytes 884744 | tf_op jit(solution)/shard_map/ppermute | solution.py:34
  4.2 16.2 %collective-permute-start.1 = (bf16[128,1152]{1,0:T(8,128)(2,1)}, bf16[128,1152]{1,0:T(8,128)(2,1)S(1)}, u32[]{:S(2)}, u32[]{:S(2)}) collective-permute-start(bf16[128,1152]{1,0:T(8,128)(2,1)} %refs_0_.1), channel_id=1, source_target_pairs={{0,2},{4,6},{1,3},{5,7},{2,0},{6,4},{3,1},{7,5},{8,10},{12,14},{9,... | collective-permute-start | bytes 884744 | tf_op jit(solution)/shard_map/ppermute | solution.py:34
  6.8 13.6 %collective-permute-start.2 = (bf16[128,1152]{1,0:T(8,128)(2,1)}, bf16[128,1152]{1,0:T(8,128)(2,1)S(1)}, u32[]{:S(2)}, u32[]{:S(2)}) collective-permute-start(bf16[128,1152]{1,0:T(8,128)(2,1)} %refs_1_.1), channel_id=1, source_target_pairs={{0,8},{4,12},{1,9},{5,13},{2,10},{6,14},{3,11},{7,15},{8,0},{12,4}... | collective-permute-start | bytes 884744 | tf_op jit(solution)/shard_map/ppermute | solution.py:34
  8.3 12.1 %collective-permute-start.3 = (bf16[128,1152]{1,0:T(8,128)(2,1)}, bf16[128,1152]{1,0:T(8,128)(2,1)S(1)}, u32[]{:S(2)}, u32[]{:S(2)}) collective-permute-start(bf16[128,1152]{1,0:T(8,128)(2,1)} %refs_1_.1), channel_id=1, source_target_pairs={{0,16},{4,20},{1,17},{5,21},{2,18},{6,22},{3,19},{7,23},{8,24},{12... | collective-permute-start | bytes 884744 | tf_op jit(solution)/shard_map/ppermute | solution.py:34
  20.4 3.1 %collective-permute-start.11 = (bf16[128,1152]{1,0:T(8,128)(2,1)S(1)}, bf16[128,1152]{1,0:T(8,128)(2,1)S(1)}, u32[]{:S(2)}, u32[]{:S(2)}) collective-permute-start(bf16[128,1152]{1,0:T(8,128)(2,1)S(1)} %collective-permute-done.3.refs_1_), channel_id=1, source_target_pairs={{0,4},{4,0},{1,5},{5,1},{2,6},{6,2},{3,7},{7,3},{8,12},{12,8},{9,1... | collective-permute-start | bytes 884744 | tf_op jit(solution)/shard_map/ppermute | solution.py:34
  21.0 4.9 %collective-permute-start.8 = (bf16[128,1152]{1,0:T(8,128)(2,1)S(1)}, bf16[128,1152]{1,0:T(8,128)(2,1)S(1)}, u32[]{:S(2)}, u32[]{:S(2)}) collective-permute-start(bf16[128,1152]{1,0:T(8,128)(2,1)S(1)} %collective-permute-done.refs_0_), channel_id=1, source_target_pairs={{0,4},{4,0},{1,5},{5,1},{2,6},{6,2},{3,7},{7,3},{8,12},{12,8},{9,1... | collective-permute-start | bytes 884744 | tf_op jit(solution)/shard_map/ppermute | solution.py:34
  21.0 4.8 %collective-permute-start.9 = (bf16[128,1152]{1,0:T(8,128)(2,1)S(1)}, bf16[128,1152]{1,0:T(8,128)(2,1)S(1)}, u32[]{:S(2)}, u32[]{:S(2)}) collective-permute-start(bf16[128,1152]{1,0:T(8,128)(2,1)S(1)} %collective-permute-done.2.refs_1_), channel_id=1, source_target_pairs={{0,4},{4,0},{1,5},{5,1},{2,6},{6,2},{3,7},{7,3},{8,12},{12,8},{9,1... | collective-permute-start | bytes 884744 | tf_op jit(solution)/shard_map/ppermute | solution.py:34
  21.5 9.0 %collective-permute-start.6 = (bf16[128,1152]{1,0:T(8,128)(2,1)S(1)}, bf16[128,1152]{1,0:T(8,128)(2,1)S(1)}, u32[]{:S(2)}, u32[]{:S(2)}) collective-permute-start(bf16[128,1152]{1,0:T(8,128)(2,1)S(1)} %collective-permute-done.1.refs_0_), channel_id=1, source_target_pairs={{0,1},{4,5},{1,0},{5,4},{2,3},{6,7},{3,2},{7,6},{8,9},{12,13},{9,8... | collective-permute-start | bytes 884744 | tf_op jit(solution)/shard_map/ppermute | solution.py:34
  22.0 9.1 %collective-permute-start.7 = (bf16[128,1152]{1,0:T(8,128)(2,1)S(1)}, bf16[128,1152]{1,0:T(8,128)(2,1)S(1)}, u32[]{:S(2)}, u32[]{:S(2)}) collective-permute-start(bf16[128,1152]{1,0:T(8,128)(2,1)S(1)} %collective-permute-done.3.refs_1_), channel_id=1, source_target_pairs={{0,8},{4,12},{1,9},{5,13},{2,10},{6,14},{3,11},{7,15},{8,0},{12,4}... | collective-permute-start | bytes 884744 | tf_op jit(solution)/shard_map/ppermute | solution.py:34
  31.1 2.0 %collective-permute-start.13 = (bf16[128,1152]{1,0:T(8,128)(2,1)S(1)}, bf16[128,1152]{1,0:T(8,128)(2,1)S(1)}, u32[]{:S(2)}, u32[]{:S(2)}) collective-permute-start(bf16[128,1152]{1,0:T(8,128)(2,1)S(1)} %collective-permute-done.7.refs_1_), channel_id=1, source_target_pairs={{0,4},{4,0},{1,5},{5,1},{2,6},{6,2},{3,7},{7,3},{8,12},{12,8},{9,1... | collective-permute-start | bytes 884744 | tf_op jit(solution)/shard_map/ppermute | solution.py:34
  50.2 12.3 %collective-permute-start.19 = (bf16[576,384]{1,0:T(8,128)(2,1)S(1)}, bf16[576,384]{1,0:T(8,128)(2,1)S(1)}, u32[]{:S(2)}, u32[]{:S(2)}) collective-permute-start(bf16[576,384]{1,0:T(8,128)(2,1)S(1)} %get-tuple-element.114), channel_id=1, source_target_pairs={{0,16},{4,20},{1,17},{5,21},{2,18},{6,22},{3,19},{7,23},{8,24},{12... | collective-permute-start | bytes 1327112 | tf_op jit(solution)/shard_map/ppermute | solution.py:34
  51.8 12.1 %collective-permute-start.14 = (bf16[584,384]{1,0:T(8,128)(2,1)S(1)}, bf16[584,384]{1,0:T(8,128)(2,1)S(1)}, u32[]{:S(2)}, u32[]{:S(2)}) collective-permute-start(bf16[584,384]{1,0:T(8,128)(2,1)S(1)} %get-tuple-element.102), channel_id=1, source_target_pairs={{0,8},{4,12},{1,9},{5,13},{2,10},{6,14},{3,11},{7,15},{8,0},{12,4}... | collective-permute-start | bytes 1345544 | tf_op jit(solution)/shard_map/ppermute | solution.py:34
  53.3 12.2 %collective-permute-start.23 = (bf16[576,384]{1,0:T(8,128)(2,1)S(1)}, bf16[576,384]{1,0:T(8,128)(2,1)S(1)}, u32[]{:S(2)}, u32[]{:S(2)}) collective-permute-start(bf16[576,384]{1,0:T(8,128)(2,1)S(1)} %get-tuple-element.122), channel_id=1, source_target_pairs={{0,1},{4,5},{1,0},{5,4},{2,3},{6,7},{3,2},{7,6},{8,9},{12,13},{9,8... | collective-permute-start | bytes 1327112 | tf_op jit(solution)/shard_map/ppermute | solution.py:34
  62.5 7.1 %collective-permute-start.20 = (bf16[288,384]{1,0:T(8,128)(2,1)S(1)}, bf16[288,384]{1,0:T(8,128)(2,1)S(1)}, u32[]{:S(2)}, u32[]{:S(2)}) collective-permute-start(bf16[288,384]{1,0:T(8,128)(2,1)S(1)} %get-tuple-element.116), channel_id=1, source_target_pairs={{0,1},{4,5},{1,0},{5,4},{2,3},{6,7},{3,2},{7,6},{8,9},{12,13},{9,8... | collective-permute-start | bytes 663560 | tf_op jit(solution)/shard_map/ppermute | solution.py:34
  63.9 7.0 %collective-permute-start.15 = (bf16[296,384]{1,0:T(8,128)(2,1)S(1)}, bf16[296,384]{1,0:T(8,128)(2,1)S(1)}, u32[]{:S(2)}, u32[]{:S(2)}) collective-permute-start(bf16[296,384]{1,0:T(8,128)(2,1)S(1)} %get-tuple-element.105), channel_id=1, source_target_pairs={{0,16},{4,20},{1,17},{5,21},{2,18},{6,22},{3,19},{7,23},{8,24},{12... | collective-permute-start | bytes 681992 | tf_op jit(solution)/shard_map/ppermute | solution.py:34
  65.5 7.6 %collective-permute-start.24 = (bf16[288,384]{1,0:T(8,128)(2,1)S(1)}, bf16[288,384]{1,0:T(8,128)(2,1)S(1)}, u32[]{:S(2)}, u32[]{:S(2)}) collective-permute-start(bf16[288,384]{1,0:T(8,128)(2,1)S(1)} %get-tuple-element.124), channel_id=1, source_target_pairs={{0,8},{4,12},{1,9},{5,13},{2,10},{6,14},{3,11},{7,15},{8,0},{12,4}... | collective-permute-start | bytes 663560 | tf_op jit(solution)/shard_map/ppermute | solution.py:34
  69.7 5.1 %collective-permute-start.21 = (bf16[144,384]{1,0:T(8,128)(2,1)S(1)}, bf16[144,384]{1,0:T(8,128)(2,1)S(1)}, u32[]{:S(2)}, u32[]{:S(2)}) collective-permute-start(bf16[144,384]{1,0:T(8,128)(2,1)S(1)} %get-tuple-element.118), channel_id=1, source_target_pairs={{0,8},{4,12},{1,9},{5,13},{2,10},{6,14},{3,11},{7,15},{8,0},{12,4}... | collective-permute-start | bytes 331784 | tf_op jit(solution)/shard_map/ppermute | solution.py:34
  71.0 8.9 %collective-permute-start.16 = (bf16[152,384]{1,0:T(8,128)(2,1)S(1)}, bf16[152,384]{1,0:T(8,128)(2,1)S(1)}, u32[]{:S(2)}, u32[]{:S(2)}) collective-permute-start(bf16[152,384]{1,0:T(8,128)(2,1)S(1)} %get-tuple-element.108), channel_id=1, source_target_pairs={{0,2},{4,6},{1,3},{5,7},{2,0},{6,4},{3,1},{7,5},{8,10},{12,14},{9,... | collective-permute-start | bytes 350216 | tf_op jit(solution)/shard_map/ppermute | solution.py:34
  73.2 4.8 %collective-permute-start.25 = (bf16[144,384]{1,0:T(8,128)(2,1)S(1)}, bf16[144,384]{1,0:T(8,128)(2,1)S(1)}, u32[]{:S(2)}, u32[]{:S(2)}) collective-permute-start(bf16[144,384]{1,0:T(8,128)(2,1)S(1)} %get-tuple-element.126), channel_id=1, source_target_pairs={{0,16},{4,20},{1,17},{5,21},{2,18},{6,22},{3,19},{7,23},{8,24},{12... | collective-permute-start | bytes 331784 | tf_op jit(solution)/shard_map/ppermute | solution.py:34
  74.8 6.8 %collective-permute-start.22 = (bf16[72,384]{1,0:T(8,128)(2,1)S(1)}, bf16[72,384]{1,0:T(8,128)(2,1)S(1)}, u32[]{:S(2)}, u32[]{:S(2)}) collective-permute-start(bf16[72,384]{1,0:T(8,128)(2,1)S(1)} %get-tuple-element.120), channel_id=1, source_target_pairs={{0,2},{4,6},{1,3},{5,7},{2,0},{6,4},{3,1},{7,5},{8,10},{12,14},{9,... | collective-permute-start | bytes 165896 | tf_op jit(solution)/shard_map/ppermute | solution.py:34
  78.0 5.8 %collective-permute-start.26 = (bf16[72,384]{1,0:T(8,128)(2,1)S(1)}, bf16[72,384]{1,0:T(8,128)(2,1)S(1)}, u32[]{:S(2)}, u32[]{:S(2)}) collective-permute-start(bf16[72,384]{1,0:T(8,128)(2,1)S(1)} %get-tuple-element.128), channel_id=1, source_target_pairs={{0,2},{4,6},{1,3},{5,7},{2,0},{6,4},{3,1},{7,5},{8,10},{12,14},{9,... | collective-permute-start | bytes 165896 | tf_op jit(solution)/shard_map/ppermute | solution.py:34
  79.9 4.4 %collective-permute-start.17 = (bf16[80,384]{1,0:T(8,128)(2,1)S(1)}, bf16[80,384]{1,0:T(8,128)(2,1)S(1)}, u32[]{:S(2)}, u32[]{:S(2)}) collective-permute-start(bf16[80,384]{1,0:T(8,128)(2,1)S(1)} %get-tuple-element.111), channel_id=1, source_target_pairs={{0,1},{4,5},{1,0},{5,4},{2,3},{6,7},{3,2},{7,6},{8,9},{12,13},{9,8... | collective-permute-start | bytes 184328 | tf_op jit(solution)/shard_map/ppermute | solution.py:34
  (9 other events, 19.2 us)

commit v8 on v7

--- a/solution.py
+++ b/solution.py
@@ -55,6 +55,15 @@
 
 def this_core():
     return lax.rem(lax.axis_index("dp"), 2)
+
+
+def load_projections(image_proj, text_proj, projs, sems):
+    core = this_core()
+    own = pltpu.make_async_copy(image_proj, projs.at[core], sems.at[0])
+    other = pltpu.make_async_copy(text_proj, projs.at[1 - core], sems.at[1])
+    own.start()
+    other.start()
+    return [own, other]
 
 
 def by_role(image_proj, text_proj, body):
@@ -164,7 +173,7 @@
     other_halves, refs = refs[: side - 1], refs[side - 1 :]
     orders = part_orders(side)
     results, refs = refs[: 2 * len(orders)], refs[2 * len(orders) :]
-    stats, last, feats, units, inverses, other_half, dy, grad, pieces, moving, sems = refs
+    stats, projs, last, feats, units, inverses, other_half, dy, grad, pieces, moving, sems = refs
     rows, width = dy.shape
     chunk_rows = rows // side
     rest = rows - chunk_rows
@@ -173,7 +182,7 @@
     unit_row, unit_column = unit_index // side, lax.rem(unit_index, side)
     scale, bias = scalars[0], scalars[1]
 
-    count = 4
+    count = 6
 
     def start(source, target):
         nonlocal count
@@ -185,7 +194,8 @@
     def places(i):
         return pl.ds(i * chunk_rows, chunk_rows)
 
-    first_copies = load_chunk(last_shards, last, sems.at[pl.ds(0, 4)])
+    first_copies = load_chunk(last_shards, last, sems.at[pl.ds(2, 4)])
+    first_copies += load_projections(image_proj, text_proj, projs, sems.at[pl.ds(0, 2)])
     other_copies = [start(other_halves[i], other_half.at[places(i)]) for i in range(side - 1)]
     unit_copies = [start(own_units[i], units.at[places(i)]) for i in range(side - 1)]
     unit_copies += [start(own_inverses[i], inverses.at[places(i)]) for i in range(side - 1)]
@@ -193,29 +203,27 @@
 
     for copy in first_copies:
         copy.wait()
-
-    def project_last(own_proj, other_proj):
-        unit, _ = project(last[1], other_proj[...])
-        other_half[rest:, :] = unit.astype(BF16)
-        unit, inverse = project(last[0], own_proj[...])
-        units[rest:, :] = unit
-        inverses[rest:, :] = jnp.broadcast_to(inverse, (chunk_rows, 128))
-
-    by_role(image_proj, text_proj, project_last)
+    unit, _ = project(last[1], projs[1])
+    other_half[rest:, :] = unit.astype(BF16)
+    unit, inverse = project(last[0], projs[0])
+    units[rest:, :] = unit
+    inverses[rest:, :] = jnp.broadcast_to(inverse, (chunk_rows, 128))
     feats[rest:, :] = last[0]
     for copy in other_copies + unit_copies:
         copy.wait()
 
+    tile_rows = 2 * chunk_rows if rows <= 4 * chunk_rows else chunk_rows
+
     def cosines(i):
-        half = units[i * chunk_rows : (i + 1) * chunk_rows, :].astype(BF16)
+        half = units[i * tile_rows : (i + 1) * tile_rows, :].astype(BF16)
         return lax.dot_general(
             half, other_half[...], (((1,), (1,)), ((), ())), preferred_element_type=F32
         )
 
     total = None
     cosine = cosines(0)
-    for i in range(side):
-        following = cosines(i + 1) if i + 1 < side else None
+    for i in range(rows // tile_rows):
+        following = cosines(i + 1) if i + 1 < rows // tile_rows else None
         if i == 0:
             terms = [
                 pair_terms(cosine[:, :chunk_rows], scale, bias, True),
@@ -230,7 +238,7 @@
         total = sums if total is None else total + sums
         inner = jnp.sum(half_grads.astype(F32) * cosine, axis=-1, keepdims=True)
         grads = jnp.dot(half_grads, other_half[...], preferred_element_type=F32)
-        place = slice(i * chunk_rows, (i + 1) * chunk_rows)
+        place = slice(i * tile_rows, (i + 1) * tile_rows)
         grads = (grads - units[place, :] * inner) * (scale * inverses[place, 0:1])
         dy[place, :] = grads.astype(BF16)
         cosine = following
@@ -325,15 +333,16 @@
         out_shape.append(jax.ShapeDtypeStruct((half_rows if g else half_rows + 8, part_width), BF16))
     out_shape.append(jax.ShapeDtypeStruct((8, part_width), F32))
     needed = 6 * width * width + 14 * rows * width + 16 * half_rows * width
-    needed += 12 * chunk_rows * rows + 2 * 1024 * 1024
+    needed += 14 * chunk_rows * rows + 2 * 1024 * 1024
     return pl.pallas_call(
         functools.partial(block_kernel, side, layout.mp),
         out_shape=out_shape,
         in_specs=[pl.BlockSpec(memory_space=pltpu.SMEM)]
-        + [vmem] * 2
+        + [pl.BlockSpec(memory_space=pltpu.HBM)] * 2
         + [anywhere] * (len(operands) - 2),
         out_specs=[vmem] * len(out_shape),
         scratch_shapes=[
+            pltpu.VMEM((2, width, width), BF16),
             pltpu.VMEM((2, chunk_rows, width), BF16),
             pltpu.VMEM((rows, width), BF16),
             pltpu.VMEM((rows, width), F32),
@@ -343,7 +352,7 @@
             pltpu.VMEM((width, width), F32),
             pltpu.VMEM((2 * half_rows, width), F32),
             pltpu.VMEM((half_rows + 8, part_width), F32),
-            pltpu.SemaphoreType.DMA((len(operands) - 2,)),
+            pltpu.SemaphoreType.DMA((len(operands),)),
         ],
         compiler_params=pltpu.CompilerParams(vmem_limit_bytes=min(needed, 60 * 1024 * 1024)),
         cost_estimate=pl.CostEstimate(
@@ -368,6 +377,30 @@
         stats[...] = jnp.broadcast_to(sums, stats.shape)
         moved = jnp.concatenate([moved, stat_rows(sums, own.shape[1])], axis=0)
     message[...] = moved.astype(BF16)
+
+
+def halve_two_kernel(own_a, arrived_a, own_b, arrived_b, keep_a, keep_b, message):
+    moved = []
+    for own, arrived, keep in ((own_a, arrived_a, keep_a), (own_b, arrived_b, keep_b)):
+        half = keep.shape[0]
+        total = own[...] + arrived[...].astype(F32)
+        keep[...] = total[:half, :]
+        moved.append(total[half:, :])
+    message[...] = jnp.concatenate(moved, axis=0).astype(BF16)
+
+
+def halve_two(own_a, arrived_a, own_b, arrived_b):
+    rows, width = own_a.shape
+    vmem = pl.BlockSpec(memory_space=pltpu.VMEM)
+    return pl.pallas_call(
+        halve_two_kernel,
+        out_shape=[jax.ShapeDtypeStruct((rows // 2, width), F32)] * 2
+        + [jax.ShapeDtypeStruct((rows, width), BF16)],
+        in_specs=[vmem] * 4,
+        out_specs=[vmem] * 3,
+        compiler_params=pltpu.CompilerParams(vmem_limit_bytes=12 * 1024 * 1024),
+        name="halve_two",
+    )(own_a, arrived_a, own_b, arrived_b)
 
 
 def halve(own, arrived, *own_stats):
@@ -445,14 +478,18 @@
     stats = [results[-1]]
 
     steps = len(orders[0])
-    for step in range(steps):
+    for step in range(steps - 1):
         arrived = [
             layout.exchange(message, *order[step]) for message, order in zip(messages, orders)
         ]
-        if step + 1 < steps:
-            for g in range(len(orders)):
-                *some, owns[g], messages[g] = halve(owns[g], arrived[g], *([] if g else stats))
-                stats = some if g == 0 else stats
+        *stats, owns[0], messages[0] = halve(owns[0], arrived[0], *stats)
+        if step + 2 < steps:
+            for g in (1, 2):
+                owns[g], messages[g] = halve(owns[g], arrived[g])
+    owns[1], owns[2], message = halve_two(owns[1], arrived[1], owns[2], arrived[2])
+    two = layout.exchange(message, *orders[1][-1])
+    piece_rows = owns[1].shape[0]
+    arrived = [layout.exchange(messages[0], *orders[0][-1]), two[:piece_rows], two[piece_rows:]]
     last_rows = 2 * out_rows
     total = jnp.concatenate(
         [own[:last_rows] + x[:last_rows].astype(F32) for own, x in zip(owns, arrived)], axis=1

time: 87.4 us -> 87.1 us (level)
  waiting for transfers between devices: 23.6 us -> 24.9 us
  Pallas kernels: 24.6 us -> 23.7 us
  starting transfers between devices: 29.8 us -> 28.9 us
    ppermute x28 -> x27, waiting for transfers between devices: 23.6 us -> 24.9 us  [send(): return lax.ppermute(value, AXES, pairs)]
    ppermute x28 -> x27, starting transfers between devices: 29.8 us -> 28.9 us  [send(): return lax.ppermute(value, AXES, pairs)]
  transfers between devices with their start and end apart: 28 -> 27, of which waited for: 15 -> 14; matrix products, arithmetic and copies ran while one was open for 1% -> 1% of each run, Pallas kernels for 9% -> 9%
where the time goes in v8:
time: 87.1 us; the launch traced here: 86.8 us
  starting transfers between devices  28.9 us (33%)
  waiting for transfers between devices  24.9 us (29%)
  Pallas kernels  23.7 us (27%)
  local copies, waits for them, and re-layouts  6.02 us (7%)
  between operations  2.16 us (2%)
  other arithmetic  1.09 us (1%)
    ppermute x27, starting transfers between devices, send(): return lax.ppermute(value, AXES, pairs)  28.9 us
    ppermute x27, waiting for transfers between devices, send(): return lax.ppermute(value, AXES, pairs)  24.9 us
    pallas_call x1, Pallas kernels, block_grads(): pl.pallas_call(functools.partial(block_kernel, side, layout.mp), out_shap...  16.3 us
    pallas_call x3, Pallas kernels, project_chunk(): pl.pallas_call(project_kernel, out_shape=[jax.ShapeDtypeStruct((rows, wid...  6.91 us
    unnamed x10, local copies, waits for them, and re-layouts  5.43 us
  transfers between devices with their start and end apart: 27, of which 14 were waited for; matrix products, arithmetic and copies ran while one was open for 1% of the time, Pallas kernels for 9%

profile of v8, /device:TPU:0, one launch (start us, length us, event | category | flops | bytes accessed | tf_op | source)
XLA Modules:
  0.0 86.8 jit_solution(14017723746126979537)
XLA Ops:
  1.2 3.0 %collective-permute-start = (bf16[128,1152]{1,0:T(8,128)(2,1)}, bf16[128,1152]{1,0:T(8,128)(2,1)S(1)}, u32[]{:S(2)}, u32[]{:S(2)}) collective-permute-start(bf16[128,1152]{1,0:T(8,128)(2,1)} %refs_0_.1), channel_id=1, source_target_pairs={{0,1},{4,5},{1,0},{5,4},{2,3},{6,7},{3,2},{7,6},{8,9},{12,13},{9,8... | collective-permute-start | bytes 884744 | tf_op jit(solution)/shard_map/ppermute | solution.py:34
  4.2 2.6 %collective-permute-start.1 = (bf16[128,1152]{1,0:T(8,128)(2,1)}, bf16[128,1152]{1,0:T(8,128)(2,1)S(1)}, u32[]{:S(2)}, u32[]{:S(2)}) collective-permute-start(bf16[128,1152]{1,0:T(8,128)(2,1)} %refs_0_.1), channel_id=1, source_target_pairs={{0,2},{4,6},{1,3},{5,7},{2,0},{6,4},{3,1},{7,5},{8,10},{12,14},{9,... | collective-permute-start | bytes 884744 | tf_op jit(solution)/shard_map/ppermute | solution.py:34
  8.3 1.5 %collective-permute-start.3 = (bf16[128,1152]{1,0:T(8,128)(2,1)}, bf16[128,1152]{1,0:T(8,128)(2,1)S(1)}, u32[]{:S(2)}, u32[]{:S(2)}) collective-permute-start(bf16[128,1152]{1,0:T(8,128)(2,1)} %refs_1_.1), channel_id=1, source_target_pairs={{0,16},{4,20},{1,17},{5,21},{2,18},{6,22},{3,19},{7,23},{8,24},{12... | collective-permute-start | bytes 884744 | tf_op jit(solution)/shard_map/ppermute | solution.py:34
  9.8 1.7 %copy-done = bf16[1152,1152]{1,0:T(8,128)(2,1)S(1)} copy-done((bf16[1152,1152]{1,0:T(8,128)(2,1)S(1)}, bf16[1152,1152]{1,0:T(8,128)(2,1)}, u32[]{:S(2)}) %copy-start) | copy-done | bytes 2654232
  11.6 1.7 %copy-done.2 = bf16[1152,1152]{1,0:T(8,128)(2,1)S(1)} copy-done((bf16[1152,1152]{1,0:T(8,128)(2,1)S(1)}, bf16[1152,1152]{1,0:T(8,128)(2,1)}, u32[]{:S(2)}) %copy-start.2) | copy-done | bytes 2654232
  15.3 2.3 %project.3 = (bf16[256,1152]{1,0:T(8,128)(2,1)S(1)}, f32[256,1152]{1,0:T(8,128)S(1)}, f32[256,128]{1,0:T(8,128)S(1)}, bf16[256,1152]{1,0:T(8,128)(2,1)S(1)}) custom-call(bf16[1152,1152]{1,0:T(8,128)(2,1)S(1)} %copy-done, bf16[1152,1152]{1,0:T(8,128)(2,1)S(1)} %copy-done.2, bf16[128,1152]{1,0:T(8,128)(2,1)S(1)} %copy-done.3, bf16[128,1152]{1,0:T(8,128)(2,1)S(1)} %copy-done.4, ...), custom_call_target="tpu_custom_call" | custom-call | flops 1358954496 | bytes 8847360 | tf_op jit(solution)/shard_map/project/pallas_call | solution.py:121
  17.9 2.6 %collective-permute-done.1.refs_0_ = bf16[128,1152]{1,0:T(8,128)(2,1)S(1)} collective-permute-done((bf16[128,1152]{1,0:T(8,128)(2,1)}, bf16[128,1152]{1,0:T(8,128)(2,1)S(1)}, u32[]{:S(2)}, u32[]{:S(2)}) %collective-permute-start.1) | collective-permute-done | bytes 294944 | tf_op jit(solution)/shard_map/ppermute | solution.py:34
  22.0 1.5 %collective-permute-start.7 = (bf16[128,1152]{1,0:T(8,128)(2,1)S(1)}, bf16[128,1152]{1,0:T(8,128)(2,1)S(1)}, u32[]{:S(2)}, u32[]{:S(2)}) collective-permute-start(bf16[128,1152]{1,0:T(8,128)(2,1)S(1)} %collective-permute-done.3.refs_1_), channel_id=1, source_target_pairs={{0,8},{4,12},{1,9},{5,13},{2,10},{6,14},{3,11},{7,15},{8,0},{12,4}... | collective-permute-start | bytes 884744 | tf_op jit(solution)/shard_map/ppermute | solution.py:34
  23.5 2.3 %project.5 = (bf16[256,1152]{1,0:T(8,128)(2,1)S(1)}, f32[256,1152]{1,0:T(8,128)S(1)}, f32[256,128]{1,0:T(8,128)S(1)}, bf16[256,1152]{1,0:T(8,128)(2,1)S(1)}) custom-call(bf16[1152,1152]{1,0:T(8,128)(2,1)S(1)} %copy-done, bf16[1152,1152]{1,0:T(8,128)(2,1)S(1)} %copy-done.2, bf16[128,1152]{1,0:T(8,128)(2,1)S(1)} %collective-permute-done.1.refs_0_, ...), custom_call_target="tpu_custom_call" | custom-call | flops 1358954496 | bytes 8847360 | tf_op jit(solution)/shard_map/project/pallas_call | solution.py:121
  25.9 2.3 %project.4 = (bf16[256,1152]{1,0:T(8,128)(2,1)S(1)}, f32[256,1152]{1,0:T(8,128)S(1)}, f32[256,128]{1,0:T(8,128)S(1)}, bf16[256,1152]{1,0:T(8,128)(2,1)S(1)}) custom-call(bf16[1152,1152]{1,0:T(8,128)(2,1)S(1)} %copy-done, bf16[1152,1152]{1,0:T(8,128)(2,1)S(1)} %copy-done.2, bf16[128,1152]{1,0:T(8,128)(2,1)S(1)} %collective-permute-done.refs_0_, ...), custom_call_target="tpu_custom_call" | custom-call | flops 1358954496 | bytes 8847360 | tf_op jit(solution)/shard_map/project/pallas_call | solution.py:121
  28.2 2.3 %collective-permute-done.6.refs_0_ = bf16[128,1152]{1,0:T(8,128)(2,1)S(1)} collective-permute-done((bf16[128,1152]{1,0:T(8,128)(2,1)S(1)}, bf16[128,1152]{1,0:T(8,128)(2,1)S(1)}, u32[]{:S(2)}, u32[]{:S(2)}) %collective-permute-start.6) | collective-permute-done | bytes 294944 | tf_op jit(solution)/shard_map/ppermute | solution.py:34
  33.1 16.3 %block.1 = (f32[576,384]{1,0:T(8,128)S(1)}, bf16[584,384]{1,0:T(8,128)(2,1)S(1)}, f32[576,384]{1,0:T(8,128)S(1)}, bf16[576,384]{1,0:T(8,128)(2,1)S(1)}, f32[576,...) custom-call(f32[2]{0:T(128)S(1)} %pad_maximum_fusion.1.scalars, ...), custom_call_target="tpu_custom_call" | custom-call | flops 8908701696 | bytes 19464192 | tf_op jit(solution)/shard_map/block/pallas_call | solution.py:337
  49.4 1.6 %collective-permute-start.14 = (bf16[584,384]{1,0:T(8,128)(2,1)S(1)}, bf16[584,384]{1,0:T(8,128)(2,1)S(1)}, u32[]{:S(2)}, u32[]{:S(2)}) collective-permute-start(bf16[584,384]{1,0:T(8,128)(2,1)S(1)} %get-tuple-element.101), channel_id=1, source_target_pairs={{0,8},{4,12},{1,9},{5,13},{2,10},{6,14},{3,11},{7,15},{8,0},{12,4}... | collective-permute-start | bytes 1345544 | tf_op jit(solution)/shard_map/ppermute | solution.py:34
  52.1 1.5 %collective-permute-start.19 = (bf16[576,384]{1,0:T(8,128)(2,1)S(1)}, bf16[576,384]{1,0:T(8,128)(2,1)S(1)}, u32[]{:S(2)}, u32[]{:S(2)}) collective-permute-start(bf16[576,384]{1,0:T(8,128)(2,1)S(1)} %get-tuple-element.113), channel_id=1, source_target_pairs={{0,16},{4,20},{1,17},{5,21},{2,18},{6,22},{3,19},{7,23},{8,24},{12... | collective-permute-start | bytes 1327112 | tf_op jit(solution)/shard_map/ppermute | solution.py:34
  53.6 8.2 %collective-permute-done.14.arrived = bf16[584,384]{1,0:T(8,128)(2,1)S(1)} collective-permute-done((bf16[584,384]{1,0:T(8,128)(2,1)S(1)}, bf16[584,384]{1,0:T(8,128)(2,1)S(1)}, u32[]{:S(2)}, u32[]{:S(2)}) %collective-permute-start.14) | collective-permute-done | bytes 448544 | tf_op jit(solution)/shard_map/ppermute | solution.py:34
  61.9 1.6 %collective-permute-start.15 = (bf16[296,384]{1,0:T(8,128)(2,1)S(1)}, bf16[296,384]{1,0:T(8,128)(2,1)S(1)}, u32[]{:S(2)}, u32[]{:S(2)}) collective-permute-start(bf16[296,384]{1,0:T(8,128)(2,1)S(1)} %get-tuple-element.104), channel_id=1, source_target_pairs={{0,16},{4,20},{1,17},{5,21},{2,18},{6,22},{3,19},{7,23},{8,24},{12... | collective-permute-start | bytes 681992 | tf_op jit(solution)/shard_map/ppermute | solution.py:34
  63.6 1.6 %collective-permute-start.23 = (bf16[288,384]{1,0:T(8,128)(2,1)S(1)}, bf16[288,384]{1,0:T(8,128)(2,1)S(1)}, u32[]{:S(2)}, u32[]{:S(2)}) collective-permute-start(bf16[288,384]{1,0:T(8,128)(2,1)S(1)} %get-tuple-element.121), channel_id=1, source_target_pairs={{0,8},{4,12},{1,9},{5,13},{2,10},{6,14},{3,11},{7,15},{8,0},{12,4}... | collective-permute-start | bytes 663560 | tf_op jit(solution)/shard_map/ppermute | solution.py:34
  66.4 2.3 %collective-permute-done.15.arrived = bf16[296,384]{1,0:T(8,128)(2,1)S(1)} collective-permute-done((bf16[296,384]{1,0:T(8,128)(2,1)S(1)}, bf16[296,384]{1,0:T(8,128)(2,1)S(1)}, u32[]{:S(2)}, u32[]{:S(2)}) %collective-permute-start.15) | collective-permute-done | bytes 227360 | tf_op jit(solution)/shard_map/ppermute | solution.py:34
  68.8 2.2 %collective-permute-start.16 = (bf16[152,384]{1,0:T(8,128)(2,1)S(1)}, bf16[152,384]{1,0:T(8,128)(2,1)S(1)}, u32[]{:S(2)}, u32[]{:S(2)}) collective-permute-start(bf16[152,384]{1,0:T(8,128)(2,1)S(1)} %get-tuple-element.107), channel_id=1, source_target_pairs={{0,2},{4,6},{1,3},{5,7},{2,0},{6,4},{3,1},{7,5},{8,10},{12,14},{9,... | collective-permute-start | bytes 350216 | tf_op jit(solution)/shard_map/ppermute | solution.py:34
  71.0 1.6 %collective-permute-start.24 = (bf16[144,384]{1,0:T(8,128)(2,1)S(1)}, bf16[144,384]{1,0:T(8,128)(2,1)S(1)}, u32[]{:S(2)}, u32[]{:S(2)}) collective-permute-start(bf16[144,384]{1,0:T(8,128)(2,1)S(1)} %get-tuple-element.123), channel_id=1, source_target_pairs={{0,16},{4,20},{1,17},{5,21},{2,18},{6,22},{3,19},{7,23},{8,24},{12... | collective-permute-start | bytes 331784 | tf_op jit(solution)/shard_map/ppermute | solution.py:34
  72.7 1.6 %collective-permute-start.21 = (bf16[144,384]{1,0:T(8,128)(2,1)S(1)}, bf16[144,384]{1,0:T(8,128)(2,1)S(1)}, u32[]{:S(2)}, u32[]{:S(2)}) collective-permute-start(bf16[144,384]{1,0:T(8,128)(2,1)S(1)} %get-tuple-element.117), channel_id=1, source_target_pairs={{0,8},{4,12},{1,9},{5,13},{2,10},{6,14},{3,11},{7,15},{8,0},{12,4}... | collective-permute-start | bytes 331784 | tf_op jit(solution)/shard_map/ppermute | solution.py:34
  74.2 1.9 %collective-permute-done.16.arrived = bf16[152,384]{1,0:T(8,128)(2,1)S(1)} collective-permute-done((bf16[152,384]{1,0:T(8,128)(2,1)S(1)}, bf16[152,384]{1,0:T(8,128)(2,1)S(1)}, u32[]{:S(2)}, u32[]{:S(2)}) %collective-permute-start.16) | collective-permute-done | bytes 116768 | tf_op jit(solution)/shard_map/ppermute | solution.py:34
  77.5 2.2 %collective-permute-start.25 = (bf16[144,384]{1,0:T(8,128)(2,1)S(1)}, bf16[144,384]{1,0:T(8,128)(2,1)S(1)}, u32[]{:S(2)}, u32[]{:S(2)}) collective-permute-start(bf16[144,384]{1,0:T(8,128)(2,1)S(1)} %get-tuple-element.125), channel_id=1, source_target_pairs={{0,2},{4,6},{1,3},{5,7},{2,0},{6,4},{3,1},{7,5},{8,10},{12,14},{9,... | collective-permute-start | bytes 331784 | tf_op jit(solution)/shard_map/ppermute | solution.py:34
  82.5 2.0 %collective-permute-done.25 = bf16[144,384]{1,0:T(8,128)(2,1)S(1)} collective-permute-done((bf16[144,384]{1,0:T(8,128)(2,1)S(1)}, bf16[144,384]{1,0:T(8,128)(2,1)S(1)}, u32[]{:S(2)}, u32[]{:S(2)}) %collective-permute-start.25) | collective-permute-done | bytes 110624 | tf_op jit(solution)/shard_map/ppermute | solution.py:34
  (63 shorter events, 16.4 us)
Async XLA Ops:
  0.6 7.7 %collective-permute-start.4 = (bf16[128,1152]{1,0:T(8,128)(2,1)}, bf16[128,1152]{1,0:T(8,128)(2,1)S(1)}, u32[]{:S(2)}, u32[]{:S(2)}) collective-permute-start(bf16[128,1152]{1,0:T(8,128)(2,1)} %refs_0_.1), channel_id=1, source_target_pairs={{0,4},{4,0},{1,5},{5,1},{2,6},{6,2},{3,7},{7,3},{8,12},{12,8},{9,1... | collective-permute-start | bytes 884744 | tf_op jit(solution)/shard_map/ppermute | solution.py:34
  1.1 8.7 %collective-permute-start.5 = (bf16[128,1152]{1,0:T(8,128)(2,1)}, bf16[128,1152]{1,0:T(8,128)(2,1)S(1)}, u32[]{:S(2)}, u32[]{:S(2)}) collective-permute-start(bf16[128,1152]{1,0:T(8,128)(2,1)} %refs_1_.1), channel_id=1, source_target_pairs={{0,4},{4,0},{1,5},{5,1},{2,6},{6,2},{3,7},{7,3},{8,12},{12,8},{9,1... | collective-permute-start | bytes 884744 | tf_op jit(solution)/shard_map/ppermute | solution.py:34
  1.2 16.6 %collective-permute-start = (bf16[128,1152]{1,0:T(8,128)(2,1)}, bf16[128,1152]{1,0:T(8,128)(2,1)S(1)}, u32[]{:S(2)}, u32[]{:S(2)}) collective-permute-start(bf16[128,1152]{1,0:T(8,128)(2,1)} %refs_0_.1), channel_id=1, source_target_pairs={{0,1},{4,5},{1,0},{5,4},{2,3},{6,7},{3,2},{7,6},{8,9},{12,13},{9,8... | collective-permute-start | bytes 884744 | tf_op jit(solution)/shard_map/ppermute | solution.py:34
  4.2 16.2 %collective-permute-start.1 = (bf16[128,1152]{1,0:T(8,128)(2,1)}, bf16[128,1152]{1,0:T(8,128)(2,1)S(1)}, u32[]{:S(2)}, u32[]{:S(2)}) collective-permute-start(bf16[128,1152]{1,0:T(8,128)(2,1)} %refs_0_.1), channel_id=1, source_target_pairs={{0,2},{4,6},{1,3},{5,7},{2,0},{6,4},{3,1},{7,5},{8,10},{12,14},{9,... | collective-permute-start | bytes 884744 | tf_op jit(solution)/shard_map/ppermute | solution.py:34
  6.8 13.6 %collective-permute-start.2 = (bf16[128,1152]{1,0:T(8,128)(2,1)}, bf16[128,1152]{1,0:T(8,128)(2,1)S(1)}, u32[]{:S(2)}, u32[]{:S(2)}) collective-permute-start(bf16[128,1152]{1,0:T(8,128)(2,1)} %refs_1_.1), channel_id=1, source_target_pairs={{0,8},{4,12},{1,9},{5,13},{2,10},{6,14},{3,11},{7,15},{8,0},{12,4}... | collective-permute-start | bytes 884744 | tf_op jit(solution)/shard_map/ppermute | solution.py:34
  8.3 12.1 %collective-permute-start.3 = (bf16[128,1152]{1,0:T(8,128)(2,1)}, bf16[128,1152]{1,0:T(8,128)(2,1)S(1)}, u32[]{:S(2)}, u32[]{:S(2)}) collective-permute-start(bf16[128,1152]{1,0:T(8,128)(2,1)} %refs_1_.1), channel_id=1, source_target_pairs={{0,16},{4,20},{1,17},{5,21},{2,18},{6,22},{3,19},{7,23},{8,24},{12... | collective-permute-start | bytes 884744 | tf_op jit(solution)/shard_map/ppermute | solution.py:34
  20.4 3.1 %collective-permute-start.11 = (bf16[128,1152]{1,0:T(8,128)(2,1)S(1)}, bf16[128,1152]{1,0:T(8,128)(2,1)S(1)}, u32[]{:S(2)}, u32[]{:S(2)}) collective-permute-start(bf16[128,1152]{1,0:T(8,128)(2,1)S(1)} %collective-permute-done.3.refs_1_), channel_id=1, source_target_pairs={{0,4},{4,0},{1,5},{5,1},{2,6},{6,2},{3,7},{7,3},{8,12},{12,8},{9,1... | collective-permute-start | bytes 884744 | tf_op jit(solution)/shard_map/ppermute | solution.py:34
  21.0 4.9 %collective-permute-start.8 = (bf16[128,1152]{1,0:T(8,128)(2,1)S(1)}, bf16[128,1152]{1,0:T(8,128)(2,1)S(1)}, u32[]{:S(2)}, u32[]{:S(2)}) collective-permute-start(bf16[128,1152]{1,0:T(8,128)(2,1)S(1)} %collective-permute-done.refs_0_), channel_id=1, source_target_pairs={{0,4},{4,0},{1,5},{5,1},{2,6},{6,2},{3,7},{7,3},{8,12},{12,8},{9,1... | collective-permute-start | bytes 884744 | tf_op jit(solution)/shard_map/ppermute | solution.py:34
  21.0 4.8 %collective-permute-start.9 = (bf16[128,1152]{1,0:T(8,128)(2,1)S(1)}, bf16[128,1152]{1,0:T(8,128)(2,1)S(1)}, u32[]{:S(2)}, u32[]{:S(2)}) collective-permute-start(bf16[128,1152]{1,0:T(8,128)(2,1)S(1)} %collective-permute-done.2.refs_1_), channel_id=1, source_target_pairs={{0,4},{4,0},{1,5},{5,1},{2,6},{6,2},{3,7},{7,3},{8,12},{12,8},{9,1... | collective-permute-start | bytes 884744 | tf_op jit(solution)/shard_map/ppermute | solution.py:34
  21.5 9.0 %collective-permute-start.6 = (bf16[128,1152]{1,0:T(8,128)(2,1)S(1)}, bf16[128,1152]{1,0:T(8,128)(2,1)S(1)}, u32[]{:S(2)}, u32[]{:S(2)}) collective-permute-start(bf16[128,1152]{1,0:T(8,128)(2,1)S(1)} %collective-permute-done.1.refs_0_), channel_id=1, source_target_pairs={{0,1},{4,5},{1,0},{5,4},{2,3},{6,7},{3,2},{7,6},{8,9},{12,13},{9,8... | collective-permute-start | bytes 884744 | tf_op jit(solution)/shard_map/ppermute | solution.py:34
  22.0 9.1 %collective-permute-start.7 = (bf16[128,1152]{1,0:T(8,128)(2,1)S(1)}, bf16[128,1152]{1,0:T(8,128)(2,1)S(1)}, u32[]{:S(2)}, u32[]{:S(2)}) collective-permute-start(bf16[128,1152]{1,0:T(8,128)(2,1)S(1)} %collective-permute-done.3.refs_1_), channel_id=1, source_target_pairs={{0,8},{4,12},{1,9},{5,13},{2,10},{6,14},{3,11},{7,15},{8,0},{12,4}... | collective-permute-start | bytes 884744 | tf_op jit(solution)/shard_map/ppermute | solution.py:34
  31.1 1.9 %collective-permute-start.12 = (bf16[128,1152]{1,0:T(8,128)(2,1)S(1)}, bf16[128,1152]{1,0:T(8,128)(2,1)S(1)}, u32[]{:S(2)}, u32[]{:S(2)}) collective-permute-start(bf16[128,1152]{1,0:T(8,128)(2,1)S(1)} %collective-permute-done.6.refs_0_), channel_id=1, source_target_pairs={{0,4},{4,0},{1,5},{5,1},{2,6},{6,2},{3,7},{7,3},{8,12},{12,8},{9,1... | collective-permute-start | bytes 884744 | tf_op jit(solution)/shard_map/ppermute | solution.py:34
  31.1 2.0 %collective-permute-start.13 = (bf16[128,1152]{1,0:T(8,128)(2,1)S(1)}, bf16[128,1152]{1,0:T(8,128)(2,1)S(1)}, u32[]{:S(2)}, u32[]{:S(2)}) collective-permute-start(bf16[128,1152]{1,0:T(8,128)(2,1)S(1)} %collective-permute-done.7.refs_1_), channel_id=1, source_target_pairs={{0,4},{4,0},{1,5},{5,1},{2,6},{6,2},{3,7},{7,3},{8,12},{12,8},{9,1... | collective-permute-start | bytes 884744 | tf_op jit(solution)/shard_map/ppermute | solution.py:34
  49.4 12.4 %collective-permute-start.14 = (bf16[584,384]{1,0:T(8,128)(2,1)S(1)}, bf16[584,384]{1,0:T(8,128)(2,1)S(1)}, u32[]{:S(2)}, u32[]{:S(2)}) collective-permute-start(bf16[584,384]{1,0:T(8,128)(2,1)S(1)} %get-tuple-element.101), channel_id=1, source_target_pairs={{0,8},{4,12},{1,9},{5,13},{2,10},{6,14},{3,11},{7,15},{8,0},{12,4}... | collective-permute-start | bytes 1345544 | tf_op jit(solution)/shard_map/ppermute | solution.py:34
  50.9 12.5 %collective-permute-start.22 = (bf16[576,384]{1,0:T(8,128)(2,1)S(1)}, bf16[576,384]{1,0:T(8,128)(2,1)S(1)}, u32[]{:S(2)}, u32[]{:S(2)}) collective-permute-start(bf16[576,384]{1,0:T(8,128)(2,1)S(1)} %get-tuple-element.119), channel_id=1, source_target_pairs={{0,1},{4,5},{1,0},{5,4},{2,3},{6,7},{3,2},{7,6},{8,9},{12,13},{9,8... | collective-permute-start | bytes 1327112 | tf_op jit(solution)/shard_map/ppermute | solution.py:34
  52.1 13.1 %collective-permute-start.19 = (bf16[576,384]{1,0:T(8,128)(2,1)S(1)}, bf16[576,384]{1,0:T(8,128)(2,1)S(1)}, u32[]{:S(2)}, u32[]{:S(2)}) collective-permute-start(bf16[576,384]{1,0:T(8,128)(2,1)S(1)} %get-tuple-element.113), channel_id=1, source_target_pairs={{0,16},{4,20},{1,17},{5,21},{2,18},{6,22},{3,19},{7,23},{8,24},{12... | collective-permute-start | bytes 1327112 | tf_op jit(solution)/shard_map/ppermute | solution.py:34
  61.9 6.8 %collective-permute-start.15 = (bf16[296,384]{1,0:T(8,128)(2,1)S(1)}, bf16[296,384]{1,0:T(8,128)(2,1)S(1)}, u32[]{:S(2)}, u32[]{:S(2)}) collective-permute-start(bf16[296,384]{1,0:T(8,128)(2,1)S(1)} %get-tuple-element.104), channel_id=1, source_target_pairs={{0,16},{4,20},{1,17},{5,21},{2,18},{6,22},{3,19},{7,23},{8,24},{12... | collective-permute-start | bytes 681992 | tf_op jit(solution)/shard_map/ppermute | solution.py:34
  63.6 7.4 %collective-permute-start.23 = (bf16[288,384]{1,0:T(8,128)(2,1)S(1)}, bf16[288,384]{1,0:T(8,128)(2,1)S(1)}, u32[]{:S(2)}, u32[]{:S(2)}) collective-permute-start(bf16[288,384]{1,0:T(8,128)(2,1)S(1)} %get-tuple-element.121), channel_id=1, source_target_pairs={{0,8},{4,12},{1,9},{5,13},{2,10},{6,14},{3,11},{7,15},{8,0},{12,4}... | collective-permute-start | bytes 663560 | tf_op jit(solution)/shard_map/ppermute | solution.py:34
  65.2 7.4 %collective-permute-start.20 = (bf16[288,384]{1,0:T(8,128)(2,1)S(1)}, bf16[288,384]{1,0:T(8,128)(2,1)S(1)}, u32[]{:S(2)}, u32[]{:S(2)}) collective-permute-start(bf16[288,384]{1,0:T(8,128)(2,1)S(1)} %get-tuple-element.115), channel_id=1, source_target_pairs={{0,1},{4,5},{1,0},{5,4},{2,3},{6,7},{3,2},{7,6},{8,9},{12,13},{9,8... | collective-permute-start | bytes 663560 | tf_op jit(solution)/shard_map/ppermute | solution.py:34
  68.8 7.4 %collective-permute-start.16 = (bf16[152,384]{1,0:T(8,128)(2,1)S(1)}, bf16[152,384]{1,0:T(8,128)(2,1)S(1)}, u32[]{:S(2)}, u32[]{:S(2)}) collective-permute-start(bf16[152,384]{1,0:T(8,128)(2,1)S(1)} %get-tuple-element.107), channel_id=1, source_target_pairs={{0,2},{4,6},{1,3},{5,7},{2,0},{6,4},{3,1},{7,5},{8,10},{12,14},{9,... | collective-permute-start | bytes 350216 | tf_op jit(solution)/shard_map/ppermute | solution.py:34
  71.0 5.3 %collective-permute-start.24 = (bf16[144,384]{1,0:T(8,128)(2,1)S(1)}, bf16[144,384]{1,0:T(8,128)(2,1)S(1)}, u32[]{:S(2)}, u32[]{:S(2)}) collective-permute-start(bf16[144,384]{1,0:T(8,128)(2,1)S(1)} %get-tuple-element.123), channel_id=1, source_target_pairs={{0,16},{4,20},{1,17},{5,21},{2,18},{6,22},{3,19},{7,23},{8,24},{12... | collective-permute-start | bytes 331784 | tf_op jit(solution)/shard_map/ppermute | solution.py:34
  72.7 4.8 %collective-permute-start.21 = (bf16[144,384]{1,0:T(8,128)(2,1)S(1)}, bf16[144,384]{1,0:T(8,128)(2,1)S(1)}, u32[]{:S(2)}, u32[]{:S(2)}) collective-permute-start(bf16[144,384]{1,0:T(8,128)(2,1)S(1)} %get-tuple-element.117), channel_id=1, source_target_pairs={{0,8},{4,12},{1,9},{5,13},{2,10},{6,14},{3,11},{7,15},{8,0},{12,4}... | collective-permute-start | bytes 331784 | tf_op jit(solution)/shard_map/ppermute | solution.py:34
  76.2 4.9 %collective-permute-start.17 = (bf16[80,384]{1,0:T(8,128)(2,1)S(1)}, bf16[80,384]{1,0:T(8,128)(2,1)S(1)}, u32[]{:S(2)}, u32[]{:S(2)}) collective-permute-start(bf16[80,384]{1,0:T(8,128)(2,1)S(1)} %get-tuple-element.110), channel_id=1, source_target_pairs={{0,1},{4,5},{1,0},{5,4},{2,3},{6,7},{3,2},{7,6},{8,9},{12,13},{9,8... | collective-permute-start | bytes 184328 | tf_op jit(solution)/shard_map/ppermute | solution.py:34
  77.5 6.9 %collective-permute-start.25 = (bf16[144,384]{1,0:T(8,128)(2,1)S(1)}, bf16[144,384]{1,0:T(8,128)(2,1)S(1)}, u32[]{:S(2)}, u32[]{:S(2)}) collective-permute-start(bf16[144,384]{1,0:T(8,128)(2,1)S(1)} %get-tuple-element.125), channel_id=1, source_target_pairs={{0,2},{4,6},{1,3},{5,7},{2,0},{6,4},{3,1},{7,5},{8,10},{12,14},{9,... | collective-permute-start | bytes 331784 | tf_op jit(solution)/shard_map/ppermute | solution.py:34
  (8 other events, 17.0 us)

commit v9 on v6

--- a/solution.py
+++ b/solution.py
@@ -231,9 +231,10 @@
 
     for copy in feat_copies:
         copy.wait()
-    for j in range(0, width, 128):
-        grad[j : j + 128, :] = lax.dot_general(
-            feats[:, j : j + 128], dy[...], (((0,), (0,)), ((), ())), preferred_element_type=F32
+    step = width // 3
+    for j in range(0, width, step):
+        grad[j : j + step, :] = lax.dot_general(
+            feats[:, j : j + step], dy[...], (((0,), (0,)), ((), ())), preferred_element_type=F32
         )
 
     sums = stats[0:1, :]

time: 86.5 us -> 86.5 us (level)
  no operation moved by 1% of the time
where the time goes in v9:
time: 86.5 us; the launch traced here: 86.2 us
  starting transfers between devices  29.8 us (34%)
  Pallas kernels  25 us (29%)
  waiting for transfers between devices  22.2 us (26%)
  local copies, waits for them, and re-layouts  6.02 us (7%)
  between operations  2.13 us (2%)
  other arithmetic  1.09 us (1%)
    ppermute x28, starting transfers between devices, send(): return lax.ppermute(value, AXES, pairs)  29.8 us
    ppermute x28, waiting for transfers between devices, send(): return lax.ppermute(value, AXES, pairs)  22.2 us
    pallas_call x1, Pallas kernels, block_grads(): pl.pallas_call(functools.partial(block_kernel, side, layout.mp), out_shap...  16.2 us
    pallas_call x3, Pallas kernels, project_chunk(): pl.pallas_call(project_kernel, out_shape=[jax.ShapeDtypeStruct((rows, wid...  8.31 us
    unnamed x10, local copies, waits for them, and re-layouts  5.43 us
  transfers between devices with their start and end apart: 28, of which 14 were waited for; matrix products, arithmetic and copies ran while one was open for 1% of the time, Pallas kernels for 10%

profile of v9, /device:TPU:0, one launch (start us, length us, event | category | flops | bytes accessed | tf_op | source)
XLA Modules:
  0.0 86.2 jit_solution(2909909923463447824)
XLA Ops:
  1.2 3.0 %collective-permute-start = (bf16[128,1152]{1,0:T(8,128)(2,1)}, bf16[128,1152]{1,0:T(8,128)(2,1)S(1)}, u32[]{:S(2)}, u32[]{:S(2)}) collective-permute-start(bf16[128,1152]{1,0:T(8,128)(2,1)} %refs_0_.1), channel_id=1, source_target_pairs={{0,1},{4,5},{1,0},{5,4},{2,3},{6,7},{3,2},{7,6},{8,9},{12,13},{9,8... | collective-permute-start | bytes 884744 | tf_op jit(solution)/shard_map/ppermute | solution.py:34
  4.2 2.6 %collective-permute-start.1 = (bf16[128,1152]{1,0:T(8,128)(2,1)}, bf16[128,1152]{1,0:T(8,128)(2,1)S(1)}, u32[]{:S(2)}, u32[]{:S(2)}) collective-permute-start(bf16[128,1152]{1,0:T(8,128)(2,1)} %refs_0_.1), channel_id=1, source_target_pairs={{0,2},{4,6},{1,3},{5,7},{2,0},{6,4},{3,1},{7,5},{8,10},{12,14},{9,... | collective-permute-start | bytes 884744 | tf_op jit(solution)/shard_map/ppermute | solution.py:34
  6.8 1.5 %collective-permute-start.2 = (bf16[128,1152]{1,0:T(8,128)(2,1)}, bf16[128,1152]{1,0:T(8,128)(2,1)S(1)}, u32[]{:S(2)}, u32[]{:S(2)}) collective-permute-start(bf16[128,1152]{1,0:T(8,128)(2,1)} %refs_1_.1), channel_id=1, source_target_pairs={{0,8},{4,12},{1,9},{5,13},{2,10},{6,14},{3,11},{7,15},{8,0},{12,4}... | collective-permute-start | bytes 884744 | tf_op jit(solution)/shard_map/ppermute | solution.py:34
  8.3 1.5 %collective-permute-start.3 = (bf16[128,1152]{1,0:T(8,128)(2,1)}, bf16[128,1152]{1,0:T(8,128)(2,1)S(1)}, u32[]{:S(2)}, u32[]{:S(2)}) collective-permute-start(bf16[128,1152]{1,0:T(8,128)(2,1)} %refs_1_.1), channel_id=1, source_target_pairs={{0,16},{4,20},{1,17},{5,21},{2,18},{6,22},{3,19},{7,23},{8,24},{12... | collective-permute-start | bytes 884744 | tf_op jit(solution)/shard_map/ppermute | solution.py:34
  9.8 1.7 %copy-done = bf16[1152,1152]{1,0:T(8,128)(2,1)S(1)} copy-done((bf16[1152,1152]{1,0:T(8,128)(2,1)S(1)}, bf16[1152,1152]{1,0:T(8,128)(2,1)}, u32[]{:S(2)}) %copy-start) | copy-done | bytes 2654232
  11.6 1.7 %copy-done.2 = bf16[1152,1152]{1,0:T(8,128)(2,1)S(1)} copy-done((bf16[1152,1152]{1,0:T(8,128)(2,1)S(1)}, bf16[1152,1152]{1,0:T(8,128)(2,1)}, u32[]{:S(2)}) %copy-start.2) | copy-done | bytes 2654232
  15.3 2.8 %project.3 = (bf16[256,1152]{1,0:T(8,128)(2,1)S(1)}, f32[256,1152]{1,0:T(8,128)S(1)}, f32[256,128]{1,0:T(8,128)S(1)}, bf16[256,1152]{1,0:T(8,128)(2,1)S(1)}) custom-call(bf16[1152,1152]{1,0:T(8,128)(2,1)S(1)} %copy-done, bf16[1152,1152]{1,0:T(8,128)(2,1)S(1)} %copy-done.2, bf16[128,1152]{1,0:T(8,128)(2,1)S(1)} %copy-done.3, bf16[128,1152]{1,0:T(8,128)(2,1)S(1)} %copy-done.4, ...), custom_call_target="tpu_custom_call" | custom-call | flops 1358954496 | bytes 8847360 | tf_op jit(solution)/shard_map/project/pallas_call | solution.py:107
  18.0 2.4 %collective-permute-done.1.refs_0_ = bf16[128,1152]{1,0:T(8,128)(2,1)S(1)} collective-permute-done((bf16[128,1152]{1,0:T(8,128)(2,1)}, bf16[128,1152]{1,0:T(8,128)(2,1)S(1)}, u32[]{:S(2)}, u32[]{:S(2)}) %collective-permute-start.1) | collective-permute-done | bytes 294944 | tf_op jit(solution)/shard_map/ppermute | solution.py:34
  22.0 1.5 %collective-permute-start.7 = (bf16[128,1152]{1,0:T(8,128)(2,1)S(1)}, bf16[128,1152]{1,0:T(8,128)(2,1)S(1)}, u32[]{:S(2)}, u32[]{:S(2)}) collective-permute-start(bf16[128,1152]{1,0:T(8,128)(2,1)S(1)} %collective-permute-done.3.refs_1_), channel_id=1, source_target_pairs={{0,8},{4,12},{1,9},{5,13},{2,10},{6,14},{3,11},{7,15},{8,0},{12,4}... | collective-permute-start | bytes 884744 | tf_op jit(solution)/shard_map/ppermute | solution.py:34
  23.5 2.8 %project.5 = (bf16[256,1152]{1,0:T(8,128)(2,1)S(1)}, f32[256,1152]{1,0:T(8,128)S(1)}, f32[256,128]{1,0:T(8,128)S(1)}, bf16[256,1152]{1,0:T(8,128)(2,1)S(1)}) custom-call(bf16[1152,1152]{1,0:T(8,128)(2,1)S(1)} %copy-done, bf16[1152,1152]{1,0:T(8,128)(2,1)S(1)} %copy-done.2, bf16[128,1152]{1,0:T(8,128)(2,1)S(1)} %collective-permute-done.1.refs_0_, ...), custom_call_target="tpu_custom_call" | custom-call | flops 1358954496 | bytes 8847360 | tf_op jit(solution)/shard_map/project/pallas_call | solution.py:107
  26.3 2.8 %project.4 = (bf16[256,1152]{1,0:T(8,128)(2,1)S(1)}, f32[256,1152]{1,0:T(8,128)S(1)}, f32[256,128]{1,0:T(8,128)S(1)}, bf16[256,1152]{1,0:T(8,128)(2,1)S(1)}) custom-call(bf16[1152,1152]{1,0:T(8,128)(2,1)S(1)} %copy-done, bf16[1152,1152]{1,0:T(8,128)(2,1)S(1)} %copy-done.2, bf16[128,1152]{1,0:T(8,128)(2,1)S(1)} %collective-permute-done.refs_0_, ...), custom_call_target="tpu_custom_call" | custom-call | flops 1358954496 | bytes 8847360 | tf_op jit(solution)/shard_map/project/pallas_call | solution.py:107
  29.1 1.3 %collective-permute-done.6.refs_0_ = bf16[128,1152]{1,0:T(8,128)(2,1)S(1)} collective-permute-done((bf16[128,1152]{1,0:T(8,128)(2,1)S(1)}, bf16[128,1152]{1,0:T(8,128)(2,1)S(1)}, u32[]{:S(2)}, u32[]{:S(2)}) %collective-permute-start.6) | collective-permute-done | bytes 294944 | tf_op jit(solution)/shard_map/ppermute | solution.py:34
  33.1 16.2 %block.1 = (f32[576,384]{1,0:T(8,128)S(1)}, bf16[584,384]{1,0:T(8,128)(2,1)S(1)}, f32[576,384]{1,0:T(8,128)S(1)}, bf16[576,384]{1,0:T(8,128)(2,1)S(1)}, f32[576,...) custom-call(f32[2]{0:T(128)S(1)} %pad_maximum_fusion.1.scalars, ...), custom_call_target="tpu_custom_call" | custom-call | flops 8908701696 | bytes 19464192 | tf_op jit(solution)/shard_map/block/pallas_call | solution.py:323
  49.3 1.6 %collective-permute-start.19 = (bf16[576,384]{1,0:T(8,128)(2,1)S(1)}, bf16[576,384]{1,0:T(8,128)(2,1)S(1)}, u32[]{:S(2)}, u32[]{:S(2)}) collective-permute-start(bf16[576,384]{1,0:T(8,128)(2,1)S(1)} %get-tuple-element.114), channel_id=1, source_target_pairs={{0,16},{4,20},{1,17},{5,21},{2,18},{6,22},{3,19},{7,23},{8,24},{12... | collective-permute-start | bytes 1327112 | tf_op jit(solution)/shard_map/ppermute | solution.py:34
  50.8 1.5 %collective-permute-start.14 = (bf16[584,384]{1,0:T(8,128)(2,1)S(1)}, bf16[584,384]{1,0:T(8,128)(2,1)S(1)}, u32[]{:S(2)}, u32[]{:S(2)}) collective-permute-start(bf16[584,384]{1,0:T(8,128)(2,1)S(1)} %get-tuple-element.102), channel_id=1, source_target_pairs={{0,8},{4,12},{1,9},{5,13},{2,10},{6,14},{3,11},{7,15},{8,0},{12,4}... | collective-permute-start | bytes 1345544 | tf_op jit(solution)/shard_map/ppermute | solution.py:34
  53.5 8.1 %collective-permute-done.19.arrived = bf16[576,384]{1,0:T(8,128)(2,1)S(1)} collective-permute-done((bf16[576,384]{1,0:T(8,128)(2,1)S(1)}, bf16[576,384]{1,0:T(8,128)(2,1)S(1)}, u32[]{:S(2)}, u32[]{:S(2)}) %collective-permute-start.19) | collective-permute-done | bytes 442400 | tf_op jit(solution)/shard_map/ppermute | solution.py:34
  63.0 1.5 %collective-permute-start.15 = (bf16[296,384]{1,0:T(8,128)(2,1)S(1)}, bf16[296,384]{1,0:T(8,128)(2,1)S(1)}, u32[]{:S(2)}, u32[]{:S(2)}) collective-permute-start(bf16[296,384]{1,0:T(8,128)(2,1)S(1)} %get-tuple-element.105), channel_id=1, source_target_pairs={{0,16},{4,20},{1,17},{5,21},{2,18},{6,22},{3,19},{7,23},{8,24},{12... | collective-permute-start | bytes 681992 | tf_op jit(solution)/shard_map/ppermute | solution.py:34
  64.6 1.6 %collective-permute-start.24 = (bf16[288,384]{1,0:T(8,128)(2,1)S(1)}, bf16[288,384]{1,0:T(8,128)(2,1)S(1)}, u32[]{:S(2)}, u32[]{:S(2)}) collective-permute-start(bf16[288,384]{1,0:T(8,128)(2,1)S(1)} %get-tuple-element.124), channel_id=1, source_target_pairs={{0,8},{4,12},{1,9},{5,13},{2,10},{6,14},{3,11},{7,15},{8,0},{12,4}... | collective-permute-start | bytes 663560 | tf_op jit(solution)/shard_map/ppermute | solution.py:34
  66.2 2.6 %collective-permute-done.20.arrived = bf16[288,384]{1,0:T(8,128)(2,1)S(1)} collective-permute-done((bf16[288,384]{1,0:T(8,128)(2,1)S(1)}, bf16[288,384]{1,0:T(8,128)(2,1)S(1)}, u32[]{:S(2)}, u32[]{:S(2)}) %collective-permute-start.20) | collective-permute-done | bytes 221216 | tf_op jit(solution)/shard_map/ppermute | solution.py:34
  70.0 2.2 %collective-permute-start.16 = (bf16[152,384]{1,0:T(8,128)(2,1)S(1)}, bf16[152,384]{1,0:T(8,128)(2,1)S(1)}, u32[]{:S(2)}, u32[]{:S(2)}) collective-permute-start(bf16[152,384]{1,0:T(8,128)(2,1)S(1)} %get-tuple-element.108), channel_id=1, source_target_pairs={{0,2},{4,6},{1,3},{5,7},{2,0},{6,4},{3,1},{7,5},{8,10},{12,14},{9,... | collective-permute-start | bytes 350216 | tf_op jit(solution)/shard_map/ppermute | solution.py:34
  72.3 1.6 %collective-permute-start.25 = (bf16[144,384]{1,0:T(8,128)(2,1)S(1)}, bf16[144,384]{1,0:T(8,128)(2,1)S(1)}, u32[]{:S(2)}, u32[]{:S(2)}) collective-permute-start(bf16[144,384]{1,0:T(8,128)(2,1)S(1)} %get-tuple-element.126), channel_id=1, source_target_pairs={{0,16},{4,20},{1,17},{5,21},{2,18},{6,22},{3,19},{7,23},{8,24},{12... | collective-permute-start | bytes 331784 | tf_op jit(solution)/shard_map/ppermute | solution.py:34
  73.9 1.9 %collective-permute-start.22 = (bf16[72,384]{1,0:T(8,128)(2,1)S(1)}, bf16[72,384]{1,0:T(8,128)(2,1)S(1)}, u32[]{:S(2)}, u32[]{:S(2)}) collective-permute-start(bf16[72,384]{1,0:T(8,128)(2,1)S(1)} %get-tuple-element.120), channel_id=1, source_target_pairs={{0,2},{4,6},{1,3},{5,7},{2,0},{6,4},{3,1},{7,5},{8,10},{12,14},{9,... | collective-permute-start | bytes 165896 | tf_op jit(solution)/shard_map/ppermute | solution.py:34
  75.8 1.3 %collective-permute-done.25.arrived = bf16[144,384]{1,0:T(8,128)(2,1)S(1)} collective-permute-done((bf16[144,384]{1,0:T(8,128)(2,1)S(1)}, bf16[144,384]{1,0:T(8,128)(2,1)S(1)}, u32[]{:S(2)}, u32[]{:S(2)}) %collective-permute-start.25) | collective-permute-done | bytes 110624 | tf_op jit(solution)/shard_map/ppermute | solution.py:34
  80.6 2.3 %collective-permute-done.26 = bf16[72,384]{1,0:T(8,128)(2,1)S(1)} collective-permute-done((bf16[72,384]{1,0:T(8,128)(2,1)S(1)}, bf16[72,384]{1,0:T(8,128)(2,1)S(1)}, u32[]{:S(2)}, u32[]{:S(2)}) %collective-permute-start.26) | collective-permute-done | bytes 55328 | tf_op jit(solution)/shard_map/ppermute | solution.py:34
  (67 shorter events, 16.2 us)
Async XLA Ops:
  0.6 7.7 %collective-permute-start.4 = (bf16[128,1152]{1,0:T(8,128)(2,1)}, bf16[128,1152]{1,0:T(8,128)(2,1)S(1)}, u32[]{:S(2)}, u32[]{:S(2)}) collective-permute-start(bf16[128,1152]{1,0:T(8,128)(2,1)} %refs_0_.1), channel_id=1, source_target_pairs={{0,4},{4,0},{1,5},{5,1},{2,6},{6,2},{3,7},{7,3},{8,12},{12,8},{9,1... | collective-permute-start | bytes 884744 | tf_op jit(solution)/shard_map/ppermute | solution.py:34
  1.1 8.7 %collective-permute-start.5 = (bf16[128,1152]{1,0:T(8,128)(2,1)}, bf16[128,1152]{1,0:T(8,128)(2,1)S(1)}, u32[]{:S(2)}, u32[]{:S(2)}) collective-permute-start(bf16[128,1152]{1,0:T(8,128)(2,1)} %refs_1_.1), channel_id=1, source_target_pairs={{0,4},{4,0},{1,5},{5,1},{2,6},{6,2},{3,7},{7,3},{8,12},{12,8},{9,1... | collective-permute-start | bytes 884744 | tf_op jit(solution)/shard_map/ppermute | solution.py:34
  1.2 16.8 %collective-permute-start = (bf16[128,1152]{1,0:T(8,128)(2,1)}, bf16[128,1152]{1,0:T(8,128)(2,1)S(1)}, u32[]{:S(2)}, u32[]{:S(2)}) collective-permute-start(bf16[128,1152]{1,0:T(8,128)(2,1)} %refs_0_.1), channel_id=1, source_target_pairs={{0,1},{4,5},{1,0},{5,4},{2,3},{6,7},{3,2},{7,6},{8,9},{12,13},{9,8... | collective-permute-start | bytes 884744 | tf_op jit(solution)/shard_map/ppermute | solution.py:34
  4.2 16.2 %collective-permute-start.1 = (bf16[128,1152]{1,0:T(8,128)(2,1)}, bf16[128,1152]{1,0:T(8,128)(2,1)S(1)}, u32[]{:S(2)}, u32[]{:S(2)}) collective-permute-start(bf16[128,1152]{1,0:T(8,128)(2,1)} %refs_0_.1), channel_id=1, source_target_pairs={{0,2},{4,6},{1,3},{5,7},{2,0},{6,4},{3,1},{7,5},{8,10},{12,14},{9,... | collective-permute-start | bytes 884744 | tf_op jit(solution)/shard_map/ppermute | solution.py:34
  6.8 13.6 %collective-permute-start.2 = (bf16[128,1152]{1,0:T(8,128)(2,1)}, bf16[128,1152]{1,0:T(8,128)(2,1)S(1)}, u32[]{:S(2)}, u32[]{:S(2)}) collective-permute-start(bf16[128,1152]{1,0:T(8,128)(2,1)} %refs_1_.1), channel_id=1, source_target_pairs={{0,8},{4,12},{1,9},{5,13},{2,10},{6,14},{3,11},{7,15},{8,0},{12,4}... | collective-permute-start | bytes 884744 | tf_op jit(solution)/shard_map/ppermute | solution.py:34
  8.3 12.1 %collective-permute-start.3 = (bf16[128,1152]{1,0:T(8,128)(2,1)}, bf16[128,1152]{1,0:T(8,128)(2,1)S(1)}, u32[]{:S(2)}, u32[]{:S(2)}) collective-permute-start(bf16[128,1152]{1,0:T(8,128)(2,1)} %refs_1_.1), channel_id=1, source_target_pairs={{0,16},{4,20},{1,17},{5,21},{2,18},{6,22},{3,19},{7,23},{8,24},{12... | collective-permute-start | bytes 884744 | tf_op jit(solution)/shard_map/ppermute | solution.py:34
  20.4 3.1 %collective-permute-start.11 = (bf16[128,1152]{1,0:T(8,128)(2,1)S(1)}, bf16[128,1152]{1,0:T(8,128)(2,1)S(1)}, u32[]{:S(2)}, u32[]{:S(2)}) collective-permute-start(bf16[128,1152]{1,0:T(8,128)(2,1)S(1)} %collective-permute-done.3.refs_1_), channel_id=1, source_target_pairs={{0,4},{4,0},{1,5},{5,1},{2,6},{6,2},{3,7},{7,3},{8,12},{12,8},{9,1... | collective-permute-start | bytes 884744 | tf_op jit(solution)/shard_map/ppermute | solution.py:34
  21.0 5.4 %collective-permute-start.8 = (bf16[128,1152]{1,0:T(8,128)(2,1)S(1)}, bf16[128,1152]{1,0:T(8,128)(2,1)S(1)}, u32[]{:S(2)}, u32[]{:S(2)}) collective-permute-start(bf16[128,1152]{1,0:T(8,128)(2,1)S(1)} %collective-permute-done.refs_0_), channel_id=1, source_target_pairs={{0,4},{4,0},{1,5},{5,1},{2,6},{6,2},{3,7},{7,3},{8,12},{12,8},{9,1... | collective-permute-start | bytes 884744 | tf_op jit(solution)/shard_map/ppermute | solution.py:34
  21.0 5.3 %collective-permute-start.9 = (bf16[128,1152]{1,0:T(8,128)(2,1)S(1)}, bf16[128,1152]{1,0:T(8,128)(2,1)S(1)}, u32[]{:S(2)}, u32[]{:S(2)}) collective-permute-start(bf16[128,1152]{1,0:T(8,128)(2,1)S(1)} %collective-permute-done.2.refs_1_), channel_id=1, source_target_pairs={{0,4},{4,0},{1,5},{5,1},{2,6},{6,2},{3,7},{7,3},{8,12},{12,8},{9,1... | collective-permute-start | bytes 884744 | tf_op jit(solution)/shard_map/ppermute | solution.py:34
  21.5 9.0 %collective-permute-start.6 = (bf16[128,1152]{1,0:T(8,128)(2,1)S(1)}, bf16[128,1152]{1,0:T(8,128)(2,1)S(1)}, u32[]{:S(2)}, u32[]{:S(2)}) collective-permute-start(bf16[128,1152]{1,0:T(8,128)(2,1)S(1)} %collective-permute-done.1.refs_0_), channel_id=1, source_target_pairs={{0,1},{4,5},{1,0},{5,4},{2,3},{6,7},{3,2},{7,6},{8,9},{12,13},{9,8... | collective-permute-start | bytes 884744 | tf_op jit(solution)/shard_map/ppermute | solution.py:34
  22.0 9.1 %collective-permute-start.7 = (bf16[128,1152]{1,0:T(8,128)(2,1)S(1)}, bf16[128,1152]{1,0:T(8,128)(2,1)S(1)}, u32[]{:S(2)}, u32[]{:S(2)}) collective-permute-start(bf16[128,1152]{1,0:T(8,128)(2,1)S(1)} %collective-permute-done.3.refs_1_), channel_id=1, source_target_pairs={{0,8},{4,12},{1,9},{5,13},{2,10},{6,14},{3,11},{7,15},{8,0},{12,4}... | collective-permute-start | bytes 884744 | tf_op jit(solution)/shard_map/ppermute | solution.py:34
  31.1 2.0 %collective-permute-start.13 = (bf16[128,1152]{1,0:T(8,128)(2,1)S(1)}, bf16[128,1152]{1,0:T(8,128)(2,1)S(1)}, u32[]{:S(2)}, u32[]{:S(2)}) collective-permute-start(bf16[128,1152]{1,0:T(8,128)(2,1)S(1)} %collective-permute-done.7.refs_1_), channel_id=1, source_target_pairs={{0,4},{4,0},{1,5},{5,1},{2,6},{6,2},{3,7},{7,3},{8,12},{12,8},{9,1... | collective-permute-start | bytes 884744 | tf_op jit(solution)/shard_map/ppermute | solution.py:34
  49.3 12.3 %collective-permute-start.19 = (bf16[576,384]{1,0:T(8,128)(2,1)S(1)}, bf16[576,384]{1,0:T(8,128)(2,1)S(1)}, u32[]{:S(2)}, u32[]{:S(2)}) collective-permute-start(bf16[576,384]{1,0:T(8,128)(2,1)S(1)} %get-tuple-element.114), channel_id=1, source_target_pairs={{0,16},{4,20},{1,17},{5,21},{2,18},{6,22},{3,19},{7,23},{8,24},{12... | collective-permute-start | bytes 1327112 | tf_op jit(solution)/shard_map/ppermute | solution.py:34
  50.8 12.1 %collective-permute-start.14 = (bf16[584,384]{1,0:T(8,128)(2,1)S(1)}, bf16[584,384]{1,0:T(8,128)(2,1)S(1)}, u32[]{:S(2)}, u32[]{:S(2)}) collective-permute-start(bf16[584,384]{1,0:T(8,128)(2,1)S(1)} %get-tuple-element.102), channel_id=1, source_target_pairs={{0,8},{4,12},{1,9},{5,13},{2,10},{6,14},{3,11},{7,15},{8,0},{12,4}... | collective-permute-start | bytes 1345544 | tf_op jit(solution)/shard_map/ppermute | solution.py:34
  52.4 12.2 %collective-permute-start.23 = (bf16[576,384]{1,0:T(8,128)(2,1)S(1)}, bf16[576,384]{1,0:T(8,128)(2,1)S(1)}, u32[]{:S(2)}, u32[]{:S(2)}) collective-permute-start(bf16[576,384]{1,0:T(8,128)(2,1)S(1)} %get-tuple-element.122), channel_id=1, source_target_pairs={{0,1},{4,5},{1,0},{5,4},{2,3},{6,7},{3,2},{7,6},{8,9},{12,13},{9,8... | collective-permute-start | bytes 1327112 | tf_op jit(solution)/shard_map/ppermute | solution.py:34
  61.6 7.1 %collective-permute-start.20 = (bf16[288,384]{1,0:T(8,128)(2,1)S(1)}, bf16[288,384]{1,0:T(8,128)(2,1)S(1)}, u32[]{:S(2)}, u32[]{:S(2)}) collective-permute-start(bf16[288,384]{1,0:T(8,128)(2,1)S(1)} %get-tuple-element.116), channel_id=1, source_target_pairs={{0,1},{4,5},{1,0},{5,4},{2,3},{6,7},{3,2},{7,6},{8,9},{12,13},{9,8... | collective-permute-start | bytes 663560 | tf_op jit(solution)/shard_map/ppermute | solution.py:34
  63.0 7.0 %collective-permute-start.15 = (bf16[296,384]{1,0:T(8,128)(2,1)S(1)}, bf16[296,384]{1,0:T(8,128)(2,1)S(1)}, u32[]{:S(2)}, u32[]{:S(2)}) collective-permute-start(bf16[296,384]{1,0:T(8,128)(2,1)S(1)} %get-tuple-element.105), channel_id=1, source_target_pairs={{0,16},{4,20},{1,17},{5,21},{2,18},{6,22},{3,19},{7,23},{8,24},{12... | collective-permute-start | bytes 681992 | tf_op jit(solution)/shard_map/ppermute | solution.py:34
  64.6 7.6 %collective-permute-start.24 = (bf16[288,384]{1,0:T(8,128)(2,1)S(1)}, bf16[288,384]{1,0:T(8,128)(2,1)S(1)}, u32[]{:S(2)}, u32[]{:S(2)}) collective-permute-start(bf16[288,384]{1,0:T(8,128)(2,1)S(1)} %get-tuple-element.124), channel_id=1, source_target_pairs={{0,8},{4,12},{1,9},{5,13},{2,10},{6,14},{3,11},{7,15},{8,0},{12,4}... | collective-permute-start | bytes 663560 | tf_op jit(solution)/shard_map/ppermute | solution.py:34
  68.8 5.1 %collective-permute-start.21 = (bf16[144,384]{1,0:T(8,128)(2,1)S(1)}, bf16[144,384]{1,0:T(8,128)(2,1)S(1)}, u32[]{:S(2)}, u32[]{:S(2)}) collective-permute-start(bf16[144,384]{1,0:T(8,128)(2,1)S(1)} %get-tuple-element.118), channel_id=1, source_target_pairs={{0,8},{4,12},{1,9},{5,13},{2,10},{6,14},{3,11},{7,15},{8,0},{12,4}... | collective-permute-start | bytes 331784 | tf_op jit(solution)/shard_map/ppermute | solution.py:34
  70.0 9.0 %collective-permute-start.16 = (bf16[152,384]{1,0:T(8,128)(2,1)S(1)}, bf16[152,384]{1,0:T(8,128)(2,1)S(1)}, u32[]{:S(2)}, u32[]{:S(2)}) collective-permute-start(bf16[152,384]{1,0:T(8,128)(2,1)S(1)} %get-tuple-element.108), channel_id=1, source_target_pairs={{0,2},{4,6},{1,3},{5,7},{2,0},{6,4},{3,1},{7,5},{8,10},{12,14},{9,... | collective-permute-start | bytes 350216 | tf_op jit(solution)/shard_map/ppermute | solution.py:34
  72.3 4.8 %collective-permute-start.25 = (bf16[144,384]{1,0:T(8,128)(2,1)S(1)}, bf16[144,384]{1,0:T(8,128)(2,1)S(1)}, u32[]{:S(2)}, u32[]{:S(2)}) collective-permute-start(bf16[144,384]{1,0:T(8,128)(2,1)S(1)} %get-tuple-element.126), channel_id=1, source_target_pairs={{0,16},{4,20},{1,17},{5,21},{2,18},{6,22},{3,19},{7,23},{8,24},{12... | collective-permute-start | bytes 331784 | tf_op jit(solution)/shard_map/ppermute | solution.py:34
  73.9 6.7 %collective-permute-start.22 = (bf16[72,384]{1,0:T(8,128)(2,1)S(1)}, bf16[72,384]{1,0:T(8,128)(2,1)S(1)}, u32[]{:S(2)}, u32[]{:S(2)}) collective-permute-start(bf16[72,384]{1,0:T(8,128)(2,1)S(1)} %get-tuple-element.120), channel_id=1, source_target_pairs={{0,2},{4,6},{1,3},{5,7},{2,0},{6,4},{3,1},{7,5},{8,10},{12,14},{9,... | collective-permute-start | bytes 165896 | tf_op jit(solution)/shard_map/ppermute | solution.py:34
  77.1 5.8 %collective-permute-start.26 = (bf16[72,384]{1,0:T(8,128)(2,1)S(1)}, bf16[72,384]{1,0:T(8,128)(2,1)S(1)}, u32[]{:S(2)}, u32[]{:S(2)}) collective-permute-start(bf16[72,384]{1,0:T(8,128)(2,1)S(1)} %get-tuple-element.128), channel_id=1, source_target_pairs={{0,2},{4,6},{1,3},{5,7},{2,0},{6,4},{3,1},{7,5},{8,10},{12,14},{9,... | collective-permute-start | bytes 165896 | tf_op jit(solution)/shard_map/ppermute | solution.py:34
  79.0 4.4 %collective-permute-start.17 = (bf16[80,384]{1,0:T(8,128)(2,1)S(1)}, bf16[80,384]{1,0:T(8,128)(2,1)S(1)}, u32[]{:S(2)}, u32[]{:S(2)}) collective-permute-start(bf16[80,384]{1,0:T(8,128)(2,1)S(1)} %get-tuple-element.111), channel_id=1, source_target_pairs={{0,1},{4,5},{1,0},{5,4},{2,3},{6,7},{3,2},{7,6},{8,9},{12,13},{9,8... | collective-permute-start | bytes 184328 | tf_op jit(solution)/shard_map/ppermute | solution.py:34
  (9 other events, 18.7 us)
